TPU v7x, 32 devices: a whole 2x2x4 slice. The times are simulated.
32 devices in a mesh: dp: 8 (over z, x), seq: 4 (over y, core).
Axes of the slice: x: 2, y: 2, z: 4, core: 2. Of those that a mesh axis runs over, the one named last changes fastest.
Arguments:
- frames: bfloat16 [8, 1024, 1280], P('dp', 'seq'), may hold values from -6 to 6
- live: int32 [8, 1024], P('dp', 'seq'), may hold values from 0 to 1
- norm_gain: float32 [1280], replicated, may hold values from 0.25 to 1.75
- w_qkv: bfloat16 [1280, 1920], P('dp')
- w_out: bfloat16 [640, 1280], P('dp'), may hold values from -0.25 to 0.25
- cotangent: bfloat16 [8, 1024, 1280], P('dp', 'seq'), may hold values from -6 to 6
Outputs:
- grad_frames: bfloat16 [8, 1024, 1280], P('dp', 'seq')
- grad_qkv: float32 [1280, 1920], P('dp', 'seq')
- grad_out: float32 [640, 1280], P('dp', 'seq')
All inputs are finite; a program needn't handle non-finite values.
Results may differ from a plain program's by a relative error of at most 0.0095.
Values may be sent and summed in bfloat16 or wider, within the bound.
A program may use at most 64 MiB of HBM per device.

v0:
```python
import math

import jax
import jax.numpy as jnp
from jax import lax
from jax.sharding import PartitionSpec as P

HEAD_DIM = 64
WIN = 512


EPS = 1e-05
NEG = -1e30


def from_behind(value, axis, steps):
    count = lax.axis_size(axis)
    leading, last = (max(0, -steps), min(count, count - steps))
    return lax.ppermute(value, axis, [(source, source + steps) for source in range(leading, last)])


def norm_rows(values_in):
    average = jnp.mean(values_in, axis=-1, keepdims=True)
    centred = values_in - average
    inverse = lax.rsqrt(jnp.mean(centred * centred, axis=-1, keepdims=True) + EPS)
    return (centred * inverse, inverse)


def against(left, right):
    return lax.dot_general(
        left, right, (((1,), (1,)), ((), ())), preferred_element_type=jnp.float32
    )


def leading(left, right):
    return lax.dot_general(
        left, right, (((0,), (0,)), ((), ())), preferred_element_type=jnp.float32
    )


def head_terms(query_head, key_head, value_head, grad_head, allowed, query_live, score_scale):
    scores = jnp.where(allowed, against(query_head, key_head) * score_scale, NEG)
    row_peak = jnp.max(scores, axis=-1, keepdims=True)
    exponent = jnp.exp(scores - row_peak)
    probabilities = exponent / jnp.sum(exponent, axis=-1, keepdims=True)
    probs_b = probabilities.astype(jnp.bfloat16)
    mixed = jnp.dot(probs_b, value_head, preferred_element_type=jnp.float32) * query_live[:, None]
    attended = mixed.astype(jnp.bfloat16)
    row_delta = jnp.sum(grad_head.astype(jnp.float32) * attended.astype(jnp.float32), axis=1)
    grad_probs = against(grad_head, value_head)
    grad_scores = (probabilities * (grad_probs - row_delta[:, None]) * score_scale).astype(
        jnp.bfloat16
    )
    grad_query = jnp.dot(grad_scores, key_head, preferred_element_type=jnp.float32)
    grad_key = leading(grad_scores, query_head)
    grad_value = leading(probs_b, grad_head)
    return (attended, grad_query, grad_key, grad_value)


def body(frames, live, norm_gain, w_qkv, w_out, cotangent):
    length = frames.shape[1]
    n_data = lax.axis_size("dp")
    n_seq = lax.axis_size("seq")
    full_qkv, full_out = (
        lax.all_gather(w_qkv, "dp", axis=0, tiled=True),
        lax.all_gather(w_out, "dp", axis=0, tiled=True),
    )
    inner = full_out.shape[0]
    heads = inner // HEAD_DIM
    hidden = frames[0].astype(jnp.float32)
    unit_rows, inverse = norm_rows(hidden)
    normed = (unit_rows * norm_gain).astype(jnp.bfloat16)
    projected = jnp.dot(normed, full_qkv, preferred_element_type=jnp.float32).astype(jnp.bfloat16)
    query = projected[:, :inner]
    key_values = projected[:, inner:]
    live_row = live[0]
    query_live = live_row.astype(jnp.float32)
    live_mark = live_row.astype(jnp.bfloat16)
    upstream = cotangent[0]
    grad_att = (against(upstream, full_out) * query_live[:, None]).astype(jnp.bfloat16)
    neighbours = -(-WIN // length)
    offsets = list(range(neighbours, 0, -1)) + list(range(-1, -neighbours - 1, -1))
    before_pairs, before_marks, after_pairs, after_marks = ([], [], [], [])
    for offset in offsets:
        distance = abs(offset)
        row_count = min(length, WIN - (distance - 1) * length)
        if offset > 0:
            send_pairs = key_values
            send_marks = live_mark
        else:
            send_pairs = key_values
            send_marks = live_mark
        got_pairs, got_marks = from_behind((send_pairs, send_marks), "seq", offset)
        if offset > 0:
            before_pairs.append(got_pairs)
            before_marks.append(got_marks)
        else:
            after_pairs.append(got_pairs)
            after_marks.append(got_marks)
    ext_pairs = jnp.concatenate(before_pairs + [key_values] + after_pairs, axis=0)
    ext_live = jnp.concatenate(before_marks + [live_mark] + after_marks, axis=0).astype(jnp.float32)
    total_span = length + 2 * WIN
    block_rows = min(length, 512)
    key_span = block_rows + 2 * WIN
    query_pos = jnp.arange(block_rows, dtype=jnp.int32)
    key_pos = jnp.arange(key_span, dtype=jnp.int32) - WIN
    in_window = jnp.abs(query_pos[:, None] - key_pos[None, :]) <= WIN
    allowances = [in_window & (ext_live[None, :] > 0.5)]
    score_scale = 1.0 / math.sqrt(HEAD_DIM)

    def split_heads(matrix):
        return matrix.reshape(matrix.shape[0], heads, HEAD_DIM).transpose(1, 0, 2)

    def merge_heads(matrix):
        return matrix.transpose(1, 0, 2).reshape(matrix.shape[1], inner)

    def one_head(inputs):
        query_head, key_head, value_head, grad_head = inputs
        out_blocks, query_blocks = ([], [])
        key_grads = jnp.zeros((total_span, HEAD_DIM), jnp.float32)
        value_grads = jnp.zeros((total_span, HEAD_DIM), jnp.float32)
        attended, grad_query, grad_key, grad_value = head_terms(
            query_head, key_head, value_head, grad_head, allowances[0], query_live, score_scale
        )
        out_blocks.append(attended)
        query_blocks.append(grad_query)
        key_grads = key_grads.at[0:key_span].add(grad_key)
        value_grads = value_grads.at[0:key_span].add(grad_value)
        return (
            jnp.concatenate(out_blocks, axis=0),
            jnp.concatenate(query_blocks, axis=0),
            key_grads,
            value_grads,
        )

    att_heads, query_heads, key_heads, value_heads = lax.map(
        one_head,
        (
            split_heads(query),
            split_heads(ext_pairs[:, :inner]),
            split_heads(ext_pairs[:, inner:]),
            split_heads(grad_att),
        ),
    )
    attention = merge_heads(att_heads)
    grad_query = merge_heads(query_heads)
    ext_grads = jnp.concatenate([merge_heads(key_heads), merge_heads(value_heads)], axis=1)
    own_grads = ext_grads[WIN : WIN + length]
    for offset in offsets:
        distance = abs(offset)
        row_count = min(length, WIN - (distance - 1) * length)
        if offset > 0:
            first_row = WIN - distance * length + length - row_count
        else:
            first_row = WIN + length + (distance - 1) * length
        arrived = from_behind(ext_grads[first_row : first_row + row_count], "seq", -offset)
        if offset > 0:
            own_grads = own_grads.at[length - row_count :].add(arrived)
        else:
            own_grads = own_grads.at[:row_count].add(arrived)
    grad_projected = jnp.concatenate([grad_query, own_grads], axis=1).astype(jnp.bfloat16)
    grad_unit = against(grad_projected, full_qkv) * norm_gain
    through = inverse * (
        grad_unit
        - jnp.mean(grad_unit, axis=-1, keepdims=True)
        - unit_rows * jnp.mean(grad_unit * unit_rows, axis=-1, keepdims=True)
    )
    grad_rows = (upstream.astype(jnp.float32) + through).astype(jnp.bfloat16)[None]
    factor = 1.0 / math.sqrt(n_data * n_seq * length)

    def blocked(left, right):
        left_tiles = left.reshape(length, n_data, left.shape[1] // n_data)
        right_tiles = right.reshape(length, n_seq, right.shape[1] // n_seq)
        tile_grid = jnp.einsum(
            "fpr,fsc->psrc", left_tiles, right_tiles, preferred_element_type=jnp.float32
        )
        return tile_grid.reshape(n_data * n_seq * left_tiles.shape[2], right_tiles.shape[2])

    sum_qkv, sum_out = (
        lax.psum_scatter(
            blocked(normed, grad_projected), ("dp", "seq"), scatter_dimension=0, tiled=True
        ),
        lax.psum_scatter(
            blocked(attention, upstream), ("dp", "seq"), scatter_dimension=0, tiled=True
        ),
    )
    return (grad_rows, sum_qkv * factor, sum_out * factor)


def solution(mesh):
    return jax.shard_map(
        body,
        mesh=mesh,
        in_specs=(
            P("dp", "seq", None),
            P("dp", "seq"),
            P(),
            P("dp", None),
            P("dp", None),
            P("dp", "seq", None),
        ),
        out_specs=(P("dp", "seq", None), P("dp", "seq"), P("dp", "seq")),
        check_vma=False,
    )
```

profile of v0, /device:TPU:0, one launch (start us, length us, event | category | flops | bytes accessed | tf_op | source)
XLA Modules:
  0.0 565.8 jit_solution(10097061881912627672)
XLA Ops:
  9.4 4.9 collective-permute-start.4
  20.0 75.3 %all-gather.3.cloned.1.call-done = bf16[1280,1920]{1,0:T(8,128)(2,1)} async-done(((bf16[160,1920]{1,0:T(8,128)(2,1)}), bf16[1280,1920]{1,0:T(8,128)(2,1)}) %all-gather.3.cloned.1.call-update) | async-done | bytes 4915216 | tf_op jit(solution)/shard_map/all_gather | solution.py:65
  95.2 4.0 convolution_convert_fusion
  100.2 4.3 collective-permute-start
  104.6 2.2 copy.24
  107.6 2.1 collective-permute-start.1
  109.8 30.4 %all-gather.5.cloned.1.call-done = bf16[640,1280]{1,0:T(8,128)(2,1)} async-done(((bf16[80,1280]{1,0:T(8,128)(2,1)}), bf16[640,1280]{1,0:T(8,128)(2,1)}) %all-gather.5.cloned.1.call-update) | async-done | bytes 1638416 | tf_op jit(solution)/shard_map/all_gather | solution.py:66
  140.1 3.1 fusion.64
  154.9 18.2 %collective-permute-done.3 = bf16[256,1280]{1,0:T(8,128)(2,1)} collective-permute-done((bf16[256,1280]{1,0:T(8,128)(2,1)}, bf16[256,1280]{1,0:T(8,128)(2,1)}, u32[]{:S(2)}, u32[]{:S(2)}) %collective-permute-start.3) | collective-permute-done | bytes 655392 | tf_op jit(solution)/shard_map/ppermute | solution.py:19
  176.3 3.5 copy.16
  179.8 3.5 copy.17
  183.4 109.7 %while.32 = (s32[]{:T(128)}, bf16[10,256,64]{1,2,0:T(8,128)(2,1)}, bf16[10,256,64]{1,2,0:T(8,128)(2,1)}, f32[10,1280,64]{1,2,0:T(8,128)S(1)}, f32[10,1280,64]{1,...) while((s32[]{:T(128)}, bf16[10,256,64]{1,2,0:T(8,128)(2,1)}, ...), condition=%wide.region_6.7_spmd.clone, body=%wide.region_2.6_spmd.clone.sunk | while | flops 258637056 | bytes 10183049 | solution.py:136
  293.1 3.8 fusion.74
  297.0 4.3 fusion.62
  301.3 2.5 collective-permute-start.11
  303.8 2.4 collective-permute-start.10
  310.1 2.2 copy.22
  312.3 20.0 %collective-permute-done.11 = f32[256,1280]{0,1:T(8,128)} collective-permute-done((f32[256,1280]{0,1:T(8,128)}, f32[256,1280]{0,1:T(8,128)}, u32[]{:S(2)}, u32[]{:S(2)}) %collective-permute-start.11) | collective-permute-done | bytes 1310752 | tf_op jit(solution)/shard_map/ppermute | solution.py:19
  332.3 26.4 %collective-permute-done.8 = f32[256,1280]{0,1:T(8,128)} collective-permute-done((f32[256,1280]{0,1:T(8,128)}, f32[256,1280]{0,1:T(8,128)}, u32[]{:S(2)}, u32[]{:S(2)}) %collective-permute-start.8) | collective-permute-done | bytes 1310752 | tf_op jit(solution)/shard_map/ppermute | solution.py:19
  358.7 3.2 fusion.61
  364.8 5.6 copy.23
  371.9 4.3 fusion.71
  377.6 25.8 %reduce-scatter.5.cloned.1.call-done = f32[80,320]{1,0:T(8,128)} async-done(((f32[2560,320]{1,0:T(8,128)}), f32[80,320]{1,0:T(8,128)}) %reduce-scatter.5.cloned.1.call-update) | async-done | bytes 102416 | tf_op jit(solution)/shard_map/reduce_scatter | solution.py:183
  405.0 152.6 %reduce-scatter.3.cloned.1.call-done = f32[160,480]{1,0:T(8,128)} async-done(((f32[5120,480]{1,0:T(8,128)}), f32[160,480]{1,0:T(8,128)}) %reduce-scatter.3.cloned.1.call-update) | async-done | bytes 307216 | tf_op jit(solution)/shard_map/reduce_scatter | solution.py:180
  (163 shorter events, 147.0 us)
Async XLA Ops:
  7.2 12.5 %copy-start = (bf16[1,256,1280]{2,1,0:T(8,128)(2,1)S(1)}, bf16[1,256,1280]{2,1,0:T(8,128)(2,1)}, u32[]{:S(2)}) copy-start(bf16[1,256,1280]{2,1,0:T(8,128)(2,1)} %param.32) | copy-start | bytes 1966084
  7.2 88.0 %copy-start.10 = (f32[1280]{0:T(1024)S(1)}, f32[1280]{0:T(1024)}, u32[]{:S(2)}) copy-start(f32[1280]{0:T(1024)} %param.34) | copy-start | bytes 15364
  7.2 88.0 %all-gather.3.cloned.1.call-start = ((), (), s32[]{:S(2)}) async-start(), calls=%async_computation.2 | async-start | bytes 5529600 | tf_op jit(solution)/shard_map/all_gather | solution.py:65
  7.9 132.2 %all-gather.5.cloned.1.call-start = ((), (), s32[]{:S(2)}) async-start(), calls=%async_computation.3 | async-start | bytes 1843200 | tf_op jit(solution)/shard_map/all_gather | solution.py:66
  8.7 394.7 %reduce-scatter.5.cloned.1.call-start = ((), (), s32[]{:S(2)}) async-start(), calls=%async_computation.5 | async-start | bytes 4055040 | tf_op jit(solution)/shard_map/reduce_scatter | solution.py:183
  9.4 97.4 %collective-permute-start.4 = (bf16[256]{0:T(256)(128)(2,1)S(1)}, bf16[256]{0:T(256)(128)(2,1)S(1)}, u32[]{:S(2)}, u32[]{:S(2)}) collective-permute-start(bf16[256]{0:T(256)(128)(2,1)S(1)} %convert_reduce_fusion.1), channel_id=1, source_target_pairs={{0,2},{1,3},{4,6},{5,7},{8,10},{9,11},{12,14},{13,15},{16,18},{17,... | collective-permute-start | bytes 1544 | tf_op jit(solution)/shard_map/ppermute | solution.py:19
  14.3 92.7 %collective-permute-start.5 = (bf16[256]{0:T(256)(128)(2,1)S(1)}, bf16[256]{0:T(256)(128)(2,1)S(1)}, u32[]{:S(2)}, u32[]{:S(2)}) collective-permute-start(bf16[256]{0:T(256)(128)(2,1)S(1)} %convert_reduce_fusion.1), channel_id=1, source_target_pairs={{0,1},{1,2},{2,3},{4,5},{5,6},{6,7},{8,9},{9,10},{10,11},{12,13},{... | collective-permute-start | bytes 1544 | tf_op jit(solution)/shard_map/ppermute | solution.py:19
  15.7 91.7 %collective-permute-start.6 = (bf16[256]{0:T(256)(128)(2,1)S(1)}, bf16[256]{0:T(256)(128)(2,1)S(1)}, u32[]{:S(2)}, u32[]{:S(2)}) collective-permute-start(bf16[256]{0:T(256)(128)(2,1)S(1)} %convert_reduce_fusion.1), channel_id=1, source_target_pairs={{1,0},{2,1},{3,2},{5,4},{6,5},{7,6},{9,8},{10,9},{11,10},{13,12},{... | collective-permute-start | bytes 1544 | tf_op jit(solution)/shard_map/ppermute | solution.py:19
  17.0 90.6 %collective-permute-start.7 = (bf16[256]{0:T(256)(128)(2,1)S(1)}, bf16[256]{0:T(256)(128)(2,1)S(1)}, u32[]{:S(2)}, u32[]{:S(2)}) collective-permute-start(bf16[256]{0:T(256)(128)(2,1)S(1)} %convert_reduce_fusion.1), channel_id=1, source_target_pairs={{2,0},{3,1},{6,4},{7,5},{10,8},{11,9},{14,12},{15,13},{18,16},{19,... | collective-permute-start | bytes 1544 | tf_op jit(solution)/shard_map/ppermute | solution.py:19
  99.3 5.3 copy-start.3
  99.3 5.3 copy-start.11
  100.2 51.1 %collective-permute-start = (bf16[256,1280]{1,0:T(8,128)(2,1)}, bf16[256,1280]{1,0:T(8,128)(2,1)}, u32[]{:S(2)}, u32[]{:S(2)}) collective-permute-start(bf16[256,1280]{1,0:T(8,128)(2,1)} %slice.121), channel_id=1, source_target_pairs={{0,2},{1,3},{4,6},{5,7},{8,10},{9,11},{12,14},{13,15},{16,18},{17,... | collective-permute-start | bytes 1966088 | tf_op jit(solution)/shard_map/ppermute | solution.py:19
  107.6 44.9 %collective-permute-start.1 = (bf16[256,1280]{1,0:T(8,128)(2,1)}, bf16[256,1280]{1,0:T(8,128)(2,1)}, u32[]{:S(2)}, u32[]{:S(2)}) collective-permute-start(bf16[256,1280]{1,0:T(8,128)(2,1)} %slice.121), channel_id=1, source_target_pairs={{0,1},{1,2},{2,3},{4,5},{5,6},{6,7},{8,9},{9,10},{10,11},{12,13},{... | collective-permute-start | bytes 1966088 | tf_op jit(solution)/shard_map/ppermute | solution.py:19
  146.8 6.9 %collective-permute-start.2 = (bf16[256,1280]{1,0:T(8,128)(2,1)}, bf16[256,1280]{1,0:T(8,128)(2,1)}, u32[]{:S(2)}, u32[]{:S(2)}) collective-permute-start(bf16[256,1280]{1,0:T(8,128)(2,1)} %slice.121), channel_id=1, source_target_pairs={{1,0},{2,1},{3,2},{5,4},{6,5},{7,6},{9,8},{10,9},{11,10},{13,12},{... | collective-permute-start | bytes 1966088 | tf_op jit(solution)/shard_map/ppermute | solution.py:19
  148.1 25.0 %collective-permute-start.3 = (bf16[256,1280]{1,0:T(8,128)(2,1)}, bf16[256,1280]{1,0:T(8,128)(2,1)}, u32[]{:S(2)}, u32[]{:S(2)}) collective-permute-start(bf16[256,1280]{1,0:T(8,128)(2,1)} %slice.121), channel_id=1, source_target_pairs={{2,0},{3,1},{6,4},{7,5},{10,8},{11,9},{14,12},{15,13},{18,16},{19,... | collective-permute-start | bytes 1966088 | tf_op jit(solution)/shard_map/ppermute | solution.py:19
  151.3 2.4 copy-start.4
  296.9 260.7 %reduce-scatter.3.cloned.1.call-start = ((), (), s32[]{:S(2)}) async-start(), calls=%async_computation.4 | async-start | bytes 10813440 | tf_op jit(solution)/shard_map/reduce_scatter | solution.py:180
  296.9 12.0 %copy-start.1 = (bf16[1,256,1280]{2,1,0:T(8,128)(2,1)S(1)}, bf16[1,256,1280]{2,1,0:T(8,128)(2,1)}, u32[]{:S(2)}) copy-start(bf16[1,256,1280]{2,1,0:T(8,128)(2,1)} %param.32) | copy-start | bytes 1966084
  301.3 31.0 %collective-permute-start.11 = (f32[256,1280]{0,1:T(8,128)}, f32[256,1280]{0,1:T(8,128)}, u32[]{:S(2)}, u32[]{:S(2)}) collective-permute-start(f32[256,1280]{0,1:T(8,128)} %get-tuple-element.375), channel_id=1, source_target_pairs={{0,2},{1,3},{4,6},{5,7},{8,10},{9,11},{12,14},{13,15},{16,18},{17,... | collective-permute-start | bytes 3932168 | tf_op jit(solution)/shard_map/ppermute | solution.py:19
  303.8 28.5 %collective-permute-start.10 = (f32[256,1280]{0,1:T(8,128)}, f32[256,1280]{0,1:T(8,128)}, u32[]{:S(2)}, u32[]{:S(2)}) collective-permute-start(f32[256,1280]{0,1:T(8,128)} %get-tuple-element.376), channel_id=1, source_target_pairs={{0,1},{1,2},{2,3},{4,5},{5,6},{6,7},{8,9},{9,10},{10,11},{12,13},{... | collective-permute-start | bytes 3932168 | tf_op jit(solution)/shard_map/ppermute | solution.py:19
  306.2 26.1 %collective-permute-start.9 = (f32[256,1280]{0,1:T(8,128)}, f32[256,1280]{0,1:T(8,128)}, u32[]{:S(2)}, u32[]{:S(2)}) collective-permute-start(f32[256,1280]{0,1:T(8,128)} %get-tuple-element.374), channel_id=1, source_target_pairs={{1,0},{2,1},{3,2},{5,4},{6,5},{7,6},{9,8},{10,9},{11,10},{13,12},{... | collective-permute-start | bytes 3932168 | tf_op jit(solution)/shard_map/ppermute | solution.py:19
  307.5 51.2 %collective-permute-start.8 = (f32[256,1280]{0,1:T(8,128)}, f32[256,1280]{0,1:T(8,128)}, u32[]{:S(2)}, u32[]{:S(2)}) collective-permute-start(f32[256,1280]{0,1:T(8,128)} %get-tuple-element.373), channel_id=1, source_target_pairs={{2,0},{3,1},{6,4},{7,5},{10,8},{11,9},{14,12},{15,13},{18,16},{19,... | collective-permute-start | bytes 3932168 | tf_op jit(solution)/shard_map/ppermute | solution.py:19
  312.3 49.7 %copy-start.9 = (bf16[10,256,64]{1,2,0:T(8,128)(2,1)S(1)}, bf16[10,256,64]{1,2,0:T(8,128)(2,1)}, u32[]{:S(2)}) copy-start(bf16[10,256,64]{1,2,0:T(8,128)(2,1)} %get-tuple-element.299) | copy-start | bytes 983044
  371.9 4.3 copy-start.8
  (4 other events, 4.8 us)
Sparse Core Ops, SparseCore 0:
  10.2 84.9 all-gather.2
  97.4 42.6 all-gather.4
  297.0 106.3 reduce-scatter.4
  405.5 151.9 reduce-scatter.2
where the time goes:
time: 570 us; the launch traced here: 566 us
  waiting for transfers between devices  350 us (61%)
  matrix products  115 us (20%)
  local copies, waits for them, and re-layouts  33.8 us (6%)
  other arithmetic  27 us (5%)
  starting transfers between devices  25.7 us (5%)
  between operations  14.1 us (2%)
    reduce_scatter x1, waiting for transfers between devices, body(): lax.psum_scatter(blocked(normed, grad_projected), ('dp', 'seq'), scatter_...  153 us
    all_gather x1, waiting for transfers between devices, body(): lax.all_gather(w_qkv, 'dp', axis=0, tiled=True)  75.3 us
    ppermute x12, waiting for transfers between devices, from_behind(): lax.ppermute(value, axis, [(source, source + steps) for source in range(l...  64.7 us
    dot_general x22, matrix products, against(): lax.dot_general(left, right, (((1,), (1,)), ((), ())), preferred_element_...  38.1 us
    all_gather x1, waiting for transfers between devices, body(): lax.all_gather(w_out, 'dp', axis=0, tiled=True)  30.4 us
    dot_general x20, matrix products, leading(): lax.dot_general(left, right, (((0,), (0,)), ((), ())), preferred_element_...  29 us
    reduce_scatter x1, waiting for transfers between devices, body(): lax.psum_scatter(blocked(attention, upstream), ('dp', 'seq'), scatter_dim...  25.8 us
    ppermute x12, starting transfers between devices, from_behind(): lax.ppermute(value, axis, [(source, source + steps) for source in range(l...  25.5 us
  transfers between devices with their start and end apart: 16, of which 7 were waited for; matrix products, arithmetic and copies ran while one was open for 8% of the time, Pallas kernels for 0%

commit v1 on v0

--- a/solution.py
+++ b/solution.py
@@ -1,8 +1,11 @@
+import functools
 import math
 
 import jax
 import jax.numpy as jnp
 from jax import lax
+from jax.experimental import pallas as pl
+from jax.experimental.pallas import tpu as pltpu
 from jax.sharding import PartitionSpec as P
 
 HEAD_DIM = 64
@@ -187,9 +190,247 @@
     return (grad_rows, sum_qkv * factor, sum_out * factor)
 
 
+def swap(value, flip):
+    count = lax.axis_size("seq")
+    return lax.ppermute(value, "seq", [(source, source ^ flip) for source in range(count)])
+
+
+def attend_kernel(score_scale, blocks, q_ref, g_ref, k_ref, v_ref, ends_ref, live_ref, qlive_ref,
+                  att_ref, dq_ref, own_ref, other_ref, bias_ref):
+    rows = q_ref.shape[1] // blocks
+    span = k_ref.shape[1]
+
+    @pl.when(pl.program_id(0) == 0)
+    def _():
+        for block in range(blocks):
+            columns = slice(block * rows, (block + 1) * rows)
+            near = jnp.abs(ends_ref[...] - qlive_ref[0:1, columns]) <= WIN
+            bias_ref[:, columns] = jnp.where(near & (live_ref[...] > 0.5), 0.0, NEG)
+
+    key_t, value_t = k_ref[...], v_ref[...]
+    key = key_t.T
+    value = value_t.T
+    key_grad = jnp.zeros((span, HEAD_DIM), jnp.float32)
+    value_grad = jnp.zeros((span, HEAD_DIM), jnp.float32)
+    for block in range(blocks):
+        columns = slice(block * rows, (block + 1) * rows)
+        query_t, grad_t = q_ref[:, columns], g_ref[:, columns]
+        scores = jnp.dot(key, query_t, preferred_element_type=jnp.float32) * score_scale
+        scores = scores + bias_ref[:, columns]
+        exponent = jnp.exp(scores - jnp.max(scores, axis=0, keepdims=True))
+        inverse = 1.0 / jnp.sum(exponent, axis=0, keepdims=True)
+        probabilities = exponent * inverse
+        probs_b = probabilities.astype(jnp.bfloat16)
+        mixed = jnp.dot(value_t, probs_b, preferred_element_type=jnp.float32)
+        attended = (mixed * qlive_ref[1:2, columns]).astype(jnp.bfloat16)
+        att_ref[:, columns] = attended
+        row_delta = jnp.sum(
+            grad_t.astype(jnp.float32) * attended.astype(jnp.float32), axis=0, keepdims=True
+        )
+        grad_probs = jnp.dot(value, grad_t, preferred_element_type=jnp.float32)
+        grad_scores = (probabilities * ((grad_probs - row_delta) * score_scale)).astype(
+            jnp.bfloat16
+        )
+        dq_ref[:, columns] = jnp.dot(
+            key_t, grad_scores, preferred_element_type=jnp.float32
+        ).astype(jnp.bfloat16)
+        key_grad += against(grad_scores, query_t)
+        value_grad += against(probs_b, grad_t)
+    half = span // 2
+    key_grad_t, value_grad_t = key_grad.T, value_grad.T
+    own_ref[0] = key_grad_t[:, :half]
+    own_ref[1] = value_grad_t[:, :half]
+    other_ref[0] = key_grad_t[:, half:].astype(jnp.bfloat16)
+    other_ref[1] = value_grad_t[:, half:].astype(jnp.bfloat16)
+
+
+def attend(query_t, grad_t, key_t, value_t, key_pos, key_live, query_rows, blocks, score_scale):
+    features, queries = query_t.shape
+    span = key_t.shape[1]
+    half = span // 2
+    heads = features // HEAD_DIM
+    by_query = pl.BlockSpec((HEAD_DIM, queries), lambda h: (h, 0))
+    by_key = pl.BlockSpec((HEAD_DIM, span), lambda h: (h, 0))
+    grads = pl.BlockSpec((2, HEAD_DIM, half), lambda h: (0, h, 0))
+    return pl.pallas_call(
+        functools.partial(attend_kernel, score_scale, blocks),
+        grid=(heads,),
+        in_specs=[
+            by_query,
+            by_query,
+            by_key,
+            by_key,
+            pl.BlockSpec((span, 1), lambda h: (0, 0)),
+            pl.BlockSpec((span, 1), lambda h: (0, 0)),
+            pl.BlockSpec((2, queries), lambda h: (0, 0)),
+        ],
+        out_specs=[by_query, by_query, grads, grads],
+        out_shape=[
+            jax.ShapeDtypeStruct((features, queries), jnp.bfloat16),
+            jax.ShapeDtypeStruct((features, queries), jnp.bfloat16),
+            jax.ShapeDtypeStruct((2, features, half), jnp.float32),
+            jax.ShapeDtypeStruct((2, features, half), jnp.bfloat16),
+        ],
+        scratch_shapes=[pltpu.VMEM((span, queries), jnp.float32)],
+        compiler_params=pltpu.CompilerParams(vmem_limit_bytes=40 * 2**20),
+        cost_estimate=pl.CostEstimate(
+            flops=10 * features * queries * span,
+            bytes_accessed=12 * features * span,
+            transcendentals=heads * queries * span,
+        ),
+    )(query_t, grad_t, key_t, value_t, key_pos, key_live, query_rows)
+
+
+def head_body(frames, live, norm_gain, w_qkv, w_out, cotangent):
+    length, width = frames.shape[1:]
+    n_data = lax.axis_size("dp")
+    n_seq = lax.axis_size("seq")
+    me = lax.axis_index("seq")
+    high, low = me // 2, me % 2
+    shard = w_qkv.shape[0]
+    inner = w_qkv.shape[1] // 3
+    part = inner // 2
+    score_scale = 1.0 / math.sqrt(HEAD_DIM)
+
+    mine_qkv = lax.dynamic_index_in_dim(w_qkv.reshape(shard, 3, 2, part), high, 2, keepdims=False)
+    mine_qkv = lax.dynamic_slice_in_dim(
+        mine_qkv.reshape(shard, 3 * part), low * (shard // 2), shard // 2, 0
+    )
+    mine_out = lax.dynamic_slice_in_dim(w_out, low * (width // 2), width // 2, 1)
+    gathered = lax.all_gather(
+        jnp.concatenate([mine_qkv, mine_out], axis=1), "dp", axis=0, tiled=True
+    )
+
+    upstream = cotangent[0]
+    marks = jnp.zeros((16, width), jnp.bfloat16).at[0, :length].set(live[0].astype(jnp.bfloat16))
+    packed = jnp.concatenate([frames[0], marks], axis=0)
+    packs = [packed, swap(packed, 2), swap(packed, 1), swap(packed, 3)]
+    cots = jnp.concatenate([upstream, swap(upstream, 2)], axis=0)
+    rows = jnp.concatenate([pack[:length] for pack in packs], axis=0)
+    key_live = jnp.concatenate([pack[length, :length] for pack in packs], axis=0)
+    key_live = key_live.astype(jnp.float32)
+    step = jnp.arange(length, dtype=jnp.float32)
+    key_pos = jnp.concatenate(
+        [step + ((me ^ flip) * length).astype(jnp.float32) for flip in (0, 2, 1, 3)]
+    )
+    queries = 2 * length
+    query_live = key_live[:queries]
+
+    unit_rows, inverse = norm_rows(rows.astype(jnp.float32))
+    normed = (unit_rows * norm_gain).astype(jnp.bfloat16)
+
+    other_qkv = swap(gathered[:, : 3 * part], 1)
+    own_out = lax.dynamic_slice_in_dim(gathered[:, 3 * part :], high * part, part, 0)
+    other_out = swap(own_out, 1)
+    own_qkv = gathered[:, : 3 * part]
+    first = low == 0
+
+    def ordered(own, other, axis):
+        return jnp.concatenate(
+            [jnp.where(first, own, other), jnp.where(first, other, own)], axis=axis
+        )
+
+    part_qkv = ordered(
+        own_qkv.reshape(n_data, shard // 2, 3 * part),
+        other_qkv.reshape(n_data, shard // 2, 3 * part),
+        1,
+    ).reshape(n_data * shard, 3 * part)
+    part_out = ordered(own_out, other_out, 1)
+
+    def turned(weights, values):
+        return lax.dot_general(
+            weights, values, (((0,), (1,)), ((), ())), preferred_element_type=jnp.float32
+        )
+
+    query_t = turned(part_qkv[:, :part], normed[:queries]).astype(jnp.bfloat16)
+    pairs_t = turned(part_qkv[:, part:], normed).astype(jnp.bfloat16)
+    grad_t = (against(part_out, cots) * query_live[None, :]).astype(jnp.bfloat16)
+
+    query_rows = jnp.stack([key_pos[:queries], query_live])
+    att_t, dq_t, own_grads, other_grads = attend(
+        query_t, grad_t, pairs_t[:part], pairs_t[part:],
+        key_pos[:, None], key_live[:, None], query_rows, 2, score_scale,
+    )
+    own_grads = own_grads + swap(other_grads, 1).astype(jnp.float32)
+
+    block = width // n_seq
+    partial_out = jnp.dot(att_t, cots, preferred_element_type=jnp.float32)
+
+    def columns_of(flip):
+        return lax.dynamic_slice_in_dim(partial_out, (me ^ flip) * block, block, 1)
+
+    arrived = [swap(columns_of(flip).astype(jnp.bfloat16), flip) for flip in (1, 2, 3)]
+    arrived = [value.astype(jnp.float32) for value in arrived]
+    same, across = columns_of(0) + arrived[0], arrived[1] + arrived[2]
+    sum_out = jnp.concatenate(
+        [jnp.where(high == 0, same, across), jnp.where(high == 0, across, same)], axis=0
+    )
+
+    grads_t = jnp.concatenate(
+        [dq_t, own_grads.reshape(2 * part, queries).astype(jnp.bfloat16)], axis=0
+    )
+    unit = part // 2
+    units = grads_t.reshape(6, unit, queries)
+    kept = jnp.array([[0, 1, 4], [2, 3, 5], [2, 3, 0], [4, 5, 1]], jnp.int32)
+
+    def pick(index):
+        chosen = lax.dynamic_index_in_dim(kept, index, 0, keepdims=False)
+        return jnp.concatenate(
+            [lax.dynamic_slice_in_dim(units, chosen[i], 1, 0)[0] for i in range(3)], axis=0
+        )
+
+    keep_t = jnp.concatenate([pick(me), swap(pick(me ^ 1), 1)], axis=1)
+    sum_qkv = lax.dot_general(
+        normed, keep_t, (((0,), (1,)), ((), ())), preferred_element_type=jnp.float32
+    )
+
+    def through_weights(piece):
+        return lax.dot_general(
+            piece, part_qkv, (((0,), (1,)), ((), ())), preferred_element_type=jnp.float32
+        )
+
+    sent = through_weights(grads_t[:, length:]).astype(jnp.bfloat16)
+    grad_unit = through_weights(grads_t[:, :length]) + swap(sent, 2).astype(jnp.float32)
+    grad_unit = grad_unit * norm_gain
+    own_unit = unit_rows[:length]
+    through = inverse[:length] * (
+        grad_unit
+        - jnp.mean(grad_unit, axis=-1, keepdims=True)
+        - own_unit * jnp.mean(grad_unit * own_unit, axis=-1, keepdims=True)
+    )
+    grad_rows = (upstream.astype(jnp.float32) + through).astype(jnp.bfloat16)[None]
+
+    out_rows = sum_out.shape[0] // n_data
+    stacked = jnp.concatenate(
+        [sum_qkv, sum_out.reshape(n_data * shard, out_rows * block // shard)], axis=1
+    ).astype(jnp.bfloat16)
+    total = lax.psum_scatter(stacked, "dp", scatter_dimension=0, tiled=True)
+    factor = 1.0 / math.sqrt(n_data * n_seq * length)
+    moved = swap(total[:, 2 * unit : 3 * unit], 2)
+    own = total[:, : 2 * unit]
+    tile_qkv = jnp.where(
+        first,
+        jnp.concatenate([own, moved], axis=1),
+        jnp.concatenate([moved, own], axis=1),
+    ).astype(jnp.float32)
+    tile_out = total[:, 3 * unit :].astype(jnp.float32).reshape(out_rows, block)
+    return (grad_rows, tile_qkv * factor, tile_out * factor)
+
+
 def solution(mesh):
+    n_seq = mesh.shape["seq"]
+
+    def whole(frames, live, norm_gain, w_qkv, w_out, cotangent):
+        heads_fit = n_seq == 4 and frames.shape[1] <= frames.shape[1] // n_seq + 2 * WIN
+        chosen = head_body if heads_fit else body
+        return split(chosen, mesh)(frames, live, norm_gain, w_qkv, w_out, cotangent)
+
+    return whole
+
+
+def split(chosen, mesh):
     return jax.shard_map(
-        body,
+        chosen,
         mesh=mesh,
         in_specs=(
             P("dp", "seq", None),

time: 570 us -> 227 us (0.40)
  waiting for transfers between devices: 350 us -> 101 us
  matrix products: 115 us -> 14.2 us
  Pallas kernels: 0 us -> 18.1 us
  starting transfers between devices: 25.7 us -> 11.4 us
  between operations: 14.1 us -> 25.7 us
  other arithmetic: 27 us -> 18.1 us
    reduce_scatter x2 -> x0, waiting for transfers between devices: 178 us -> none  [the longest x1 153 us: body(): lax.psum_scatter(blocked(normed, grad_projected), ('dp', 'seq'), scatter_...]
    all_gather x2 -> x1, waiting for transfers between devices: 106 us -> 8.75 us  [head_body(): lax.all_gather(jnp.concatenate([mine_qkv, mine_out], axis=1), 'dp', axis=...]
    dot_general x43 -> x6, matrix products: 77 us -> 12.3 us  [the longest x2 4.48 us: through_weights(): lax.dot_general(piece, part_qkv, (((0,), (1,)), ((), ())), preferred_elem...]
    unnamed x4 -> x3, waiting for transfers between devices: 1.41 us -> 40.5 us
    dot_general x22 -> x1, matrix products: 38.1 us -> 1.91 us  [against(): lax.dot_general(left, right, (((1,), (1,)), ((), ())), preferred_element_...]
    pallas_call x0 -> x1, Pallas kernels: none -> 18.1 us  [attend(): pl.pallas_call(functools.partial(attend_kernel, score_scale, blocks), gri...]
    ppermute x12 -> x13, starting transfers between devices: 25.5 us -> 11.3 us  [swap(): lax.ppermute(value, 'seq', [(source, source ^ flip) for source in range(c...]
    ppermute x12 -> x13, waiting for transfers between devices: 64.7 us -> 52.1 us  [swap(): lax.ppermute(value, 'seq', [(source, source ^ flip) for source in range(c...]
  transfers between devices with their start and end apart: 16 -> 15, of which waited for: 7 -> 9; matrix products, arithmetic and copies ran while one was open for 8% -> 18% of each run, Pallas kernels for 0% -> 0%
where the time goes in v1:
time: 227 us; the launch traced here: 226 us
  waiting for transfers between devices  101 us (44%)
  local copies, waits for them, and re-layouts  36.9 us (16%)
  between operations  25.7 us (11%)
  other arithmetic  18.1 us (8%)
  Pallas kernels  18.1 us (8%)
  matrix products  14.2 us (6%)
  starting transfers between devices  11.4 us (5%)
    ppermute x13, waiting for transfers between devices, swap(): lax.ppermute(value, 'seq', [(source, source ^ flip) for source in range(c...  52.1 us
    unnamed x3, waiting for transfers between devices  40.5 us
    pallas_call x1, Pallas kernels, attend(): pl.pallas_call(functools.partial(attend_kernel, score_scale, blocks), gri...  18.1 us
    ppermute x13, starting transfers between devices, swap(): lax.ppermute(value, 'seq', [(source, source ^ flip) for source in range(c...  11.3 us
    unnamed x33, local copies, waits for them, and re-layouts  9.21 us
    all_gather x1, waiting for transfers between devices, head_body(): lax.all_gather(jnp.concatenate([mine_qkv, mine_out], axis=1), 'dp', axis=...  8.75 us
  transfers between devices with their start and end apart: 15, of which 9 were waited for; matrix products, arithmetic and copies ran while one was open for 18% of the time, Pallas kernels for 0%

profile of v1, /device:TPU:0, one launch (start us, length us, event | category | flops | bytes accessed | tf_op | source)
XLA Modules:
  0.0 225.7 jit_solution(1534961296793929039)
XLA Ops:
  7.3 2.4 %reshape.174 = bf16[160,3,2,320]{3,2,1,0:T(2,128)(2,1)S(1)} reshape(bf16[160,1920]{1,0:T(8,128)(2,1)} %param.12) | data formatting | bytes 1228800 | tf_op jit(solution)/shard_map/reshape | solution.py:295
  9.7 2.5 %dynamic-slice_reduce_fusion = bf16[160,3,320]{2,1,0:T(4,128)(2,1)S(1)} fusion(bf16[160,3,2,320]{3,2,1,0:T(2,128)(2,1)S(1)} %reshape.174, s32[]{:T(128)S(6)} %select_n.114), kind=kLoop, calls=%fused_computation.45 | loop fusion | bytes 614404 | tf_op jit(solution)/shard_map/jit(dynamic_index_in_dim)/dynamic_slice | solution.py:295
  13.6 2.5 %collective-permute-start.2 = (bf16[272,1280]{1,0:T(8,128)(2,1)S(1)}, bf16[272,1280]{1,0:T(8,128)(2,1)}, u32[]{:S(2)}, u32[]{:S(2)}) collective-permute-start(bf16[272,1280]{1,0:T(8,128)(2,1)S(1)} %fusion.27), channel_id=1, source_target_pairs={{0,3},{1,2},{2,1},{3,0},{4,7},{5,6},{6,5},{7,4},{8,11},{9,10},{10,... | collective-permute-start | bytes 2088968 | tf_op jit(solution)/shard_map/ppermute | solution.py:195
  16.8 2.0 collective-permute-start.5
  19.1 13.0 %collective-permute-done.2 = bf16[272,1280]{1,0:T(8,128)(2,1)} collective-permute-done((bf16[272,1280]{1,0:T(8,128)(2,1)S(1)}, bf16[272,1280]{1,0:T(8,128)(2,1)}, u32[]{:S(2)}, u32[]{:S(2)}) %collective-permute-start.2) | collective-permute-done | bytes 696352 | tf_op jit(solution)/shard_map/ppermute | solution.py:195
  34.4 13.7 %collective-permute-done = bf16[272,1280]{1,0:T(8,128)(2,1)} collective-permute-done((bf16[272,1280]{1,0:T(8,128)(2,1)S(1)}, bf16[272,1280]{1,0:T(8,128)(2,1)}, u32[]{:S(2)}, u32[]{:S(2)}) %collective-permute-start) | collective-permute-done | bytes 696352 | tf_op jit(solution)/shard_map/ppermute | solution.py:195
  50.4 2.6 %fusion.2 = f32[1024]{0:T(1024)S(1)} fusion(f32[1024]{0:T(1024)S(1)} %broadcast_multiply_fusion, bf16[256,1280]{1,0:T(8,128)(2,1)S(1)} %slice.139, bf16[256,1280]{1,0:T(8,128)(2,1)S(1)} %slice.138, bf16[256,1280]{1,0:T(8,128)(2,1)S(1)} %slice.137, bf16[256,1280]{1,0:T(8,128)(2,1)S(1)} %bitcast.47), kind=kLoop, calls=%fused_computation.4 | loop fusion | flops 14416896 | bytes 2629632 | tf_op jit(solution)/shard_map/reduce_sum | solution.py:28
  53.0 4.3 %multiply_convert_fusion = (bf16[1024,1280]{1,0:T(8,128)(2,1)}, f32[1024,1280]{1,0:T(8,128)}) fusion(f32[1280]{0:T(1024)S(1)} %copy-done.10, f32[1024]{0:T(1024)S(1)} %add_rsqrt_fusion, f32[1024]{0:T(1024)S(1)} %broadcast_multiply_fusion, bf16[256,1280]{1,0:T(8,128)(2,1)S(1)} %slice.139, bf16[256,1280]{1,0:T(8,128)(2,1)S(1)} %slice.138, ...), kind=kLoop, calls=%fused_computation.5 | loop fusion | flops 15728640 | bytes 10499072 | tf_op jit(solution)/shard_map/convert_element_type | solution.py:320
  57.4 8.7 %all-gather.2.cloned.1.call-done = bf16[640,1600]{1,0:T(8,128)(2,1)} async-done(((bf16[80,1600]{1,0:T(8,128)(2,1)}), bf16[640,1600]{1,0:T(8,128)(2,1)}) %all-gather.2.cloned.1.call-update) | async-done | bytes 2048016 | tf_op jit(solution)/shard_map/all_gather | solution.py:300
  73.3 1.9 fusion.14.g_ref
  78.8 2.3 copy-done.7
  81.9 2.5 %fusion.5 = bf16[640,1024]{1,0:T(8,128)(2,1)S(1)} fusion(bf16[1024,1280]{1,0:T(8,128)(2,1)S(1)} %copy-done.7, bf16[1280,960]{1,0:T(8,128)(2,1)S(1)} %bitcast.50), kind=kOutput, calls=%fused_computation.13 | convolution fusion | flops 1678376960 | bytes 5570560 | tf_op jit(solution)/shard_map/dot_general | solution.py:341
  84.5 18.1 %shard_map.94 = (bf16[320,512]{1,0:T(8,128)(2,1)S(1)}, bf16[320,512]{1,0:T(8,128)(2,1)S(1)}, f32[2,320,512]{2,1,0:T(8,128)S(1)}, bf16[2,320,512]{2,1,0:T(8,128)(2,1)}) custom-call(bf16[320,512]{1,0:T(8,128)(2,1)S(1)} %fusion.11.q_ref, bf16[320,512]{1,0:T(8,128)(2,1)S(1)} %fusion.14.g_ref, bf16[320,1024]{1,0:T(8,128)(2,1)S(1)} %get-tuple-element.47.k_ref, ...), custom_call_target="tpu_custom_call" | custom-call | flops 1677721600 | bytes 3932160 | tf_op jit(solution)/shard_map/pallas_call | solution.py:255
  124.5 3.4 %collective-permute-done.11 = bf16[320,320]{1,0:T(8,128)(2,1)} collective-permute-done((bf16[320,320]{1,0:T(8,128)(2,1)}, bf16[320,320]{1,0:T(8,128)(2,1)}, u32[]{:S(2)}, u32[]{:S(2)}) %collective-permute-start.11) | collective-permute-done | bytes 204832 | tf_op jit(solution)/shard_map/ppermute | solution.py:195
  127.9 5.7 %collective-permute-done.10 = bf16[320,320]{1,0:T(8,128)(2,1)} collective-permute-done((bf16[320,320]{1,0:T(8,128)(2,1)}, bf16[320,320]{1,0:T(8,128)(2,1)}, u32[]{:S(2)}, u32[]{:S(2)}) %collective-permute-start.10) | collective-permute-done | bytes 204832 | tf_op jit(solution)/shard_map/ppermute | solution.py:195
  136.1 2.3 %reshape.178 = bf16[1280,160]{1,0:T(8,128)(2,1)} reshape(bf16[640,320]{1,0:T(8,128)(2,1)} %pad_maximum_fusion.8) | data formatting | bytes 819200 | tf_op jit(solution)/shard_map/reshape | solution.py:405
  138.4 2.1 copy.35
  140.5 2.6 %convolution_convert_fusion = bf16[1280,480]{0,1:T(8,128)(2,1)S(1)} fusion(bf16[1024,1280]{1,0:T(8,128)(2,1)S(1)} %copy-done.8, bf16[480,512]{1,0:T(8,128)(2,1)} %collective-permute-done.8, bf16[160,512]{1,0:T(8,128)(2,1)S(1)} %get-tuple-element.52, bf16[160,512]{1,0:T(8,128)(2,1)} %get-tuple-element.53, bf16[160,512]{1,0:T(8,128)(2,1)S(1)} %get-tuple-element.48), kind=kOutput, calls=%fused_computation.6 | convolution fusion | flops 1262837760 | bytes 4833280 | tf_op jit(solution)/shard_map/dot_general | solution.py:383
  144.3 3.7 %copy.38 = bf16[1280,640]{1,0:T(8,128)(2,1)} copy(bf16[1280,640]{0,1:T(8,128)(2,1)} %pad_maximum_fusion.2) | data formatting | bytes 3276800
  148.1 2.0 convolution_convert_fusion.1
  151.6 14.8 %collective-permute-done.7 = bf16[256,1280]{1,0:T(8,128)(2,1)S(1)} collective-permute-done((bf16[256,1280]{1,0:T(8,128)(2,1)S(1)}, bf16[256,1280]{1,0:T(8,128)(2,1)S(1)}, u32[]{:S(2)}, u32[]{:S(2)}) %collective-permute-start.7) | collective-permute-done | bytes 655392 | tf_op jit(solution)/shard_map/ppermute | solution.py:195
  166.4 2.5 %fusion.41 = (f32[256]{0:T(256)S(1)}, f32[256]{0:T(256)S(1)}, f32[256,1280]{1,0:T(8,128)S(1)}) fusion(f32[1024,1280]{1,0:T(8,128)} %get-tuple-element.38, f32[1280]{0:T(1024)S(1)} %copy-done.11, bf16[256,1280]{1,0:T(8,128)(2,1)S(1)} %collective-permute-done.7, bf16[1280,960]{1,0:T(8,128)(2,1)S(1)} %bitcast.52, bf16[640,512]{1,0:T(8,128)(2,1)S(1)} %bitcast.55, ...), kind=kOutput, calls=%fused_computation.101 | convolution fusion | flops 632094208 | bytes 6724608 | tf_op jit(solution)/shard_map/dot_general | solution.py:388
  168.9 2.7 %fusion.28 = bf16[1,256,1280]{2,1,0:T(8,128)(2,1)} fusion(f32[1024,1280]{1,0:T(8,128)} %get-tuple-element.38, f32[256,1280]{1,0:T(8,128)S(1)} %get-tuple-element.70, f32[256]{0:T(256)S(1)} %broadcast_multiply_fusion.1, f32[256]{0:T(256)S(1)} %broadcast_multiply_fusion.2, f32[256]{0:T(256)S(1)} %slice-done.1, bf16[1,256,1280]{2,1,0:T(8,128)(2,1)} %param.14), kind=kLoop, calls=%fused_computation.47 | loop fusion | flops 2293760 | bytes 3935232 | tf_op jit(solution)/shard_map/broadcast_in_dim | solution.py:401
  171.6 40.5 %reduce-scatter.4.cloned.1.call-done = bf16[160,640]{1,0:T(8,128)(2,1)} async-done(((bf16[1280,640]{1,0:T(8,128)(2,1)}), bf16[160,640]{1,0:T(8,128)(2,1)}) %reduce-scatter.4.cloned.1.call-update) | async-done | bytes 204816
  (111 shorter events, 41.4 us)
Async XLA Ops:
  7.2 5.4 %copy-start = (bf16[80,1280]{1,0:T(8,128)(2,1)S(1)}, bf16[80,1280]{1,0:T(8,128)(2,1)}, u32[]{:S(2)}) copy-start(bf16[80,1280]{1,0:T(8,128)(2,1)} %param.13) | copy-start | bytes 614404
  7.2 6.4 %copy-start.13 = (s32[1,256]{1,0:T(1,128)S(1)}, s32[1,256]{1,0:T(1,128)}, u32[]{:S(2)}) copy-start(s32[1,256]{1,0:T(1,128)} %param.10) | copy-start | bytes 3076
  7.2 6.4 %copy-start.1 = (bf16[1,256,1280]{2,1,0:T(8,128)(2,1)S(1)}, bf16[1,256,1280]{2,1,0:T(8,128)(2,1)}, u32[]{:S(2)}) copy-start(bf16[1,256,1280]{2,1,0:T(8,128)(2,1)} %param.9) | copy-start | bytes 1966084
  7.2 58.9 %all-gather.2.cloned.1.call-start = ((), (), s32[]{:S(2)}) async-start(), calls=%async_computation.1 | async-start | bytes 2396160 | tf_op jit(solution)/shard_map/all_gather | solution.py:300
  13.5 198.6 %reduce-scatter.4.cloned.1.call-start = ((), (), s32[]{:S(2)}) async-start(), calls=%async_computation.2 | async-start | bytes 1843200
  13.6 18.5 %collective-permute-start.2 = (bf16[272,1280]{1,0:T(8,128)(2,1)S(1)}, bf16[272,1280]{1,0:T(8,128)(2,1)}, u32[]{:S(2)}, u32[]{:S(2)}) collective-permute-start(bf16[272,1280]{1,0:T(8,128)(2,1)S(1)} %fusion.27), channel_id=1, source_target_pairs={{0,3},{1,2},{2,1},{3,0},{4,7},{5,6},{6,5},{7,4},{8,11},{9,10},{10,... | collective-permute-start | bytes 2088968 | tf_op jit(solution)/shard_map/ppermute | solution.py:195
  16.1 17.1 %collective-permute-start.1 = (bf16[272,1280]{1,0:T(8,128)(2,1)S(1)}, bf16[272,1280]{1,0:T(8,128)(2,1)}, u32[]{:S(2)}, u32[]{:S(2)}) collective-permute-start(bf16[272,1280]{1,0:T(8,128)(2,1)S(1)} %fusion.27), channel_id=1, source_target_pairs={{0,1},{1,0},{2,3},{3,2},{4,5},{5,4},{6,7},{7,6},{8,9},{9,8},{10,11... | collective-permute-start | bytes 2088968 | tf_op jit(solution)/shard_map/ppermute | solution.py:195
  16.8 31.4 %collective-permute-start = (bf16[272,1280]{1,0:T(8,128)(2,1)S(1)}, bf16[272,1280]{1,0:T(8,128)(2,1)}, u32[]{:S(2)}, u32[]{:S(2)}) collective-permute-start(bf16[272,1280]{1,0:T(8,128)(2,1)S(1)} %fusion.27), channel_id=1, source_target_pairs={{0,2},{1,3},{2,0},{3,1},{4,6},{5,7},{6,4},{7,5},{8,10},{9,11},{10,... | collective-permute-start | bytes 2088968 | tf_op jit(solution)/shard_map/ppermute | solution.py:195
  16.8 56.5 %collective-permute-start.5 = (bf16[256,1280]{1,0:T(8,128)(2,1)}, bf16[256,1280]{1,0:T(8,128)(2,1)}, u32[]{:S(2)}, u32[]{:S(2)}) collective-permute-start(bf16[256,1280]{1,0:T(8,128)(2,1)} %bitcast), channel_id=1, source_target_pairs={{0,2},{1,3},{2,0},{3,1},{4,6},{5,7},{6,4},{7,5},{8,10},{9,11},{10,... | collective-permute-start | bytes 1966088 | tf_op jit(solution)/shard_map/ppermute | solution.py:195
  53.0 98.5 %copy-start.12 = (f32[1024]{0:T(1024)}, f32[1024]{0:T(1024)S(1)}, u32[]{:S(2)}) copy-start(f32[1024]{0:T(1024)S(1)} %add_rsqrt_fusion) | copy-start | bytes 12292
  68.9 6.4 %collective-permute-start.3 = (bf16[640,960]{0,1:T(8,128)(2,1)}, bf16[640,960]{0,1:T(8,128)(2,1)}, u32[]{:S(2)}, u32[]{:S(2)}) collective-permute-start(bf16[640,960]{0,1:T(8,128)(2,1)} %copy.30), channel_id=1, source_target_pairs={{0,1},{1,0},{2,3},{3,2},{4,5},{5,4},{6,7},{7,6},{8,9},{9,8},{10,11... | collective-permute-start | bytes 3686408 | tf_op jit(solution)/shard_map/ppermute | solution.py:195
  71.2 1.9 collective-permute-start.4
  78.8 5.6 %copy-start.2 = (bf16[8,160,960]{2,1,0:T(8,128)(2,1)}, bf16[8,160,960]{2,1,0:T(8,128)(2,1)S(1)}, u32[]{:S(2)}) copy-start(bf16[8,160,960]{2,1,0:T(8,128)(2,1)S(1)} %pad_maximum_fusion.1) | copy-start | bytes 7372804
  102.6 19.2 %collective-permute-start.6 = (bf16[2,320,512]{2,1,0:T(8,128)(2,1)}, bf16[2,320,512]{2,1,0:T(8,128)(2,1)S(1)}, u32[]{:S(2)}, u32[]{:S(2)}) collective-permute-start(bf16[2,320,512]{2,1,0:T(8,128)(2,1)} %get-tuple-element.21), channel_id=1, source_target_pairs={{0,1},{1,0},{2,3},{3,2},{4,5},{5,4},{6,7},{7,6},{8,9},{9,8},{10,11... | collective-permute-start | bytes 1966088 | tf_op jit(solution)/shard_map/ppermute | solution.py:195
  119.6 4.9 %collective-permute-start.9 = (bf16[320,320]{1,0:T(8,128)(2,1)}, bf16[320,320]{1,0:T(8,128)(2,1)}, u32[]{:S(2)}, u32[]{:S(2)}) collective-permute-start(bf16[320,320]{1,0:T(8,128)(2,1)} %get-tuple-element.43), channel_id=1, source_target_pairs={{0,1},{1,0},{2,3},{3,2},{4,5},{5,4},{6,7},{7,6},{8,9},{9,8},{10,11... | collective-permute-start | bytes 614408 | tf_op jit(solution)/shard_map/ppermute | solution.py:195
  119.8 8.1 %collective-permute-start.11 = (bf16[320,320]{1,0:T(8,128)(2,1)}, bf16[320,320]{1,0:T(8,128)(2,1)}, u32[]{:S(2)}, u32[]{:S(2)}) collective-permute-start(bf16[320,320]{1,0:T(8,128)(2,1)} %get-tuple-element.44), channel_id=1, source_target_pairs={{0,3},{1,2},{2,1},{3,0},{4,7},{5,6},{6,5},{7,4},{8,11},{9,10},{10,... | collective-permute-start | bytes 614408 | tf_op jit(solution)/shard_map/ppermute | solution.py:195
  121.2 12.4 %collective-permute-start.10 = (bf16[320,320]{1,0:T(8,128)(2,1)}, bf16[320,320]{1,0:T(8,128)(2,1)}, u32[]{:S(2)}, u32[]{:S(2)}) collective-permute-start(bf16[320,320]{1,0:T(8,128)(2,1)} %get-tuple-element.45), channel_id=1, source_target_pairs={{0,2},{1,3},{2,0},{3,1},{4,6},{5,7},{6,4},{7,5},{8,10},{9,11},{10,... | collective-permute-start | bytes 614408 | tf_op jit(solution)/shard_map/ppermute | solution.py:195
  124.5 15.9 %copy-start.8 = (bf16[1024,1280]{1,0:T(8,128)(2,1)S(1)}, bf16[1024,1280]{1,0:T(8,128)(2,1)}, u32[]{:S(2)}) copy-start(bf16[1024,1280]{1,0:T(8,128)(2,1)} %get-tuple-element.37) | copy-start | bytes 7864324
  124.5 15.9 %collective-permute-start.8 = (bf16[480,512]{1,0:T(8,128)(2,1)}, bf16[480,512]{1,0:T(8,128)(2,1)}, u32[]{:S(2)}, u32[]{:S(2)}) collective-permute-start(bf16[480,512]{1,0:T(8,128)(2,1)} %pad_maximum_fusion.7), channel_id=1, source_target_pairs={{0,1},{1,0},{2,3},{3,2},{4,5},{5,4},{6,7},{7,6},{8,9},{9,8},{10,11... | collective-permute-start | bytes 1474568 | tf_op jit(solution)/shard_map/ppermute | solution.py:195
  144.3 3.7 %copy-start.3 = (bf16[8,160,960]{2,1,0:T(8,128)(2,1)S(1)}, bf16[8,160,960]{2,1,0:T(8,128)(2,1)}, u32[]{:S(2)}) copy-start(bf16[8,160,960]{2,1,0:T(8,128)(2,1)} %copy-done.2) | copy-start | bytes 7372804
  148.0 18.3 %copy-start.6 = (bf16[2,320,512]{2,1,0:T(8,128)(2,1)S(1)}, bf16[2,320,512]{2,1,0:T(8,128)(2,1)}, u32[]{:S(2)}) copy-start(bf16[2,320,512]{2,1,0:T(8,128)(2,1)} %copy-done.5) | copy-start | bytes 1966084
  148.0 18.3 %copy-start.11 = (f32[1280]{0:T(1024)S(1)}, f32[1280]{0:T(1024)}, u32[]{:S(2)}) copy-start(f32[1280]{0:T(1024)} %param.11) | copy-start | bytes 15364
  150.0 16.3 %collective-permute-start.7 = (bf16[256,1280]{1,0:T(8,128)(2,1)S(1)}, bf16[256,1280]{1,0:T(8,128)(2,1)S(1)}, u32[]{:S(2)}, u32[]{:S(2)}) collective-permute-start(bf16[256,1280]{1,0:T(8,128)(2,1)S(1)} %convolution_convert_fusion.1), channel_id=1, source_target_pairs={{0,2},{1,3},{2,0},{3,1},{4,6},{5,7},{6,4},{7,5},{8,10},{9,11},{10,... | collective-permute-start | bytes 1966088 | tf_op jit(solution)/shard_map/ppermute | solution.py:195
  213.4 4.5 %collective-permute-start.12 = (bf16[160,160]{0,1:T(8,128)(2,1)S(1)}, bf16[160,160]{0,1:T(8,128)(2,1)S(1)}, u32[]{:S(2)}, u32[]{:S(2)}) collective-permute-start(bf16[160,160]{0,1:T(8,128)(2,1)S(1)} %copy.42), channel_id=1, source_target_pairs={{0,2},{1,3},{2,0},{3,1},{4,6},{5,7},{6,4},{7,5},{8,10},{9,11},{10,... | collective-permute-start | bytes 153608 | tf_op jit(solution)/shard_map/ppermute | solution.py:195
  (7 other events, 14.2 us)
Sparse Core Ops, SparseCore 0:
  13.6 52.4 all-gather.1
  148.1 63.9 reduce-scatter.3

commit v2 on v1

--- a/solution.py
+++ b/solution.py
@@ -281,6 +281,239 @@
     )(query_t, grad_t, key_t, value_t, key_pos, key_live, query_rows)
 
 
+MESH = pl.DeviceIdType.MESH
+
+
+def gather_kernel(piece_ref, out_ref, line_send, line_recv, side_send, side_recv,
+                  core_send, core_recv, local_sem):
+    count = out_ref.shape[0]
+    dp, seq = lax.axis_index("dp"), lax.axis_index("seq")
+    z, x, core = dp // 2, dp % 2, seq % 2
+    mate = seq + 1 - 2 * core
+    steps = 2 * count - 1
+    above, below = z < count - 1, z > 0
+
+    barrier = pltpu.get_barrier_semaphore()
+    pl.semaphore_signal(barrier, inc=1, device_id={"dp": 2 * z + 1 - x}, device_id_type=MESH)
+    pl.semaphore_signal(barrier, inc=1, device_id={"seq": mate}, device_id_type=MESH)
+
+    @pl.when(above)
+    def _():
+        pl.semaphore_signal(barrier, inc=1, device_id={"dp": dp + 2}, device_id_type=MESH)
+
+    @pl.when(below)
+    def _():
+        pl.semaphore_signal(barrier, inc=1, device_id={"dp": dp - 2}, device_id_type=MESH)
+
+    pl.semaphore_wait(barrier, 2 + above.astype(jnp.int32) + below.astype(jnp.int32))
+
+    def line(hop, up):
+        origin = z - hop if up else z + hop
+        source = piece_ref if hop == 0 else out_ref.at[origin, x, core]
+        flow = 0 if up else 1
+        return pltpu.make_async_remote_copy(
+            src_ref=source, dst_ref=out_ref.at[origin, x, core],
+            send_sem=line_send.at[flow, hop], recv_sem=line_recv.at[flow, hop],
+            device_id={"dp": dp + 2 if up else dp - 2}, device_id_type=MESH,
+        )
+
+    def line_arrival(hop, up):
+        origin = z - hop if up else z + hop
+        flow = 0 if up else 1
+        return pltpu.make_async_remote_copy(
+            src_ref=piece_ref, dst_ref=out_ref.at[origin, x, core],
+            send_sem=line_send.at[flow, hop - 1], recv_sem=line_recv.at[flow, hop - 1],
+            device_id={"dp": dp + 2 if up else dp - 2}, device_id_type=MESH,
+        )
+
+    def side(step, origin, column):
+        source = piece_ref if step == 0 else out_ref.at[origin, x, core]
+        return pltpu.make_async_remote_copy(
+            src_ref=source, dst_ref=out_ref.at[origin, column, core],
+            send_sem=side_send.at[step], recv_sem=side_recv.at[step],
+            device_id={"dp": 2 * z + 1 - x}, device_id_type=MESH,
+        )
+
+    def across(slot, origin, column, half):
+        source = piece_ref if slot == 0 else out_ref.at[origin, column, core]
+        return pltpu.make_async_remote_copy(
+            src_ref=source, dst_ref=out_ref.at[origin, column, half],
+            send_sem=core_send.at[slot], recv_sem=core_recv.at[slot],
+            device_id={"seq": mate}, device_id_type=MESH,
+        )
+
+    waves = [(0, z, None)]
+    for hop in range(1, count):
+        waves.append((hop, z - hop, z >= hop))
+        waves.append((count - 1 + hop, z + hop, z + hop < count))
+
+    def guarded(condition, action):
+        if condition is None:
+            action()
+        else:
+            pl.when(condition)(action)
+
+    keep = pltpu.make_async_copy(piece_ref, out_ref.at[z, x, core], local_sem)
+    keep.start()
+    pl.when(above)(lambda: line(0, True).start())
+    pl.when(below)(lambda: line(0, False).start())
+    side(0, z, x).start()
+    across(0, z, x, core).start()
+
+    def side_wave(step, origin):
+        side(step, origin, 1 - x).wait_recv()
+        across(steps + step, origin, 1 - x, core).start()
+
+    for step, origin, condition in waves[1:]:
+        up = step < count
+        hop = step if up else step - count + 1
+
+        def forward(step=step, origin=origin, up=up, hop=hop):
+            line_arrival(hop, up).wait_recv()
+            if hop < count - 1:
+                pl.when(above if up else below)(lambda: line(hop, up).start())
+            side(step, origin, x).start()
+            across(step, origin, x, core).start()
+
+        guarded(condition, forward)
+        if not up:
+            for late, place, holds in waves:
+                late_hop = late if late < count else late - count + 1
+                if late_hop == hop - 1:
+                    guarded(holds, functools.partial(side_wave, late, place))
+    for late, place, holds in waves[-2:]:
+        guarded(holds, functools.partial(side_wave, late, place))
+
+    keep.wait()
+    for step, origin, condition in waves:
+        def finish(step=step, origin=origin):
+            side(step, origin, x).wait_send()
+            across(step, origin, x, core).wait_send()
+            across(steps + step, origin, 1 - x, core).wait_send()
+            across(step, origin, x, 1 - core).wait_recv()
+            across(steps + step, origin, 1 - x, 1 - core).wait_recv()
+            up = step < count
+            hop = step if up else step - count + 1
+            if step == 0:
+                pl.when(above)(lambda: line(0, True).wait_send())
+                pl.when(below)(lambda: line(0, False).wait_send())
+            elif hop < count - 1:
+                pl.when(above if up else below)(lambda: line(hop, up).wait_send())
+
+        guarded(condition, finish)
+
+
+def gather_pieces(piece, count):
+    steps = 2 * count - 1
+    dma = pltpu.SemaphoreType.DMA
+    return pl.pallas_call(
+        gather_kernel,
+        out_shape=jax.ShapeDtypeStruct((count, 2, 2) + piece.shape, piece.dtype),
+        in_specs=[pl.BlockSpec(memory_space=pltpu.VMEM)],
+        out_specs=pl.BlockSpec(memory_space=pltpu.VMEM),
+        scratch_shapes=[
+            dma((2, count)), dma((2, count)), dma((steps,)), dma((steps,)),
+            dma((2 * steps,)), dma((2 * steps,)), dma(()),
+        ],
+        compiler_params=pltpu.CompilerParams(
+            collective_id=0, has_side_effects=True, vmem_limit_bytes=24 * 2**20
+        ),
+        cost_estimate=pl.CostEstimate(
+            flops=0, bytes_accessed=64 * piece.size * count, transcendentals=0
+        ),
+    )(piece)
+
+
+def sum_kernel(chunks, factor, *refs):
+    ins, outs = refs[:2], refs[2:4]
+    beside, summed, lined = refs[4:6], refs[6:8], refs[8:10]
+    side_send, side_recv, line_send, line_recv = refs[10:]
+    count = ins[0].shape[0]
+    dp = lax.axis_index("dp")
+    z, x = dp // 2, dp % 2
+    neighbour = 2 * z + 1 - x
+    peers = [lax.rem(z + step, count) for step in range(1, count)]
+
+    barrier = pltpu.get_barrier_semaphore()
+    pl.semaphore_signal(barrier, inc=1, device_id={"dp": neighbour}, device_id_type=MESH)
+    for peer in peers:
+        pl.semaphore_signal(barrier, inc=1, device_id={"dp": 2 * peer + x}, device_id_type=MESH)
+    pl.semaphore_wait(barrier, count)
+
+    def rows_of(which, chunk):
+        size = ins[which].shape[2] // chunks
+        return pl.ds(chunk * size, size)
+
+    def side(which, chunk):
+        return pltpu.make_async_remote_copy(
+            src_ref=ins[which].at[:, 1 - x, rows_of(which, chunk)],
+            dst_ref=beside[which].at[chunk],
+            send_sem=side_send.at[which, chunk], recv_sem=side_recv.at[which, chunk],
+            device_id={"dp": neighbour}, device_id_type=MESH,
+        )
+
+    def line(which, chunk, step):
+        peer = peers[step]
+        return pltpu.make_async_remote_copy(
+            src_ref=summed[which].at[chunk, peer],
+            dst_ref=lined[which].at[chunk, step],
+            send_sem=line_send.at[which, chunk, step], recv_sem=line_recv.at[which, chunk, step],
+            device_id={"dp": 2 * peer + x}, device_id_type=MESH,
+        )
+
+    both = [(chunk, which) for chunk in range(chunks) for which in (0, 1)]
+    for chunk, which in both:
+        side(which, chunk).start()
+    for chunk, which in both:
+        side(which, chunk).wait_recv()
+        for step in range(count - 1):
+            peer = peers[step]
+            summed[which][chunk, peer] = (
+                ins[which][peer, x, rows_of(which, chunk)].astype(jnp.float32)
+                + beside[which][chunk, peer].astype(jnp.float32)
+            ).astype(jnp.bfloat16)
+            line(which, chunk, step).start()
+    for chunk, which in both:
+        total = ins[which][z, x, rows_of(which, chunk)].astype(jnp.float32)
+        total = total + beside[which][chunk, z].astype(jnp.float32)
+        for step in range(count - 1):
+            line(which, chunk, step).wait_recv()
+            total = total + lined[which][chunk, step].astype(jnp.float32)
+        outs[which][rows_of(which, chunk)] = total * factor
+    for chunk, which in both:
+        side(which, chunk).wait_send()
+        for step in range(count - 1):
+            line(which, chunk, step).wait_send()
+
+
+def sum_tiles(arrays, count, chunks, factor):
+    tiles = [a.reshape(count, 2, a.shape[0] // (2 * count), a.shape[1]) for a in arrays]
+    vmem = pl.BlockSpec(memory_space=pltpu.VMEM)
+    dma = pltpu.SemaphoreType.DMA
+
+    def slots(lead):
+        return [
+            pltpu.VMEM((chunks, lead, t.shape[2] // chunks, t.shape[3]), t.dtype) for t in tiles
+        ]
+
+    return pl.pallas_call(
+        functools.partial(sum_kernel, chunks, factor),
+        out_shape=[jax.ShapeDtypeStruct(t.shape[2:], jnp.float32) for t in tiles],
+        in_specs=[vmem, vmem],
+        out_specs=[vmem, vmem],
+        scratch_shapes=slots(count) + slots(count) + slots(count - 1) + [
+            dma((2, chunks)), dma((2, chunks)),
+            dma((2, chunks, count - 1)), dma((2, chunks, count - 1)),
+        ],
+        compiler_params=pltpu.CompilerParams(
+            collective_id=1, has_side_effects=True, vmem_limit_bytes=24 * 2**20
+        ),
+        cost_estimate=pl.CostEstimate(
+            flops=0, bytes_accessed=64 * tiles[0].size, transcendentals=0
+        ),
+    )(*tiles)
+
+
 def head_body(frames, live, norm_gain, w_qkv, w_out, cotangent):
     length, width = frames.shape[1:]
     n_data = lax.axis_size("dp")
@@ -297,9 +530,7 @@
         mine_qkv.reshape(shard, 3 * part), low * (shard // 2), shard // 2, 0
     )
     mine_out = lax.dynamic_slice_in_dim(w_out, low * (width // 2), width // 2, 1)
-    gathered = lax.all_gather(
-        jnp.concatenate([mine_qkv, mine_out], axis=1), "dp", axis=0, tiled=True
-    )
+    packed_weights = jnp.concatenate([mine_out, mine_qkv], axis=1)
 
     upstream = cotangent[0]
     marks = jnp.zeros((16, width), jnp.bfloat16).at[0, :length].set(live[0].astype(jnp.bfloat16))
@@ -319,23 +550,13 @@
     unit_rows, inverse = norm_rows(rows.astype(jnp.float32))
     normed = (unit_rows * norm_gain).astype(jnp.bfloat16)
 
-    other_qkv = swap(gathered[:, : 3 * part], 1)
-    own_out = lax.dynamic_slice_in_dim(gathered[:, 3 * part :], high * part, part, 0)
-    other_out = swap(own_out, 1)
-    own_qkv = gathered[:, : 3 * part]
-    first = low == 0
-
-    def ordered(own, other, axis):
-        return jnp.concatenate(
-            [jnp.where(first, own, other), jnp.where(first, other, own)], axis=axis
-        )
-
-    part_qkv = ordered(
-        own_qkv.reshape(n_data, shard // 2, 3 * part),
-        other_qkv.reshape(n_data, shard // 2, 3 * part),
-        1,
-    ).reshape(n_data * shard, 3 * part)
-    part_out = ordered(own_out, other_out, 1)
+    gathered = gather_pieces(packed_weights, n_data // 2)
+    part_qkv = gathered[..., width // 2 :].reshape(n_data * shard, 3 * part)
+    halves = gathered[..., : width // 2].reshape(n_data, 2, shard // 2, width // 2)
+    halves = lax.dynamic_slice_in_dim(halves, high * (n_data // 2), n_data // 2, 0)
+    part_out = jnp.concatenate(
+        [halves[:, half].reshape(part, width // 2) for half in (0, 1)], axis=1
+    )
 
     def turned(weights, values):
         return lax.dot_general(
@@ -370,16 +591,21 @@
         [dq_t, own_grads.reshape(2 * part, queries).astype(jnp.bfloat16)], axis=0
     )
     unit = part // 2
-    units = grads_t.reshape(6, unit, queries)
-    kept = jnp.array([[0, 1, 4], [2, 3, 5], [2, 3, 0], [4, 5, 1]], jnp.int32)
-
-    def pick(index):
-        chosen = lax.dynamic_index_in_dim(kept, index, 0, keepdims=False)
-        return jnp.concatenate(
-            [lax.dynamic_slice_in_dim(units, chosen[i], 1, 0)[0] for i in range(3)], axis=0
-        )
-
-    keep_t = jnp.concatenate([pick(me), swap(pick(me ^ 1), 1)], axis=1)
+
+    def units(start, count):
+        return lax.dynamic_slice_in_dim(grads_t, start * unit, count * unit, 0)
+
+    beside = swap(units(2 * (high + 1 - low), 2), 1)
+    facing = swap(units(4 * (1 - high) + low, 1), 2)
+    corner = swap(units(4 * (1 - high) + 1 - low, 1), 3)
+    two = jnp.concatenate([units(2 * (high + low), 2), beside], axis=1)
+    one = jnp.concatenate(
+        [facing[:, length:], facing[:, :length], corner[:, length:], corner[:, :length]], axis=1
+    )
+    first = low == 0
+    keep_t = jnp.where(
+        first, jnp.concatenate([two, one], axis=0), jnp.concatenate([one, two], axis=0)
+    )
     sum_qkv = lax.dot_general(
         normed, keep_t, (((0,), (1,)), ((), ())), preferred_element_type=jnp.float32
     )
@@ -389,8 +615,12 @@
             piece, part_qkv, (((0,), (1,)), ((), ())), preferred_element_type=jnp.float32
         )
 
-    sent = through_weights(grads_t[:, length:]).astype(jnp.bfloat16)
-    grad_unit = through_weights(grads_t[:, :length]) + swap(sent, 2).astype(jnp.float32)
+    arrived = swap(through_weights(grads_t[:, length:]).astype(jnp.bfloat16), 2)
+    factor = 1.0 / math.sqrt(n_data * n_seq * length)
+    tile_qkv, tile_out = sum_tiles(
+        [sum_qkv.astype(jnp.bfloat16), sum_out.astype(jnp.bfloat16)], n_data // 2, 5, factor
+    )
+    grad_unit = through_weights(grads_t[:, :length]) + arrived.astype(jnp.float32)
     grad_unit = grad_unit * norm_gain
     own_unit = unit_rows[:length]
     through = inverse[:length] * (
@@ -400,28 +630,14 @@
     )
     grad_rows = (upstream.astype(jnp.float32) + through).astype(jnp.bfloat16)[None]
 
-    out_rows = sum_out.shape[0] // n_data
-    stacked = jnp.concatenate(
-        [sum_qkv, sum_out.reshape(n_data * shard, out_rows * block // shard)], axis=1
-    ).astype(jnp.bfloat16)
-    total = lax.psum_scatter(stacked, "dp", scatter_dimension=0, tiled=True)
-    factor = 1.0 / math.sqrt(n_data * n_seq * length)
-    moved = swap(total[:, 2 * unit : 3 * unit], 2)
-    own = total[:, : 2 * unit]
-    tile_qkv = jnp.where(
-        first,
-        jnp.concatenate([own, moved], axis=1),
-        jnp.concatenate([moved, own], axis=1),
-    ).astype(jnp.float32)
-    tile_out = total[:, 3 * unit :].astype(jnp.float32).reshape(out_rows, block)
-    return (grad_rows, tile_qkv * factor, tile_out * factor)
+    return (grad_rows, tile_qkv, tile_out)
 
 
 def solution(mesh):
     n_seq = mesh.shape["seq"]
 
     def whole(frames, live, norm_gain, w_qkv, w_out, cotangent):
-        heads_fit = n_seq == 4 and frames.shape[1] <= frames.shape[1] // n_seq + 2 * WIN
+        heads_fit = n_seq == 4 and mesh.shape["dp"] == 8 and frames.shape[1] <= frames.shape[1] // n_seq + 2 * WIN
         chosen = head_body if heads_fit else body
         return split(chosen, mesh)(frames, live, norm_gain, w_qkv, w_out, cotangent)
 

time: 227 us -> 163 us (0.72)
  waiting for transfers between devices: 101 us -> 14.5 us
  Pallas kernels: 18.1 us -> 75.5 us
  between operations: 25.7 us -> 1.22 us
  local copies, waits for them, and re-layouts: 36.9 us -> 19.1 us
  matrix products: 14.2 us -> 21.1 us
    pallas_call x0 -> x2, Pallas kernels: none -> 57.8 us  [the longest x1 31.9 us: gather_pieces(): pl.pallas_call(gather_kernel, out_shape=jax.ShapeDtypeStruct((count, 2, 2...]
    unnamed x3 -> x0, waiting for transfers between devices: 40.5 us -> none
    ppermute x13 -> x12, waiting for transfers between devices: 52.1 us -> 14.5 us  [swap(): lax.ppermute(value, 'seq', [(source, source ^ flip) for source in range(c...]
    all_gather x1 -> x0, waiting for transfers between devices: 8.75 us -> none  [head_body(): lax.all_gather(jnp.concatenate([mine_qkv, mine_out], axis=1), 'dp', axis=...]
    dot_general x1, matrix products: 2.57 us -> 9.07 us  [head_body(): lax.dot_general(normed, keep_t, (((0,), (1,)), ((), ())), preferred_eleme...]
    unnamed x33 -> x38, local copies, waits for them, and re-layouts: 9.21 us -> 3.06 us
    reshape x2 -> x0, local copies, waits for them, and re-layouts: 4.32 us -> none  [head_body(): sum_out.reshape(n_data * shard, out_rows * block // shard)]
    slice x7 -> x5, local copies, waits for them, and re-layouts: 6.92 us -> 2.99 us  [the longest x1 1.88 us: head_body(): part_qkv = gathered[..., width // 2:].reshape(n_data * shard, 3 * part)]
  transfers between devices with their start and end apart: 15 -> 12, of which waited for: 9 -> 4; matrix products, arithmetic and copies ran while one was open for 18% -> 27% of each run, Pallas kernels for 0% -> 36%
where the time goes in v2:
time: 163 us; the launch traced here: 161 us
  Pallas kernels  75.5 us (46%)
  matrix products  21.1 us (13%)
  other arithmetic  19.3 us (12%)
  local copies, waits for them, and re-layouts  19.1 us (12%)
  waiting for transfers between devices  14.5 us (9%)
  starting transfers between devices  10.5 us (6%)
    pallas_call x1, Pallas kernels, gather_pieces(): pl.pallas_call(gather_kernel, out_shape=jax.ShapeDtypeStruct((count, 2, 2...  31.9 us
    pallas_call x1, Pallas kernels, sum_tiles(): pl.pallas_call(functools.partial(sum_kernel, chunks, factor), out_shape=[...  25.9 us
    pallas_call x1, Pallas kernels, attend(): pl.pallas_call(functools.partial(attend_kernel, score_scale, blocks), gri...  17.7 us
    ppermute x12, waiting for transfers between devices, swap(): lax.ppermute(value, 'seq', [(source, source ^ flip) for source in range(c...  14.5 us
    ppermute x12, starting transfers between devices, swap(): lax.ppermute(value, 'seq', [(source, source ^ flip) for source in range(c...  10.5 us
    dot_general x1, matrix products, head_body(): lax.dot_general(normed, keep_t, (((0,), (1,)), ((), ())), preferred_eleme...  9.07 us
    dot_general x2, matrix products, through_weights(): lax.dot_general(piece, part_qkv, (((0,), (1,)), ((), ())), preferred_elem...  5.29 us
    convert_element_type x1, other arithmetic, head_body(): normed = (unit_rows * norm_gain).astype(jnp.bfloat16)  5.2 us
  transfers between devices with their start and end apart: 12, of which 4 were waited for; matrix products, arithmetic and copies ran while one was open for 27% of the time, Pallas kernels for 36%

profile of v2, /device:TPU:0, one launch (start us, length us, event | category | flops | bytes accessed | tf_op | source)
XLA Modules:
  0.0 161.3 jit_solution(13663177089681222467)
XLA Ops:
  1.4 2.0 %fusion.42 = bf16[272,1280]{1,0:T(8,128)(2,1)} fusion(bf16[1,256]{1,0:T(2,128)(2,1)S(1)} %get-tuple-element.51, bf16[256,1280]{1,0:T(8,128)(2,1)} %bitcast.30), kind=kLoop, calls=%fused_computation.65 | loop fusion | flops 2088960 | bytes 1352192 | tf_op jit(solution)/shard_map/concatenate | solution.py:537
  3.4 2.4 %collective-permute-start.2 = (bf16[272,1280]{1,0:T(8,128)(2,1)}, bf16[272,1280]{1,0:T(8,128)(2,1)}, u32[]{:S(2)}, u32[]{:S(2)}) collective-permute-start(bf16[272,1280]{1,0:T(8,128)(2,1)} %fusion.42), channel_id=1, source_target_pairs={{0,3},{1,2},{2,1},{3,0},{4,7},{5,6},{6,5},{7,4},{8,11},{9,10},{10,... | collective-permute-start | bytes 2088968 | tf_op jit(solution)/shard_map/ppermute | solution.py:195
  6.5 2.0 %collective-permute-start.3 = (bf16[256,1280]{1,0:T(8,128)(2,1)}, bf16[256,1280]{1,0:T(8,128)(2,1)}, u32[]{:S(2)}, u32[]{:S(2)}) collective-permute-start(bf16[256,1280]{1,0:T(8,128)(2,1)} %bitcast.43), channel_id=1, source_target_pairs={{0,2},{1,3},{2,0},{3,1},{4,6},{5,7},{6,4},{7,5},{8,10},{9,11},{10,... | collective-permute-start | bytes 1966088 | tf_op jit(solution)/shard_map/ppermute | solution.py:195
  8.5 2.3 %reshape.155 = bf16[160,3,2,320]{3,2,1,0:T(2,128)(2,1)S(1)} reshape(bf16[160,1920]{1,0:T(8,128)(2,1)} %param.11) | data formatting | bytes 1228800 | tf_op jit(solution)/shard_map/reshape | solution.py:528
  10.8 2.5 %dynamic-slice_reduce_fusion = bf16[160,3,320]{2,1,0:T(4,128)(2,1)S(1)} fusion(bf16[160,3,2,320]{3,2,1,0:T(2,128)(2,1)S(1)} %reshape.155, s32[]{:T(128)S(6)} %select_n.71), kind=kLoop, calls=%fused_computation.64 | loop fusion | bytes 614404 | tf_op jit(solution)/shard_map/jit(dynamic_index_in_dim)/dynamic_slice | solution.py:528
  13.8 31.9 %shard_map.85 = bf16[4,2,2,80,1600]{4,3,2,1,0:T(8,128)(2,1)S(1)} custom-call(bf16[80,1600]{1,0:T(8,128)(2,1)S(1)} %pad_maximum_fusion.5.piece_ref), custom_call_target="tpu_custom_call" | custom-call | bytes 32768000 | tf_op jit(solution)/shard_map/pallas_call | solution.py:409
  45.8 1.9 %slice.98 = bf16[4,2,2,80,960]{4,3,2,1,0:T(8,128)(2,1)} slice(bf16[4,2,2,80,1600]{4,3,2,1,0:T(8,128)(2,1)S(1)} %shard_map.85), slice={[0:4], [0:2], [0:2], [0:80], [640:1600]} | slice | bytes 4915200 | tf_op jit(solution)/shard_map/slice | solution.py:554
  54.0 2.6 %fusion.2 = f32[1024]{0:T(1024)S(1)} fusion(f32[1024]{0:T(1024)S(1)} %broadcast_multiply_fusion, bf16[256,1280]{1,0:T(8,128)(2,1)S(1)} %slice.120, bf16[256,1280]{1,0:T(8,128)(2,1)S(1)} %slice.119, bf16[256,1280]{1,0:T(8,128)(2,1)S(1)} %slice.118, bf16[256,1280]{1,0:T(8,128)(2,1)S(1)} %bitcast.32), kind=kLoop, calls=%fused_computation.4 | loop fusion | flops 14416896 | bytes 2629632 | tf_op jit(solution)/shard_map/reduce_sum | solution.py:28
  59.0 5.2 %multiply_convert_fusion = (bf16[1024,1280]{1,0:T(8,128)(2,1)S(1)}, f32[1024,1280]{1,0:T(8,128)}) fusion(f32[1280]{0:T(1024)S(1)} %copy-done.13, f32[1024]{0:T(1024)S(1)} %add_rsqrt_fusion, f32[1024]{0:T(1024)S(1)} %broadcast_multiply_fusion, bf16[256,1280]{1,0:T(8,128)(2,1)S(1)} %slice.120, bf16[256,1280]{1,0:T(8,128)(2,1)S(1)} %slice.119, ...), kind=kLoop, calls=%fused_computation.5 | loop fusion | flops 15728640 | bytes 10499072 | tf_op jit(solution)/shard_map/convert_element_type | solution.py:551
  64.2 2.5 %fusion.5 = bf16[640,1024]{1,0:T(8,128)(2,1)S(1)} fusion(bf16[1024,1280]{1,0:T(8,128)(2,1)S(1)} %get-tuple-element.29, bf16[1280,960]{1,0:T(8,128)(2,1)S(1)} %bitcast.35), kind=kOutput, calls=%fused_computation.17 | convolution fusion | flops 1678376960 | bytes 5570560 | tf_op jit(solution)/shard_map/dot_general | solution.py:562
  68.2 1.7 %fusion.14.g_ref = bf16[320,512]{1,0:T(8,128)(2,1)S(1)} fusion(bf16[256,1280]{1,0:T(8,128)(2,1)} %collective-permute-done.3, bf16[256,1280]{1,0:T(8,128)(2,1)S(1)} %bitcast.44, bf16[320,640]{1,0:T(8,128)(2,1)S(1)} %bitcast.47, bf16[320,640]{1,0:T(8,128)(2,1)S(1)} %bitcast.46, f32[512]{0:T(512)S(1)} %maximum_convert_fusion.1), kind=kOutput, calls=%fused_computation.29 | convolution fusion | flops 424017920 | bytes 2459648 | tf_op jit(solution)/shard_map/dot_general | solution.py:33
  69.9 17.7 %shard_map.86 = (bf16[320,512]{1,0:T(8,128)(2,1)S(1)}, bf16[320,512]{1,0:T(8,128)(2,1)S(1)}, f32[2,320,512]{2,1,0:T(8,128)S(1)}, bf16[2,320,512]{2,1,0:T(8,128)(2,1)S(1)}) custom-call(bf16[320,512]{1,0:T(8,128)(2,1)S(1)} %fusion.11.q_ref, bf16[320,512]{1,0:T(8,128)(2,1)S(1)} %fusion.14.g_ref, bf16[320,1024]{1,0:T(8,128)(2,1)S(1)} %get-tuple-element.39.k_ref, ...), custom_call_target="tpu_custom_call" | custom-call | flops 1677721600 | bytes 3932160 | tf_op jit(solution)/shard_map/pallas_call | solution.py:255
  88.0 1.7 %fusion.38 = f32[320,1280]{1,0:T(8,128)S(1)} fusion(bf16[320,512]{1,0:T(8,128)(2,1)S(1)} %get-tuple-element.24, bf16[256,1280]{1,0:T(8,128)(2,1)} %collective-permute-done.3, bf16[256,1280]{1,0:T(8,128)(2,1)S(1)} %bitcast.45), kind=kOutput, calls=%fused_computation.60 | convolution fusion | flops 422051840 | bytes 3276800 | tf_op jit(solution)/shard_map/dot_general | solution.py:578
  91.9 1.5 collective-permute-start.10
  93.4 5.9 %collective-permute-done.11 = bf16[320,320]{1,0:T(8,128)(2,1)} collective-permute-done((bf16[320,320]{1,0:T(8,128)(2,1)S(1)}, bf16[320,320]{1,0:T(8,128)(2,1)}, u32[]{:S(2)}, u32[]{:S(2)}) %collective-permute-start.11) | collective-permute-done | bytes 204832 | tf_op jit(solution)/shard_map/ppermute | solution.py:195
  99.3 5.7 %collective-permute-done.10 = bf16[320,320]{1,0:T(8,128)(2,1)} collective-permute-done((bf16[320,320]{1,0:T(8,128)(2,1)S(1)}, bf16[320,320]{1,0:T(8,128)(2,1)}, u32[]{:S(2)}, u32[]{:S(2)}) %collective-permute-start.10) | collective-permute-done | bytes 204832 | tf_op jit(solution)/shard_map/ppermute | solution.py:195
  105.0 1.6 select_convert_fusion.1
  112.0 1.7 %convolution_convert_fusion.1 = bf16[256,1280]{1,0:T(8,128)(2,1)} fusion(bf16[1280,960]{1,0:T(8,128)(2,1)S(1)} %bitcast.37, bf16[640,512]{1,0:T(8,128)(2,1)S(1)} %bitcast.40, bf16[320,512]{1,0:T(8,128)(2,1)S(1)} %get-tuple-element.21), kind=kOutput, calls=%fused_computation.8 | convolution fusion | flops 630456320 | bytes 4096000 | tf_op jit(solution)/shard_map/dot_general | solution.py:614
  114.3 1.6 collective-permute-done.7
  117.2 9.1 %convolution_convert_fusion = bf16[1280,480]{0,1:T(8,128)(2,1)} fusion(bf16[1024,1280]{1,0:T(8,128)(2,1)S(1)} %copy-done.8, bf16[160,256]{1,0:T(8,128)(2,1)S(1)} %get-tuple-element.49, bf16[160,256]{1,0:T(8,128)(2,1)S(1)} %get-tuple-element.48, bf16[160,256]{1,0:T(8,128)(2,1)S(1)} %get-tuple-element.47, bf16[160,256]{1,0:T(8,128)(2,1)S(1)} %get-tuple-element.46, ...), kind=kOutput, calls=%fused_computation.6 | convolution fusion | flops 1271193600 | bytes 4833281 | tf_op jit(solution)/shard_map/dot_general | solution.py:609
  126.2 1.6 copy.25
  127.8 25.9 %shard_map.87 = (f32[160,480]{1,0:T(8,128)S(1)}, f32[80,320]{1,0:T(8,128)S(1)}) custom-call(bf16[4,2,160,480]{3,2,1,0:T(8,128)(2,1)S(1)} %bitcast.28, bf16[4,2,80,320]{3,2,1,0:T(8,128)(2,1)S(1)} %bitcast.29), custom_call_target="tpu_custom_call" | custom-call | bytes 39321600 | tf_op jit(solution)/shard_map/pallas_call | solution.py:499
  153.8 3.6 %fusion.60 = (f32[256]{0:T(256)S(1)}, f32[256]{0:T(256)S(1)}, f32[256,1280]{1,0:T(8,128)S(1)}) fusion(f32[1024,1280]{1,0:T(8,128)} %get-tuple-element.30, f32[1280]{0:T(1024)S(1)} %copy-done.13, bf16[256,1280]{1,0:T(8,128)(2,1)} %collective-permute-done.5, bf16[1280,960]{1,0:T(8,128)(2,1)} %bitcast.34, bf16[640,512]{1,0:T(8,128)(2,1)} %bitcast.41, ...), kind=kOutput, calls=%fused_computation.111 | convolution fusion | flops 632094208 | bytes 6724608 | tf_op jit(solution)/shard_map/dot_general | solution.py:614
  157.4 2.5 %fusion.43 = bf16[1,256,1280]{2,1,0:T(8,128)(2,1)} fusion(f32[1024,1280]{1,0:T(8,128)} %get-tuple-element.30, f32[256,1280]{1,0:T(8,128)S(1)} %get-tuple-element.52, f32[256]{0:T(256)S(1)} %broadcast_multiply_fusion.1, f32[256]{0:T(256)S(1)} %broadcast_multiply_fusion.2, f32[256]{0:T(256)S(1)} %slice-done, bf16[1,256,1280]{2,1,0:T(8,128)(2,1)S(1)} %copy-done.10), kind=kLoop, calls=%fused_computation.66 | loop fusion | flops 2293760 | bytes 3935232 | tf_op jit(solution)/shard_map/broadcast_in_dim | solution.py:631
  (95 shorter events, 23.0 us)
Async XLA Ops:
  0.6 13.0 %copy-start = (bf16[80,1280]{1,0:T(8,128)(2,1)S(1)}, bf16[80,1280]{1,0:T(8,128)(2,1)}, u32[]{:S(2)}) copy-start(bf16[80,1280]{1,0:T(8,128)(2,1)} %param.12) | copy-start | bytes 614404
  3.4 46.7 %collective-permute-start.2 = (bf16[272,1280]{1,0:T(8,128)(2,1)}, bf16[272,1280]{1,0:T(8,128)(2,1)}, u32[]{:S(2)}, u32[]{:S(2)}) collective-permute-start(bf16[272,1280]{1,0:T(8,128)(2,1)} %fusion.42), channel_id=1, source_target_pairs={{0,3},{1,2},{2,1},{3,0},{4,7},{5,6},{6,5},{7,4},{8,11},{9,10},{10,... | collective-permute-start | bytes 2088968 | tf_op jit(solution)/shard_map/ppermute | solution.py:195
  5.8 45.4 %collective-permute-start.1 = (bf16[272,1280]{1,0:T(8,128)(2,1)}, bf16[272,1280]{1,0:T(8,128)(2,1)}, u32[]{:S(2)}, u32[]{:S(2)}) collective-permute-start(bf16[272,1280]{1,0:T(8,128)(2,1)} %fusion.42), channel_id=1, source_target_pairs={{0,1},{1,0},{2,3},{3,2},{4,5},{5,4},{6,7},{7,6},{8,9},{9,8},{10,11... | collective-permute-start | bytes 2088968 | tf_op jit(solution)/shard_map/ppermute | solution.py:195
  6.5 45.9 %collective-permute-start = (bf16[272,1280]{1,0:T(8,128)(2,1)}, bf16[272,1280]{1,0:T(8,128)(2,1)}, u32[]{:S(2)}, u32[]{:S(2)}) collective-permute-start(bf16[272,1280]{1,0:T(8,128)(2,1)} %fusion.42), channel_id=1, source_target_pairs={{0,2},{1,3},{2,0},{3,1},{4,6},{5,7},{6,4},{7,5},{8,10},{9,11},{10,... | collective-permute-start | bytes 2088968 | tf_op jit(solution)/shard_map/ppermute | solution.py:195
  6.5 61.3 %collective-permute-start.3 = (bf16[256,1280]{1,0:T(8,128)(2,1)}, bf16[256,1280]{1,0:T(8,128)(2,1)}, u32[]{:S(2)}, u32[]{:S(2)}) collective-permute-start(bf16[256,1280]{1,0:T(8,128)(2,1)} %bitcast.43), channel_id=1, source_target_pairs={{0,2},{1,3},{2,0},{3,1},{4,6},{5,7},{6,4},{7,5},{8,10},{9,11},{10,... | collective-permute-start | bytes 1966088 | tf_op jit(solution)/shard_map/ppermute | solution.py:195
  49.1 4.4 %copy-start.1 = (bf16[1,256,1280]{2,1,0:T(8,128)(2,1)S(1)}, bf16[1,256,1280]{2,1,0:T(8,128)(2,1)}, u32[]{:S(2)}) copy-start(bf16[1,256,1280]{2,1,0:T(8,128)(2,1)} %param.8) | copy-start | bytes 1966084
  53.5 5.2 %copy-start.2 = (bf16[256,1280]{1,0:T(8,128)(2,1)}, bf16[256,1280]{1,0:T(8,128)(2,1)S(1)}, u32[]{:S(2)}) copy-start(bf16[256,1280]{1,0:T(8,128)(2,1)S(1)} %slice.118) | copy-start | bytes 1966084
  53.5 5.4 %copy-start.17 = (bf16[256]{0:T(256)(128)(2,1)S(1)}, bf16[256]{0:T(256)(128)(2,1)}, u32[]{:S(2)}) copy-start(bf16[256]{0:T(256)(128)(2,1)} %convert_reduce_fusion.1) | copy-start | bytes 1540
  53.5 5.4 %copy-start.13 = (f32[1280]{0:T(1024)S(1)}, f32[1280]{0:T(1024)}, u32[]{:S(2)}) copy-start(f32[1280]{0:T(1024)} %param.10) | copy-start | bytes 15364
  56.6 7.5 %copy-start.14 = (f32[1024]{0:T(1024)}, f32[1024]{0:T(1024)S(1)}, u32[]{:S(2)}) copy-start(f32[1024]{0:T(1024)S(1)} %add_rsqrt_fusion) | copy-start | bytes 12292
  59.0 5.2 %copy-start.3 = (bf16[4,2,2,80,960]{4,3,2,1,0:T(8,128)(2,1)S(1)}, bf16[4,2,2,80,960]{4,3,2,1,0:T(8,128)(2,1)}, u32[]{:S(2)}) copy-start(bf16[4,2,2,80,960]{4,3,2,1,0:T(8,128)(2,1)} %slice.98) | copy-start | bytes 7372804
  87.6 19.1 %collective-permute-start.4 = (bf16[2,320,512]{2,1,0:T(8,128)(2,1)S(1)}, bf16[2,320,512]{2,1,0:T(8,128)(2,1)}, u32[]{:S(2)}, u32[]{:S(2)}) collective-permute-start(bf16[2,320,512]{2,1,0:T(8,128)(2,1)S(1)} %get-tuple-element.23), channel_id=1, source_target_pairs={{0,1},{1,0},{2,3},{3,2},{4,5},{5,4},{6,7},{7,6},{8,9},{9,8},{10,11... | collective-permute-start | bytes 1966088 | tf_op jit(solution)/shard_map/ppermute | solution.py:195
  91.2 2.2 %collective-permute-start.9 = (bf16[320,320]{1,0:T(8,128)(2,1)S(1)}, bf16[320,320]{1,0:T(8,128)(2,1)S(1)}, u32[]{:S(2)}, u32[]{:S(2)}) collective-permute-start(bf16[320,320]{1,0:T(8,128)(2,1)S(1)} %get-tuple-element.33), channel_id=1, source_target_pairs={{0,1},{1,0},{2,3},{3,2},{4,5},{5,4},{6,7},{7,6},{8,9},{9,8},{10,11... | collective-permute-start | bytes 614408 | tf_op jit(solution)/shard_map/ppermute | solution.py:195
  91.4 7.9 %collective-permute-start.11 = (bf16[320,320]{1,0:T(8,128)(2,1)S(1)}, bf16[320,320]{1,0:T(8,128)(2,1)}, u32[]{:S(2)}, u32[]{:S(2)}) collective-permute-start(bf16[320,320]{1,0:T(8,128)(2,1)S(1)} %get-tuple-element.34), channel_id=1, source_target_pairs={{0,3},{1,2},{2,1},{3,0},{4,7},{5,6},{6,5},{7,4},{8,11},{9,10},{10,... | collective-permute-start | bytes 614408 | tf_op jit(solution)/shard_map/ppermute | solution.py:195
  91.9 13.2 %collective-permute-start.10 = (bf16[320,320]{1,0:T(8,128)(2,1)S(1)}, bf16[320,320]{1,0:T(8,128)(2,1)}, u32[]{:S(2)}, u32[]{:S(2)}) collective-permute-start(bf16[320,320]{1,0:T(8,128)(2,1)S(1)} %get-tuple-element.35), channel_id=1, source_target_pairs={{0,2},{1,3},{2,0},{3,1},{4,6},{5,7},{6,4},{7,5},{8,10},{9,11},{10,... | collective-permute-start | bytes 614408 | tf_op jit(solution)/shard_map/ppermute | solution.py:195
  106.7 5.3 %copy-start.4 = (bf16[4,2,2,80,960]{4,3,2,1,0:T(8,128)(2,1)S(1)}, bf16[4,2,2,80,960]{4,3,2,1,0:T(8,128)(2,1)}, u32[]{:S(2)}) copy-start(bf16[4,2,2,80,960]{4,3,2,1,0:T(8,128)(2,1)} %slice.98) | copy-start | bytes 7372804
  108.2 5.6 %copy-start.5 = (bf16[2,320,512]{2,1,0:T(8,128)(2,1)}, bf16[2,320,512]{2,1,0:T(8,128)(2,1)S(1)}, u32[]{:S(2)}) copy-start(bf16[2,320,512]{2,1,0:T(8,128)(2,1)S(1)} %add_convert_fusion.1) | copy-start | bytes 1966084
  108.7 7.2 %collective-permute-start.7 = (bf16[160,512]{1,0:T(8,128)(2,1)S(1)}, bf16[160,512]{1,0:T(8,128)(2,1)S(1)}, u32[]{:S(2)}, u32[]{:S(2)}) collective-permute-start(bf16[160,512]{1,0:T(8,128)(2,1)S(1)} %get-tuple-element.42), channel_id=1, source_target_pairs={{0,2},{1,3},{2,0},{3,1},{4,6},{5,7},{6,4},{7,5},{8,10},{9,11},{10,... | collective-permute-start | bytes 491528 | tf_op jit(solution)/shard_map/ppermute | solution.py:195
  109.2 7.9 %collective-permute-start.8 = (bf16[160,512]{1,0:T(8,128)(2,1)S(1)}, bf16[160,512]{1,0:T(8,128)(2,1)S(1)}, u32[]{:S(2)}, u32[]{:S(2)}) collective-permute-start(bf16[160,512]{1,0:T(8,128)(2,1)S(1)} %get-tuple-element.43), channel_id=1, source_target_pairs={{0,3},{1,2},{2,1},{3,0},{4,7},{5,6},{6,5},{7,4},{8,11},{9,10},{10,... | collective-permute-start | bytes 491528 | tf_op jit(solution)/shard_map/ppermute | solution.py:195
  110.8 6.4 %copy-start.8 = (bf16[1024,1280]{1,0:T(8,128)(2,1)S(1)}, bf16[1024,1280]{1,0:T(8,128)(2,1)}, u32[]{:S(2)}) copy-start(bf16[1024,1280]{1,0:T(8,128)(2,1)} %copy-done.7) | copy-start | bytes 7864324
  110.8 6.3 %collective-permute-start.6 = (bf16[320,512]{1,0:T(8,128)(2,1)S(1)}, bf16[320,512]{1,0:T(8,128)(2,1)S(1)}, u32[]{:S(2)}, u32[]{:S(2)}) collective-permute-start(bf16[320,512]{1,0:T(8,128)(2,1)S(1)} %get-tuple-element.41), channel_id=1, source_target_pairs={{0,1},{1,0},{2,3},{3,2},{4,5},{5,4},{6,7},{7,6},{8,9},{9,8},{10,11... | collective-permute-start | bytes 983048 | tf_op jit(solution)/shard_map/ppermute | solution.py:195
  113.8 40.0 %collective-permute-start.5 = (bf16[256,1280]{1,0:T(8,128)(2,1)}, bf16[256,1280]{1,0:T(8,128)(2,1)}, u32[]{:S(2)}, u32[]{:S(2)}) collective-permute-start(bf16[256,1280]{1,0:T(8,128)(2,1)} %convolution_convert_fusion.1), channel_id=1, source_target_pairs={{0,2},{1,3},{2,0},{3,1},{4,6},{5,7},{6,4},{7,5},{8,10},{9,11},{10,... | collective-permute-start | bytes 1966088 | tf_op jit(solution)/shard_map/ppermute | solution.py:195
  153.8 3.6 %copy-start.10 = (bf16[1,256,1280]{2,1,0:T(8,128)(2,1)S(1)}, bf16[1,256,1280]{2,1,0:T(8,128)(2,1)}, u32[]{:S(2)}) copy-start(bf16[1,256,1280]{2,1,0:T(8,128)(2,1)} %param.13) | copy-start | bytes 1966084
  153.8 3.6 %slice-start = ((f32[1024]{0:T(1024)}), f32[256]{0:T(256)S(1)}, s32[]{:S(2)}) async-start(f32[1024]{0:T(1024)} %copy-done.14), calls=%async_computation | async-start | bytes 2048 | tf_op jit(solution)/shard_map/slice | solution.py:626
  (7 other events, 12.7 us)

commit v3 on v2

--- a/solution.py
+++ b/solution.py
@@ -215,7 +215,9 @@
     for block in range(blocks):
         columns = slice(block * rows, (block + 1) * rows)
         query_t, grad_t = q_ref[:, columns], g_ref[:, columns]
-        scores = jnp.dot(key, query_t, preferred_element_type=jnp.float32) * score_scale
+        scores = jnp.dot(
+            key, (query_t * score_scale).astype(jnp.bfloat16), preferred_element_type=jnp.float32
+        )
         scores = scores + bias_ref[:, columns]
         exponent = jnp.exp(scores - jnp.max(scores, axis=0, keepdims=True))
         inverse = 1.0 / jnp.sum(exponent, axis=0, keepdims=True)
@@ -227,8 +229,10 @@
         row_delta = jnp.sum(
             grad_t.astype(jnp.float32) * attended.astype(jnp.float32), axis=0, keepdims=True
         )
-        grad_probs = jnp.dot(value, grad_t, preferred_element_type=jnp.float32)
-        grad_scores = (probabilities * ((grad_probs - row_delta) * score_scale)).astype(
+        grad_probs = jnp.dot(
+            value, (grad_t * score_scale).astype(jnp.bfloat16), preferred_element_type=jnp.float32
+        )
+        grad_scores = (probabilities * (grad_probs - row_delta * score_scale)).astype(
             jnp.bfloat16
         )
         dq_ref[:, columns] = jnp.dot(
@@ -525,10 +529,15 @@
     part = inner // 2
     score_scale = 1.0 / math.sqrt(HEAD_DIM)
 
-    mine_qkv = lax.dynamic_index_in_dim(w_qkv.reshape(shard, 3, 2, part), high, 2, keepdims=False)
-    mine_qkv = lax.dynamic_slice_in_dim(
-        mine_qkv.reshape(shard, 3 * part), low * (shard // 2), shard // 2, 0
-    )
+    own_rows = lax.dynamic_slice_in_dim(w_qkv, low * (shard // 2), shard // 2, 0)
+    choices = [
+        jnp.concatenate(
+            [own_rows[:, (2 * i + half) * part : (2 * i + half + 1) * part] for i in range(3)],
+            axis=1,
+        )
+        for half in (0, 1)
+    ]
+    mine_qkv = jnp.where(high == 0, choices[0], choices[1])
     mine_out = lax.dynamic_slice_in_dim(w_out, low * (width // 2), width // 2, 1)
     packed_weights = jnp.concatenate([mine_out, mine_qkv], axis=1)
 
@@ -572,20 +581,11 @@
         query_t, grad_t, pairs_t[:part], pairs_t[part:],
         key_pos[:, None], key_live[:, None], query_rows, 2, score_scale,
     )
-    own_grads = own_grads + swap(other_grads, 1).astype(jnp.float32)
-
     block = width // n_seq
+    other_grads = swap(other_grads, 1)
     partial_out = jnp.dot(att_t, cots, preferred_element_type=jnp.float32)
-
-    def columns_of(flip):
-        return lax.dynamic_slice_in_dim(partial_out, (me ^ flip) * block, block, 1)
-
-    arrived = [swap(columns_of(flip).astype(jnp.bfloat16), flip) for flip in (1, 2, 3)]
-    arrived = [value.astype(jnp.float32) for value in arrived]
-    same, across = columns_of(0) + arrived[0], arrived[1] + arrived[2]
-    sum_out = jnp.concatenate(
-        [jnp.where(high == 0, same, across), jnp.where(high == 0, across, same)], axis=0
-    )
+    other_grads, partial_out = lax.optimization_barrier((other_grads, partial_out))
+    own_grads = own_grads + other_grads.astype(jnp.float32)
 
     grads_t = jnp.concatenate(
         [dq_t, own_grads.reshape(2 * part, queries).astype(jnp.bfloat16)], axis=0
@@ -598,6 +598,11 @@
     beside = swap(units(2 * (high + 1 - low), 2), 1)
     facing = swap(units(4 * (1 - high) + low, 1), 2)
     corner = swap(units(4 * (1 - high) + 1 - low, 1), 3)
+
+    def columns_of(flip):
+        return lax.dynamic_slice_in_dim(partial_out, (me ^ flip) * block, block, 1)
+
+    columns = [swap(columns_of(flip).astype(jnp.bfloat16), flip) for flip in (1, 2, 3)]
     two = jnp.concatenate([units(2 * (high + low), 2), beside], axis=1)
     one = jnp.concatenate(
         [facing[:, length:], facing[:, :length], corner[:, length:], corner[:, :length]], axis=1
@@ -606,8 +611,15 @@
     keep_t = jnp.where(
         first, jnp.concatenate([two, one], axis=0), jnp.concatenate([one, two], axis=0)
     )
+    keep_t, late_t = lax.optimization_barrier((keep_t, grads_t))
     sum_qkv = lax.dot_general(
         normed, keep_t, (((0,), (1,)), ((), ())), preferred_element_type=jnp.float32
+    )
+
+    columns = [value.astype(jnp.float32) for value in columns]
+    same, across = columns_of(0) + columns[0], columns[1] + columns[2]
+    sum_out = jnp.concatenate(
+        [jnp.where(high == 0, same, across), jnp.where(high == 0, across, same)], axis=0
     )
 
     def through_weights(piece):
@@ -615,12 +627,14 @@
             piece, part_qkv, (((0,), (1,)), ((), ())), preferred_element_type=jnp.float32
         )
 
-    arrived = swap(through_weights(grads_t[:, length:]).astype(jnp.bfloat16), 2)
+    sent = through_weights(late_t[:, length:]).astype(jnp.bfloat16)
+    sent, sum_qkv = lax.optimization_barrier((sent, sum_qkv.astype(jnp.bfloat16)))
+    arrived = swap(sent, 2)
     factor = 1.0 / math.sqrt(n_data * n_seq * length)
     tile_qkv, tile_out = sum_tiles(
-        [sum_qkv.astype(jnp.bfloat16), sum_out.astype(jnp.bfloat16)], n_data // 2, 5, factor
-    )
-    grad_unit = through_weights(grads_t[:, :length]) + arrived.astype(jnp.float32)
+        [sum_qkv, sum_out.astype(jnp.bfloat16)], n_data // 2, 5, factor
+    )
+    grad_unit = through_weights(late_t[:, :length]) + arrived.astype(jnp.float32)
     grad_unit = grad_unit * norm_gain
     own_unit = unit_rows[:length]
     through = inverse[:length] * (

time: 163 us -> 172 us (1.055)
  waiting for transfers between devices: 14.5 us -> 30.8 us
  matrix products: 21.1 us -> 14.7 us
  local copies, waits for them, and re-layouts: 19.1 us -> 14.3 us
  other arithmetic: 19.3 us -> 23.3 us
    ppermute x12, waiting for transfers between devices: 14.5 us -> 30.8 us  [swap(): lax.ppermute(value, 'seq', [(source, source ^ flip) for source in range(c...]
    select_n x0 -> x2, other arithmetic: none -> 7.32 us  [the longest x1 7.2 us: head_body(): jnp.where(first, jnp.concatenate([two, one], axis=0), jnp.concatenate([on...]
    dot_general x1, matrix products: 9.07 us -> 2.6 us  [head_body(): lax.dot_general(normed, keep_t, (((0,), (1,)), ((), ())), preferred_eleme...]
    reshape x2 -> x0, local copies, waits for them, and re-layouts: 2.63 us -> none  [the longest x1 2.3 us: head_body(): w_qkv.reshape(shard, 3, 2, part)]
    dynamic_slice x2 -> x0, local copies, waits for them, and re-layouts: 2.54 us -> none  [the longest x1 2.52 us: head_body(): lax.dynamic_index_in_dim(w_qkv.reshape(shard, 3, 2, part), high, 2, keepd...]
  transfers between devices with their start and end apart: 12 -> 12, of which waited for: 4 -> 5; matrix products, arithmetic and copies ran while one was open for 27% -> 17% of each run, Pallas kernels for 36% -> 34%
where the time goes in v3:
time: 172 us; the launch traced here: 170 us
  Pallas kernels  75.5 us (44%)
  waiting for transfers between devices  30.8 us (18%)
  other arithmetic  23.3 us (14%)
  matrix products  14.7 us (9%)
  local copies, waits for them, and re-layouts  14.3 us (8%)
  starting transfers between devices  10.6 us (6%)
    pallas_call x1, Pallas kernels, gather_pieces(): pl.pallas_call(gather_kernel, out_shape=jax.ShapeDtypeStruct((count, 2, 2...  31.9 us
    ppermute x12, waiting for transfers between devices, swap(): lax.ppermute(value, 'seq', [(source, source ^ flip) for source in range(c...  30.8 us
    pallas_call x1, Pallas kernels, sum_tiles(): pl.pallas_call(functools.partial(sum_kernel, chunks, factor), out_shape=[...  25.3 us
    pallas_call x1, Pallas kernels, attend(): pl.pallas_call(functools.partial(attend_kernel, score_scale, blocks), gri...  18.3 us
    ppermute x12, starting transfers between devices, swap(): lax.ppermute(value, 'seq', [(source, source ^ flip) for source in range(c...  10.6 us
    select_n x1, other arithmetic, head_body(): jnp.where(first, jnp.concatenate([two, one], axis=0), jnp.concatenate([on...  7.2 us
    convert_element_type x1, other arithmetic, head_body(): normed = (unit_rows * norm_gain).astype(jnp.bfloat16)  5.2 us
    dot_general x2, matrix products, through_weights(): lax.dot_general(piece, part_qkv, (((0,), (1,)), ((), ())), preferred_elem...  5.2 us
  transfers between devices with their start and end apart: 12, of which 5 were waited for; matrix products, arithmetic and copies ran while one was open for 17% of the time, Pallas kernels for 34%

profile of v3, /device:TPU:0, one launch (start us, length us, event | category | flops | bytes accessed | tf_op | source)
XLA Modules:
  0.0 170.2 jit_solution(14274360292393853680)
XLA Ops:
  2.5 2.5 %collective-permute-start.2 = (bf16[272,1280]{1,0:T(8,128)(2,1)S(1)}, bf16[272,1280]{1,0:T(8,128)(2,1)}, u32[]{:S(2)}, u32[]{:S(2)}) collective-permute-start(bf16[272,1280]{1,0:T(8,128)(2,1)S(1)} %fusion.20), channel_id=1, source_target_pairs={{0,3},{1,2},{2,1},{3,0},{4,7},{5,6},{6,5},{7,4},{8,11},{9,10},{10,... | collective-permute-start | bytes 2088968 | tf_op jit(solution)/shard_map/ppermute | solution.py:195
  5.7 2.0 %collective-permute-start.3 = (bf16[256,1280]{1,0:T(8,128)(2,1)}, bf16[256,1280]{1,0:T(8,128)(2,1)}, u32[]{:S(2)}, u32[]{:S(2)}) collective-permute-start(bf16[256,1280]{1,0:T(8,128)(2,1)} %bitcast.43), channel_id=1, source_target_pairs={{0,2},{1,3},{2,0},{3,1},{4,6},{5,7},{6,4},{7,5},{8,10},{9,11},{10,... | collective-permute-start | bytes 1966088 | tf_op jit(solution)/shard_map/ppermute | solution.py:195
  9.0 31.9 %shard_map.85 = bf16[4,2,2,80,1600]{4,3,2,1,0:T(8,128)(2,1)S(1)} custom-call(bf16[80,1600]{1,0:T(8,128)(2,1)S(1)} %pad_maximum_fusion.6.piece_ref), custom_call_target="tpu_custom_call" | custom-call | bytes 32768000 | tf_op jit(solution)/shard_map/pallas_call | solution.py:413
  41.1 1.9 %slice.122 = bf16[4,2,2,80,960]{4,3,2,1,0:T(8,128)(2,1)} slice(bf16[4,2,2,80,1600]{4,3,2,1,0:T(8,128)(2,1)S(1)} %shard_map.85), slice={[0:4], [0:2], [0:2], [0:80], [640:1600]} | slice | bytes 4915200 | tf_op jit(solution)/shard_map/slice | solution.py:563
  46.6 1.4 slice.142
  48.5 2.6 %fusion.2 = f32[1024]{0:T(1024)S(1)} fusion(f32[1024]{0:T(1024)S(1)} %broadcast_multiply_fusion, bf16[256,1280]{1,0:T(8,128)(2,1)S(1)} %slice.144, bf16[256,1280]{1,0:T(8,128)(2,1)S(1)} %slice.143, bf16[256,1280]{1,0:T(8,128)(2,1)S(1)} %slice.142, bf16[256,1280]{1,0:T(8,128)(2,1)S(1)} %bitcast.33), kind=kLoop, calls=%fused_computation.4 | loop fusion | flops 14416896 | bytes 2629632 | tf_op jit(solution)/shard_map/reduce_sum | solution.py:28
  53.4 5.2 %multiply_convert_fusion = (bf16[1024,1280]{1,0:T(8,128)(2,1)S(1)}, f32[1024,1280]{1,0:T(8,128)}) fusion(f32[1280]{0:T(1024)S(1)} %copy-done.13, f32[1024]{0:T(1024)S(1)} %add_rsqrt_fusion, f32[1024]{0:T(1024)S(1)} %broadcast_multiply_fusion, bf16[256,1280]{1,0:T(8,128)(2,1)S(1)} %slice.144, bf16[256,1280]{1,0:T(8,128)(2,1)} %copy-done.2, ...), kind=kLoop, calls=%fused_computation.5 | loop fusion | flops 15728640 | bytes 10499072 | tf_op jit(solution)/shard_map/convert_element_type | solution.py:560
  58.6 2.5 %fusion.5 = bf16[640,1024]{1,0:T(8,128)(2,1)S(1)} fusion(bf16[1024,1280]{1,0:T(8,128)(2,1)S(1)} %get-tuple-element.41, bf16[1280,960]{1,0:T(8,128)(2,1)S(1)} %bitcast.36), kind=kOutput, calls=%fused_computation.16 | convolution fusion | flops 1678376960 | bytes 5570560 | tf_op jit(solution)/shard_map/dot_general | solution.py:571
  62.6 1.7 %fusion.14.g_ref = bf16[320,512]{1,0:T(8,128)(2,1)S(1)} fusion(bf16[256,1280]{1,0:T(8,128)(2,1)} %collective-permute-done.3, bf16[256,1280]{1,0:T(8,128)(2,1)S(1)} %bitcast.45, bf16[320,640]{1,0:T(8,128)(2,1)S(1)} %bitcast.47, bf16[320,640]{1,0:T(8,128)(2,1)S(1)} %bitcast.46, f32[512]{0:T(512)S(1)} %maximum_convert_fusion.1), kind=kOutput, calls=%fused_computation.28 | convolution fusion | flops 424017920 | bytes 2459648 | tf_op jit(solution)/shard_map/dot_general | solution.py:33
  64.4 18.3 %shard_map.86 = (bf16[320,512]{1,0:T(8,128)(2,1)S(1)}, bf16[320,512]{1,0:T(8,128)(2,1)S(1)}, f32[2,320,512]{2,1,0:T(8,128)S(1)}, bf16[2,320,512]{2,1,0:T(8,128)(2,1)}) custom-call(bf16[320,512]{1,0:T(8,128)(2,1)S(1)} %fusion.11.q_ref, bf16[320,512]{1,0:T(8,128)(2,1)S(1)} %fusion.14.g_ref, bf16[320,1024]{1,0:T(8,128)(2,1)S(1)} %get-tuple-element.51.k_ref, ...), custom_call_target="tpu_custom_call" | custom-call | flops 1677721600 | bytes 3932160 | tf_op jit(solution)/shard_map/pallas_call | solution.py:259
  83.0 1.9 %fusion.16 = f32[320,1280]{1,0:T(8,128)S(1)} fusion(bf16[320,512]{1,0:T(8,128)(2,1)S(1)} %get-tuple-element.30, bf16[256,1280]{1,0:T(8,128)(2,1)} %collective-permute-done.3, bf16[256,1280]{1,0:T(8,128)(2,1)} %bitcast.44), kind=kOutput, calls=%fused_computation.35 | convolution fusion | flops 422051840 | bytes 3276800 | tf_op jit(solution)/shard_map/dot_general | solution.py:586
  89.1 3.7 %collective-permute-done.6 = bf16[160,512]{1,0:T(8,128)(2,1)S(1)} collective-permute-done((bf16[160,512]{1,0:T(8,128)(2,1)S(1)}, bf16[160,512]{1,0:T(8,128)(2,1)S(1)}, u32[]{:S(2)}, u32[]{:S(2)}) %collective-permute-start.6) | collective-permute-done | bytes 163872 | tf_op jit(solution)/shard_map/ppermute | solution.py:195
  92.8 2.4 %collective-permute-done.7 = bf16[160,512]{1,0:T(8,128)(2,1)S(1)} collective-permute-done((bf16[160,512]{1,0:T(8,128)(2,1)S(1)}, bf16[160,512]{1,0:T(8,128)(2,1)S(1)}, u32[]{:S(2)}, u32[]{:S(2)}) %collective-permute-start.7) | collective-permute-done | bytes 163872 | tf_op jit(solution)/shard_map/ppermute | solution.py:195
  95.2 7.2 %maximum_select_fusion = bf16[480,1024]{1,0:T(8,128)(2,1)S(1)} fusion(bf16[160,256]{1,0:T(8,128)(2,1)S(1)} %get-tuple-element.67, bf16[160,256]{1,0:T(8,128)(2,1)S(1)} %get-tuple-element.66, bf16[160,256]{1,0:T(8,128)(2,1)S(1)} %get-tuple-element.65, bf16[160,256]{1,0:T(8,128)(2,1)S(1)} %get-tuple-element.64, ...), kind=kLoop, calls=%fused_computation.34 | loop fusion | flops 12288000 | bytes 1966081 | tf_op jit(solution)/shard_map/jit(_where)/select_n | solution.py:611
  102.4 2.6 %convolution_convert_fusion = bf16[1280,480]{0,1:T(8,128)(2,1)} fusion(bf16[480,1024]{1,0:T(8,128)(2,1)S(1)} %maximum_select_fusion, bf16[1024,1280]{1,0:T(8,128)(2,1)S(1)} %copy-done.8), kind=kOutput, calls=%fused_computation.6 | convolution fusion | flops 1258905600 | bytes 4833280 | tf_op jit(solution)/shard_map/dot_general | solution.py:615
  105.0 1.7 %convolution_convert_fusion.1 = bf16[256,1280]{1,0:T(8,128)(2,1)} fusion(bf16[1280,960]{1,0:T(8,128)(2,1)S(1)} %bitcast.38, bf16[960,512]{1,0:T(8,128)(2,1)S(1)} %pad_maximum_fusion.1), kind=kOutput, calls=%fused_computation.8 | convolution fusion | flops 629473280 | bytes 3768320 | tf_op jit(solution)/shard_map/dot_general | solution.py:626
  107.7 1.6 collective-permute-start.11
  109.8 18.9 %collective-permute-done.11 = bf16[320,320]{1,0:T(8,128)(2,1)S(1)} collective-permute-done((bf16[320,320]{1,0:T(8,128)(2,1)S(1)}, bf16[320,320]{1,0:T(8,128)(2,1)S(1)}, u32[]{:S(2)}, u32[]{:S(2)}) %collective-permute-start.11) | collective-permute-done | bytes 204832 | tf_op jit(solution)/shard_map/ppermute | solution.py:195
  128.7 5.8 %collective-permute-done.10 = bf16[320,320]{1,0:T(8,128)(2,1)S(1)} collective-permute-done((bf16[320,320]{1,0:T(8,128)(2,1)S(1)}, bf16[320,320]{1,0:T(8,128)(2,1)S(1)}, u32[]{:S(2)}, u32[]{:S(2)}) %collective-permute-start.10) | collective-permute-done | bytes 204832 | tf_op jit(solution)/shard_map/ppermute | solution.py:195
  134.5 1.3 select_convert_fusion.1
  135.9 1.6 copy.21
  137.5 25.3 %shard_map.87 = (f32[160,480]{1,0:T(8,128)S(1)}, f32[80,320]{1,0:T(8,128)S(1)}) custom-call(bf16[4,2,160,480]{3,2,1,0:T(8,128)(2,1)S(1)} %bitcast.29, bf16[4,2,80,320]{3,2,1,0:T(8,128)(2,1)S(1)} %bitcast.30), custom_call_target="tpu_custom_call" | custom-call | bytes 39321600 | tf_op jit(solution)/shard_map/pallas_call | solution.py:503
  162.8 3.5 %fusion.33 = (f32[256]{0:T(256)S(1)}, f32[256]{0:T(256)S(1)}, f32[256,1280]{1,0:T(8,128)S(1)}) fusion(f32[1024,1280]{1,0:T(8,128)} %get-tuple-element.42, f32[1280]{0:T(1024)S(1)} %copy-done.13, bf16[256,1280]{1,0:T(8,128)(2,1)} %collective-permute-done.8, bf16[1280,960]{1,0:T(8,128)(2,1)} %bitcast.35, bf16[960,512]{1,0:T(8,128)(2,1)S(1)} %pad_maximum_fusion.1), kind=kOutput, calls=%fused_computation.83 | convolution fusion | flops 631111168 | bytes 6236160 | tf_op jit(solution)/shard_map/dot_general | solution.py:626
  166.3 2.5 %fusion.21 = bf16[1,256,1280]{2,1,0:T(8,128)(2,1)} fusion(f32[1024,1280]{1,0:T(8,128)} %get-tuple-element.42, f32[256,1280]{1,0:T(8,128)S(1)} %get-tuple-element.70, f32[256]{0:T(256)S(1)} %broadcast_multiply_fusion.1, f32[256]{0:T(256)S(1)} %broadcast_multiply_fusion.2, f32[256]{0:T(256)S(1)} %slice-done, bf16[1,256,1280]{2,1,0:T(8,128)(2,1)S(1)} %copy-done.10), kind=kLoop, calls=%fused_computation.40 | loop fusion | flops 2293760 | bytes 3935232 | tf_op jit(solution)/shard_map/broadcast_in_dim | solution.py:645
  (91 shorter events, 19.4 us)
Async XLA Ops:
  0.6 7.1 %copy-start = (bf16[80,1280]{1,0:T(8,128)(2,1)S(1)}, bf16[80,1280]{1,0:T(8,128)(2,1)}, u32[]{:S(2)}) copy-start(bf16[80,1280]{1,0:T(8,128)(2,1)} %param.12) | copy-start | bytes 614404
  2.5 41.7 %collective-permute-start.2 = (bf16[272,1280]{1,0:T(8,128)(2,1)S(1)}, bf16[272,1280]{1,0:T(8,128)(2,1)}, u32[]{:S(2)}, u32[]{:S(2)}) collective-permute-start(bf16[272,1280]{1,0:T(8,128)(2,1)S(1)} %fusion.20), channel_id=1, source_target_pairs={{0,3},{1,2},{2,1},{3,0},{4,7},{5,6},{6,5},{7,4},{8,11},{9,10},{10,... | collective-permute-start | bytes 2088968 | tf_op jit(solution)/shard_map/ppermute | solution.py:195
  5.0 40.4 %collective-permute-start.1 = (bf16[272,1280]{1,0:T(8,128)(2,1)S(1)}, bf16[272,1280]{1,0:T(8,128)(2,1)}, u32[]{:S(2)}, u32[]{:S(2)}) collective-permute-start(bf16[272,1280]{1,0:T(8,128)(2,1)S(1)} %fusion.20), channel_id=1, source_target_pairs={{0,1},{1,0},{2,3},{3,2},{4,5},{5,4},{6,7},{7,6},{8,9},{9,8},{10,11... | collective-permute-start | bytes 2088968 | tf_op jit(solution)/shard_map/ppermute | solution.py:195
  5.7 40.9 %collective-permute-start = (bf16[272,1280]{1,0:T(8,128)(2,1)S(1)}, bf16[272,1280]{1,0:T(8,128)(2,1)}, u32[]{:S(2)}, u32[]{:S(2)}) collective-permute-start(bf16[272,1280]{1,0:T(8,128)(2,1)S(1)} %fusion.20), channel_id=1, source_target_pairs={{0,2},{1,3},{2,0},{3,1},{4,6},{5,7},{6,4},{7,5},{8,10},{9,11},{10,... | collective-permute-start | bytes 2088968 | tf_op jit(solution)/shard_map/ppermute | solution.py:195
  5.7 56.5 %collective-permute-start.3 = (bf16[256,1280]{1,0:T(8,128)(2,1)}, bf16[256,1280]{1,0:T(8,128)(2,1)}, u32[]{:S(2)}, u32[]{:S(2)}) collective-permute-start(bf16[256,1280]{1,0:T(8,128)(2,1)} %bitcast.43), channel_id=1, source_target_pairs={{0,2},{1,3},{2,0},{3,1},{4,6},{5,7},{6,4},{7,5},{8,10},{9,11},{10,... | collective-permute-start | bytes 1966088 | tf_op jit(solution)/shard_map/ppermute | solution.py:195
  44.2 3.7 %copy-start.1 = (bf16[1,256,1280]{2,1,0:T(8,128)(2,1)S(1)}, bf16[1,256,1280]{2,1,0:T(8,128)(2,1)}, u32[]{:S(2)}) copy-start(bf16[1,256,1280]{2,1,0:T(8,128)(2,1)} %param.8) | copy-start | bytes 1966084
  48.0 3.1 %copy-start.3 = (bf16[256,1280]{1,0:T(8,128)(2,1)}, bf16[256,1280]{1,0:T(8,128)(2,1)S(1)}, u32[]{:S(2)}) copy-start(bf16[256,1280]{1,0:T(8,128)(2,1)S(1)} %slice.142) | copy-start | bytes 1966084
  48.5 4.9 %copy-start.13 = (f32[1280]{0:T(1024)S(1)}, f32[1280]{0:T(1024)}, u32[]{:S(2)}) copy-start(f32[1280]{0:T(1024)} %param.10) | copy-start | bytes 15364
  51.1 58.7 %copy-start.14 = (f32[1024]{0:T(1024)}, f32[1024]{0:T(1024)S(1)}, u32[]{:S(2)}) copy-start(f32[1024]{0:T(1024)S(1)} %add_rsqrt_fusion) | copy-start | bytes 12292
  53.4 5.2 %copy-start.4 = (bf16[4,2,2,80,960]{4,3,2,1,0:T(8,128)(2,1)S(1)}, bf16[4,2,2,80,960]{4,3,2,1,0:T(8,128)(2,1)}, u32[]{:S(2)}) copy-start(bf16[4,2,2,80,960]{4,3,2,1,0:T(8,128)(2,1)} %slice.122) | copy-start | bytes 7372804
  58.6 2.7 %copy-start.7 = (bf16[1024,1280]{1,0:T(8,128)(2,1)}, bf16[1024,1280]{1,0:T(8,128)(2,1)S(1)}, u32[]{:S(2)}) copy-start(bf16[1024,1280]{1,0:T(8,128)(2,1)S(1)} %get-tuple-element.41) | copy-start | bytes 7864324
  82.7 2.3 %collective-permute-start.4 = (bf16[2,320,512]{2,1,0:T(8,128)(2,1)}, bf16[2,320,512]{2,1,0:T(8,128)(2,1)S(1)}, u32[]{:S(2)}, u32[]{:S(2)}) collective-permute-start(bf16[2,320,512]{2,1,0:T(8,128)(2,1)} %get-tuple-element.29), channel_id=1, source_target_pairs={{0,1},{1,0},{2,3},{3,2},{4,5},{5,4},{6,7},{7,6},{8,9},{9,8},{10,11... | collective-permute-start | bytes 1966088 | tf_op jit(solution)/shard_map/ppermute | solution.py:195
  84.9 22.4 %copy-start.6 = (f32[320,1280]{1,0:T(8,128)}, f32[320,1280]{1,0:T(8,128)S(1)}, u32[]{:S(2)}) copy-start(f32[320,1280]{1,0:T(8,128)S(1)} %fusion.16) | copy-start | bytes 4915204
  85.7 7.1 %collective-permute-start.6 = (bf16[160,512]{1,0:T(8,128)(2,1)S(1)}, bf16[160,512]{1,0:T(8,128)(2,1)S(1)}, u32[]{:S(2)}, u32[]{:S(2)}) collective-permute-start(bf16[160,512]{1,0:T(8,128)(2,1)S(1)} %get-tuple-element.54), channel_id=1, source_target_pairs={{0,2},{1,3},{2,0},{3,1},{4,6},{5,7},{6,4},{7,5},{8,10},{9,11},{10,... | collective-permute-start | bytes 491528 | tf_op jit(solution)/shard_map/ppermute | solution.py:195
  86.3 8.9 %collective-permute-start.7 = (bf16[160,512]{1,0:T(8,128)(2,1)S(1)}, bf16[160,512]{1,0:T(8,128)(2,1)S(1)}, u32[]{:S(2)}, u32[]{:S(2)}) collective-permute-start(bf16[160,512]{1,0:T(8,128)(2,1)S(1)} %get-tuple-element.55), channel_id=1, source_target_pairs={{0,3},{1,2},{2,1},{3,0},{4,7},{5,6},{6,5},{7,4},{8,11},{9,10},{10,... | collective-permute-start | bytes 491528 | tf_op jit(solution)/shard_map/ppermute | solution.py:195
  88.5 13.9 %copy-start.8 = (bf16[1024,1280]{1,0:T(8,128)(2,1)S(1)}, bf16[1024,1280]{1,0:T(8,128)(2,1)}, u32[]{:S(2)}) copy-start(bf16[1024,1280]{1,0:T(8,128)(2,1)} %copy-done.7) | copy-start | bytes 7864324
  88.5 6.6 %collective-permute-start.5 = (bf16[320,512]{1,0:T(8,128)(2,1)S(1)}, bf16[320,512]{1,0:T(8,128)(2,1)S(1)}, u32[]{:S(2)}, u32[]{:S(2)}) collective-permute-start(bf16[320,512]{1,0:T(8,128)(2,1)S(1)} %get-tuple-element.53), channel_id=1, source_target_pairs={{0,1},{1,0},{2,3},{3,2},{4,5},{5,4},{6,7},{7,6},{8,9},{9,8},{10,11... | collective-permute-start | bytes 983048 | tf_op jit(solution)/shard_map/ppermute | solution.py:195
  102.4 2.6 %copy-start.5 = (bf16[4,2,2,80,960]{4,3,2,1,0:T(8,128)(2,1)S(1)}, bf16[4,2,2,80,960]{4,3,2,1,0:T(8,128)(2,1)}, u32[]{:S(2)}) copy-start(bf16[4,2,2,80,960]{4,3,2,1,0:T(8,128)(2,1)} %slice.122) | copy-start | bytes 7372804
  106.7 56.1 %collective-permute-start.8 = (bf16[256,1280]{1,0:T(8,128)(2,1)}, bf16[256,1280]{1,0:T(8,128)(2,1)}, u32[]{:S(2)}, u32[]{:S(2)}) collective-permute-start(bf16[256,1280]{1,0:T(8,128)(2,1)} %convolution_convert_fusion.1), channel_id=1, source_target_pairs={{0,2},{1,3},{2,0},{3,1},{4,6},{5,7},{6,4},{7,5},{8,10},{9,11},{10,... | collective-permute-start | bytes 1966088 | tf_op jit(solution)/shard_map/ppermute | solution.py:195
  107.6 2.2 %collective-permute-start.9 = (bf16[320,320]{1,0:T(8,128)(2,1)S(1)}, bf16[320,320]{1,0:T(8,128)(2,1)S(1)}, u32[]{:S(2)}, u32[]{:S(2)}) collective-permute-start(bf16[320,320]{1,0:T(8,128)(2,1)S(1)} %get-tuple-element.45), channel_id=1, source_target_pairs={{0,1},{1,0},{2,3},{3,2},{4,5},{5,4},{6,7},{7,6},{8,9},{9,8},{10,11... | collective-permute-start | bytes 614408 | tf_op jit(solution)/shard_map/ppermute | solution.py:195
  107.7 20.9 %collective-permute-start.11 = (bf16[320,320]{1,0:T(8,128)(2,1)S(1)}, bf16[320,320]{1,0:T(8,128)(2,1)S(1)}, u32[]{:S(2)}, u32[]{:S(2)}) collective-permute-start(bf16[320,320]{1,0:T(8,128)(2,1)S(1)} %get-tuple-element.46), channel_id=1, source_target_pairs={{0,3},{1,2},{2,1},{3,0},{4,7},{5,6},{6,5},{7,4},{8,11},{9,10},{10,... | collective-permute-start | bytes 614408 | tf_op jit(solution)/shard_map/ppermute | solution.py:195
  109.3 25.2 %collective-permute-start.10 = (bf16[320,320]{1,0:T(8,128)(2,1)S(1)}, bf16[320,320]{1,0:T(8,128)(2,1)S(1)}, u32[]{:S(2)}, u32[]{:S(2)}) collective-permute-start(bf16[320,320]{1,0:T(8,128)(2,1)S(1)} %get-tuple-element.47), channel_id=1, source_target_pairs={{0,2},{1,3},{2,0},{3,1},{4,6},{5,7},{6,4},{7,5},{8,10},{9,11},{10,... | collective-permute-start | bytes 614408 | tf_op jit(solution)/shard_map/ppermute | solution.py:195
  162.8 3.5 %copy-start.10 = (bf16[1,256,1280]{2,1,0:T(8,128)(2,1)S(1)}, bf16[1,256,1280]{2,1,0:T(8,128)(2,1)}, u32[]{:S(2)}) copy-start(bf16[1,256,1280]{2,1,0:T(8,128)(2,1)} %param.13) | copy-start | bytes 1966084
  162.8 3.5 %slice-start = ((f32[1024]{0:T(1024)}), f32[256]{0:T(256)S(1)}, s32[]{:S(2)}) async-start(f32[1024]{0:T(1024)} %copy-done.14), calls=%async_computation | async-start | bytes 2048 | tf_op jit(solution)/shard_map/slice | solution.py:640
  (5 other events, 7.7 us)

commit v4 on v3

--- a/solution.py
+++ b/solution.py
@@ -518,6 +518,36 @@
     )(*tiles)
 
 
+def assemble_kernel(two_ref, beside_ref, facing_ref, corner_ref, out_ref):
+    low = lax.axis_index("seq") % 2
+    queries = two_ref.shape[1]
+    length, unit = queries // 2, facing_ref.shape[0]
+
+    def place(two_row, one_row):
+        out_ref[two_row : two_row + 2 * unit, :queries] = two_ref[...]
+        out_ref[two_row : two_row + 2 * unit, queries:] = beside_ref[...]
+        rows = slice(one_row, one_row + unit)
+        for start, piece in ((0, facing_ref), (queries, corner_ref)):
+            out_ref[rows, start : start + length] = piece[:, length:]
+            out_ref[rows, start + length : start + queries] = piece[:, :length]
+
+    pl.when(low == 0)(lambda: place(0, 2 * unit))
+    pl.when(low == 1)(lambda: place(unit, 0))
+
+
+def assemble(two, beside, facing, corner):
+    vmem = pl.BlockSpec(memory_space=pltpu.VMEM)
+    rows, queries = two.shape
+    return pl.pallas_call(
+        assemble_kernel,
+        out_shape=jax.ShapeDtypeStruct((rows + facing.shape[0], 2 * queries), two.dtype),
+        in_specs=[vmem] * 4,
+        out_specs=vmem,
+        compiler_params=pltpu.CompilerParams(vmem_limit_bytes=16 * 2**20),
+        cost_estimate=pl.CostEstimate(flops=0, bytes_accessed=8 * two.size, transcendentals=0),
+    )(two, beside, facing, corner)
+
+
 def head_body(frames, live, norm_gain, w_qkv, w_out, cotangent):
     length, width = frames.shape[1:]
     n_data = lax.axis_size("dp")
@@ -603,15 +633,8 @@
         return lax.dynamic_slice_in_dim(partial_out, (me ^ flip) * block, block, 1)
 
     columns = [swap(columns_of(flip).astype(jnp.bfloat16), flip) for flip in (1, 2, 3)]
-    two = jnp.concatenate([units(2 * (high + low), 2), beside], axis=1)
-    one = jnp.concatenate(
-        [facing[:, length:], facing[:, :length], corner[:, length:], corner[:, :length]], axis=1
-    )
-    first = low == 0
-    keep_t = jnp.where(
-        first, jnp.concatenate([two, one], axis=0), jnp.concatenate([one, two], axis=0)
-    )
-    keep_t, late_t = lax.optimization_barrier((keep_t, grads_t))
+    keep_t = assemble(units(2 * (high + low), 2), beside, facing, corner)
+    keep_t, late_t, columns = lax.optimization_barrier((keep_t, grads_t, columns))
     sum_qkv = lax.dot_general(
         normed, keep_t, (((0,), (1,)), ((), ())), preferred_element_type=jnp.float32
     )

time: 172 us -> 151 us (0.88)
  waiting for transfers between devices: 30.8 us -> 15.9 us
  other arithmetic: 23.3 us -> 16.4 us
  local copies, waits for them, and re-layouts: 14.3 us -> 17.9 us
    ppermute x12, waiting for transfers between devices: 30.8 us -> 15.9 us  [swap(): lax.ppermute(value, 'seq', [(source, source ^ flip) for source in range(c...]
    select_n x1 -> x0, other arithmetic: 7.2 us -> none  [head_body(): jnp.where(first, jnp.concatenate([two, one], axis=0), jnp.concatenate([on...]
  transfers between devices with their start and end apart: 12 -> 12, of which waited for: 5 -> 2; matrix products, arithmetic and copies ran while one was open for 17% -> 21% of each run, Pallas kernels for 34% -> 38%
where the time goes in v4:
time: 151 us; the launch traced here: 150 us
  Pallas kernels  75.6 us (50%)
  local copies, waits for them, and re-layouts  17.9 us (12%)
  other arithmetic  16.4 us (11%)
  waiting for transfers between devices  15.9 us (11%)
  matrix products  13.8 us (9%)
  starting transfers between devices  9.43 us (6%)
    pallas_call x1, Pallas kernels, gather_pieces(): pl.pallas_call(gather_kernel, out_shape=jax.ShapeDtypeStruct((count, 2, 2...  31.9 us
    pallas_call x1, Pallas kernels, sum_tiles(): pl.pallas_call(functools.partial(sum_kernel, chunks, factor), out_shape=[...  25.3 us
    pallas_call x1, Pallas kernels, attend(): pl.pallas_call(functools.partial(attend_kernel, score_scale, blocks), gri...  18.3 us
    ppermute x12, waiting for transfers between devices, swap(): lax.ppermute(value, 'seq', [(source, source ^ flip) for source in range(c...  15.9 us
    ppermute x12, starting transfers between devices, swap(): lax.ppermute(value, 'seq', [(source, source ^ flip) for source in range(c...  9.43 us
    convert_element_type x1, other arithmetic, head_body(): normed = (unit_rows * norm_gain).astype(jnp.bfloat16)  5.2 us
    dot_general x2, matrix products, through_weights(): lax.dot_general(piece, part_qkv, (((0,), (1,)), ((), ())), preferred_elem...  4.27 us
    slice x3, local copies, waits for them, and re-layouts, head_body(): rows = jnp.concatenate([pack[:length] for pack in packs], axis=0)  3.63 us
  transfers between devices with their start and end apart: 12, of which 2 were waited for; matrix products, arithmetic and copies ran while one was open for 21% of the time, Pallas kernels for 38%

profile of v4, /device:TPU:0, one launch (start us, length us, event | category | flops | bytes accessed | tf_op | source)
XLA Modules:
  0.0 150.1 jit_solution(513334687450371194)
XLA Ops:
  2.5 2.5 %collective-permute-start.2 = (bf16[272,1280]{1,0:T(8,128)(2,1)S(1)}, bf16[272,1280]{1,0:T(8,128)(2,1)}, u32[]{:S(2)}, u32[]{:S(2)}) collective-permute-start(bf16[272,1280]{1,0:T(8,128)(2,1)S(1)} %fusion.21), channel_id=1, source_target_pairs={{0,3},{1,2},{2,1},{3,0},{4,7},{5,6},{6,5},{7,4},{8,11},{9,10},{10,... | collective-permute-start | bytes 2088968 | tf_op jit(solution)/shard_map/ppermute | solution.py:195
  5.7 2.0 %collective-permute-start.3 = (bf16[256,1280]{1,0:T(8,128)(2,1)}, bf16[256,1280]{1,0:T(8,128)(2,1)}, u32[]{:S(2)}, u32[]{:S(2)}) collective-permute-start(bf16[256,1280]{1,0:T(8,128)(2,1)} %bitcast.43), channel_id=1, source_target_pairs={{0,2},{1,3},{2,0},{3,1},{4,6},{5,7},{6,4},{7,5},{8,10},{9,11},{10,... | collective-permute-start | bytes 1966088 | tf_op jit(solution)/shard_map/ppermute | solution.py:195
  7.7 1.2 fusion.34
  9.0 31.9 %shard_map.85 = bf16[4,2,2,80,1600]{4,3,2,1,0:T(8,128)(2,1)S(1)} custom-call(bf16[80,1600]{1,0:T(8,128)(2,1)S(1)} %pad_maximum_fusion.6.piece_ref), custom_call_target="tpu_custom_call" | custom-call | bytes 32768000 | tf_op jit(solution)/shard_map/pallas_call | solution.py:413
  40.9 1.3 slice.113
  42.2 1.9 %slice.110 = bf16[4,2,2,80,960]{4,3,2,1,0:T(8,128)(2,1)} slice(bf16[4,2,2,80,1600]{4,3,2,1,0:T(8,128)(2,1)S(1)} %shard_map.85), slice={[0:4], [0:2], [0:2], [0:80], [640:1600]} | slice | bytes 4915200 | tf_op jit(solution)/shard_map/slice | solution.py:593
  44.4 2.2 %constant_dynamic-slice_fusion = (bf16[4,1,80,640]{3,2,1,0:T(8,128)(2,1)}, bf16[4,1,80,640]{3,2,1,0:T(8,128)(2,1)}) fusion(bf16[8,2,80,640]{3,2,1,0:T(8,128)(2,1)} %bitcast.42, s32[]{:T(128)S(6)} %select_n.70, s32[]{:T(128)S(6)} %add.147), kind=kLoop, calls=%fused_computation.60 | loop fusion | bytes 1638408 | tf_op jit(solution)/shard_map/slice | solution.py:597
  48.9 1.4 slice.126
  50.8 2.6 %fusion.2 = f32[1024]{0:T(1024)S(1)} fusion(f32[1024]{0:T(1024)S(1)} %broadcast_multiply_fusion, bf16[256,1280]{1,0:T(8,128)(2,1)S(1)} %slice.128, bf16[256,1280]{1,0:T(8,128)(2,1)S(1)} %slice.127, bf16[256,1280]{1,0:T(8,128)(2,1)S(1)} %slice.126, bf16[256,1280]{1,0:T(8,128)(2,1)S(1)} %bitcast.33), kind=kLoop, calls=%fused_computation.4 | loop fusion | flops 14416896 | bytes 2629632 | tf_op jit(solution)/shard_map/reduce_sum | solution.py:28
  55.8 5.2 %multiply_convert_fusion = (bf16[1024,1280]{1,0:T(8,128)(2,1)S(1)}, f32[1024,1280]{1,0:T(8,128)}) fusion(f32[1280]{0:T(1024)S(1)} %copy-done.16, f32[1024]{0:T(1024)S(1)} %add_rsqrt_fusion, f32[1024]{0:T(1024)S(1)} %broadcast_multiply_fusion, bf16[256,1280]{1,0:T(8,128)(2,1)S(1)} %slice.128, bf16[256,1280]{1,0:T(8,128)(2,1)} %copy-done.2, ...), kind=kLoop, calls=%fused_computation.5 | loop fusion | flops 15728640 | bytes 10499072 | tf_op jit(solution)/shard_map/convert_element_type | solution.py:590
  61.0 2.5 %fusion.6 = bf16[640,1024]{1,0:T(8,128)(2,1)S(1)} fusion(bf16[1024,1280]{1,0:T(8,128)(2,1)S(1)} %get-tuple-element.47, bf16[1280,960]{1,0:T(8,128)(2,1)S(1)} %bitcast.35), kind=kOutput, calls=%fused_computation.18 | convolution fusion | flops 1678376960 | bytes 5570560 | tf_op jit(solution)/shard_map/dot_general | solution.py:601
  64.9 1.7 %fusion.15.g_ref = bf16[320,512]{1,0:T(8,128)(2,1)S(1)} fusion(bf16[256,1280]{1,0:T(8,128)(2,1)} %collective-permute-done.3, bf16[256,1280]{1,0:T(8,128)(2,1)S(1)} %bitcast.45, bf16[320,640]{1,0:T(8,128)(2,1)S(1)} %bitcast.47, bf16[320,640]{1,0:T(8,128)(2,1)S(1)} %bitcast.46, f32[512]{0:T(512)S(1)} %maximum_convert_fusion.1), kind=kOutput, calls=%fused_computation.29 | convolution fusion | flops 424017920 | bytes 2459648 | tf_op jit(solution)/shard_map/dot_general | solution.py:33
  66.6 18.3 %shard_map.86 = (bf16[320,512]{1,0:T(8,128)(2,1)S(1)}, bf16[320,512]{1,0:T(8,128)(2,1)S(1)}, f32[2,320,512]{2,1,0:T(8,128)S(1)}, bf16[2,320,512]{2,1,0:T(8,128)(2,1)}) custom-call(bf16[320,512]{1,0:T(8,128)(2,1)S(1)} %fusion.12.q_ref, bf16[320,512]{1,0:T(8,128)(2,1)S(1)} %fusion.15.g_ref, bf16[320,1024]{1,0:T(8,128)(2,1)S(1)} %get-tuple-element.57.k_ref, ...), custom_call_target="tpu_custom_call" | custom-call | flops 1677721600 | bytes 3932160 | tf_op jit(solution)/shard_map/pallas_call | solution.py:259
  85.2 1.9 %fusion.17 = f32[320,1280]{1,0:T(8,128)S(1)} fusion(bf16[320,512]{1,0:T(8,128)(2,1)S(1)} %get-tuple-element.33, bf16[256,1280]{1,0:T(8,128)(2,1)} %collective-permute-done.3, bf16[256,1280]{1,0:T(8,128)(2,1)} %bitcast.44), kind=kOutput, calls=%fused_computation.35 | convolution fusion | flops 422051840 | bytes 3276800 | tf_op jit(solution)/shard_map/dot_general | solution.py:616
  90.1 1.5 %collective-permute-start.10 = (bf16[320,320]{1,0:T(8,128)(2,1)S(1)}, bf16[320,320]{1,0:T(8,128)(2,1)S(1)}, u32[]{:S(2)}, u32[]{:S(2)}) collective-permute-start(bf16[320,320]{1,0:T(8,128)(2,1)S(1)} %get-tuple-element.51), channel_id=1, source_target_pairs={{0,3},{1,2},{2,1},{3,0},{4,7},{5,6},{6,5},{7,4},{8,11},{9,10},{10,... | collective-permute-start | bytes 614408 | tf_op jit(solution)/shard_map/ppermute | solution.py:195
  92.1 1.9 %collective-permute-done.7.corner_ref = bf16[160,512]{1,0:T(8,128)(2,1)S(1)} collective-permute-done((bf16[160,512]{1,0:T(8,128)(2,1)S(1)}, bf16[160,512]{1,0:T(8,128)(2,1)S(1)}, u32[]{:S(2)}, u32[]{:S(2)}) %collective-permute-start.7) | collective-permute-done | bytes 163872 | tf_op jit(solution)/shard_map/ppermute | solution.py:195
  94.6 13.9 %collective-permute-done.6.facing_ref = bf16[160,512]{1,0:T(8,128)(2,1)S(1)} collective-permute-done((bf16[160,512]{1,0:T(8,128)(2,1)S(1)}, bf16[160,512]{1,0:T(8,128)(2,1)S(1)}, u32[]{:S(2)}, u32[]{:S(2)}) %collective-permute-start.6) | collective-permute-done | bytes 163872 | tf_op jit(solution)/shard_map/ppermute | solution.py:195
  110.0 2.6 %convolution_convert_fusion = bf16[1280,480]{0,1:T(8,128)(2,1)} fusion(bf16[480,1024]{1,0:T(8,128)(2,1)S(1)} %shard_map.87, bf16[1024,1280]{1,0:T(8,128)(2,1)S(1)} %copy-done.9), kind=kOutput, calls=%fused_computation.6 | convolution fusion | flops 1258905600 | bytes 4833280 | tf_op jit(solution)/shard_map/dot_general | solution.py:638
  112.6 1.7 %convolution_convert_fusion.1 = bf16[256,1280]{1,0:T(8,128)(2,1)} fusion(bf16[1280,960]{1,0:T(8,128)(2,1)S(1)} %bitcast.37, bf16[960,512]{1,0:T(8,128)(2,1)S(1)} %pad_maximum_fusion.1), kind=kOutput, calls=%fused_computation.10 | convolution fusion | flops 629473280 | bytes 3768320 | tf_op jit(solution)/shard_map/dot_general | solution.py:649
  114.9 1.6 %copy.21 = bf16[1280,480]{1,0:T(8,128)(2,1)S(1)} copy(bf16[1280,480]{0,1:T(8,128)(2,1)} %convolution_convert_fusion) | data formatting | bytes 2457600 | tf_op jit(solution)/shard_map/optimization_barrier | solution.py:654
  116.5 1.7 %select_convert_fusion.1 = (bf16[320,320]{1,0:T(8,128)(2,1)S(1)}, bf16[320,320]{1,0:T(8,128)(2,1)S(1)}) fusion(bf16[320,320]{1,0:T(8,128)(2,1)S(1)} %collective-permute-done.10, bf16[320,320]{1,0:T(8,128)(2,1)} %copy-done.14, bf16[320,320]{1,0:T(8,128)(2,1)} %copy-done.15, f32[320,1280]{1,0:T(8,128)} %copy-done.7, s32[]{:T(128)S(6)} %select_n.79, pred[]{:T(512)S(6)} %eq.4), kind=kLoop, calls=%fused_computation.43 | loop fusion | flops 921600 | bytes 1433605 | tf_op jit(solution)/shard_map/convert.1 | solution.py:679
  118.2 25.3 %shard_map.88 = (f32[160,480]{1,0:T(8,128)S(1)}, f32[80,320]{1,0:T(8,128)S(1)}) custom-call(bf16[4,2,160,480]{3,2,1,0:T(8,128)(2,1)S(1)} %bitcast.29, bf16[4,2,80,320]{3,2,1,0:T(8,128)(2,1)S(1)} %bitcast.30), custom_call_target="tpu_custom_call" | custom-call | bytes 39321600 | tf_op jit(solution)/shard_map/pallas_call | solution.py:503
  143.6 2.5 %fusion.31 = (f32[256]{0:T(256)S(1)}, f32[256]{0:T(256)S(1)}, f32[256,1280]{1,0:T(8,128)S(1)}) fusion(f32[1024,1280]{1,0:T(8,128)} %get-tuple-element.48, f32[1280]{0:T(1024)S(1)} %copy-done.16, bf16[256,1280]{1,0:T(8,128)(2,1)S(1)} %collective-permute-done.11, bf16[1280,960]{1,0:T(8,128)(2,1)S(1)} %bitcast.38, bf16[960,512]{1,0:T(8,128)(2,1)S(1)} %pad_maximum_fusion.1), kind=kOutput, calls=%fused_computation.82 | convolution fusion | flops 631111168 | bytes 6400000 | tf_op jit(solution)/shard_map/dot_general | solution.py:649
  146.2 2.5 %fusion.22 = bf16[1,256,1280]{2,1,0:T(8,128)(2,1)} fusion(f32[1024,1280]{1,0:T(8,128)} %get-tuple-element.48, f32[256,1280]{1,0:T(8,128)S(1)} %get-tuple-element.72, f32[256]{0:T(256)S(1)} %broadcast_multiply_fusion.1, f32[256]{0:T(256)S(1)} %broadcast_multiply_fusion.2, f32[256]{0:T(256)S(1)} %slice-done, bf16[1,256,1280]{2,1,0:T(8,128)(2,1)S(1)} %copy-done.11), kind=kLoop, calls=%fused_computation.40 | loop fusion | flops 2293760 | bytes 3935232 | tf_op jit(solution)/shard_map/broadcast_in_dim | solution.py:668
  (95 shorter events, 17.2 us)
Async XLA Ops:
  0.6 7.1 %copy-start = (bf16[80,1280]{1,0:T(8,128)(2,1)S(1)}, bf16[80,1280]{1,0:T(8,128)(2,1)}, u32[]{:S(2)}) copy-start(bf16[80,1280]{1,0:T(8,128)(2,1)} %param.12) | copy-start | bytes 614404
  2.5 44.1 %collective-permute-start.2 = (bf16[272,1280]{1,0:T(8,128)(2,1)S(1)}, bf16[272,1280]{1,0:T(8,128)(2,1)}, u32[]{:S(2)}, u32[]{:S(2)}) collective-permute-start(bf16[272,1280]{1,0:T(8,128)(2,1)S(1)} %fusion.21), channel_id=1, source_target_pairs={{0,3},{1,2},{2,1},{3,0},{4,7},{5,6},{6,5},{7,4},{8,11},{9,10},{10,... | collective-permute-start | bytes 2088968 | tf_op jit(solution)/shard_map/ppermute | solution.py:195
  5.0 42.8 %collective-permute-start.1 = (bf16[272,1280]{1,0:T(8,128)(2,1)S(1)}, bf16[272,1280]{1,0:T(8,128)(2,1)}, u32[]{:S(2)}, u32[]{:S(2)}) collective-permute-start(bf16[272,1280]{1,0:T(8,128)(2,1)S(1)} %fusion.21), channel_id=1, source_target_pairs={{0,1},{1,0},{2,3},{3,2},{4,5},{5,4},{6,7},{7,6},{8,9},{9,8},{10,11... | collective-permute-start | bytes 2088968 | tf_op jit(solution)/shard_map/ppermute | solution.py:195
  5.7 43.3 %collective-permute-start = (bf16[272,1280]{1,0:T(8,128)(2,1)S(1)}, bf16[272,1280]{1,0:T(8,128)(2,1)}, u32[]{:S(2)}, u32[]{:S(2)}) collective-permute-start(bf16[272,1280]{1,0:T(8,128)(2,1)S(1)} %fusion.21), channel_id=1, source_target_pairs={{0,2},{1,3},{2,0},{3,1},{4,6},{5,7},{6,4},{7,5},{8,10},{9,11},{10,... | collective-permute-start | bytes 2088968 | tf_op jit(solution)/shard_map/ppermute | solution.py:195
  5.7 58.8 %collective-permute-start.3 = (bf16[256,1280]{1,0:T(8,128)(2,1)}, bf16[256,1280]{1,0:T(8,128)(2,1)}, u32[]{:S(2)}, u32[]{:S(2)}) collective-permute-start(bf16[256,1280]{1,0:T(8,128)(2,1)} %bitcast.43), channel_id=1, source_target_pairs={{0,2},{1,3},{2,0},{3,1},{4,6},{5,7},{6,4},{7,5},{8,10},{9,11},{10,... | collective-permute-start | bytes 1966088 | tf_op jit(solution)/shard_map/ppermute | solution.py:195
  44.4 5.9 %copy-start.1 = (bf16[1,256,1280]{2,1,0:T(8,128)(2,1)S(1)}, bf16[1,256,1280]{2,1,0:T(8,128)(2,1)}, u32[]{:S(2)}) copy-start(bf16[1,256,1280]{2,1,0:T(8,128)(2,1)} %param.8) | copy-start | bytes 1966084
  48.9 4.5 %copy-start.2 = (bf16[256,1280]{1,0:T(8,128)(2,1)}, bf16[256,1280]{1,0:T(8,128)(2,1)S(1)}, u32[]{:S(2)}) copy-start(bf16[256,1280]{1,0:T(8,128)(2,1)S(1)} %slice.127) | copy-start | bytes 1966084
  50.3 3.1 %copy-start.3 = (bf16[256,1280]{1,0:T(8,128)(2,1)}, bf16[256,1280]{1,0:T(8,128)(2,1)S(1)}, u32[]{:S(2)}) copy-start(bf16[256,1280]{1,0:T(8,128)(2,1)S(1)} %slice.126) | copy-start | bytes 1966084
  50.3 5.5 %copy-start.16 = (f32[1280]{0:T(1024)S(1)}, f32[1280]{0:T(1024)}, u32[]{:S(2)}) copy-start(f32[1280]{0:T(1024)} %param.10) | copy-start | bytes 15364
  53.4 61.4 %copy-start.17 = (f32[1024]{0:T(1024)}, f32[1024]{0:T(1024)S(1)}, u32[]{:S(2)}) copy-start(f32[1024]{0:T(1024)S(1)} %add_rsqrt_fusion) | copy-start | bytes 12292
  55.8 5.2 %copy-start.4 = (bf16[4,2,2,80,960]{4,3,2,1,0:T(8,128)(2,1)S(1)}, bf16[4,2,2,80,960]{4,3,2,1,0:T(8,128)(2,1)}, u32[]{:S(2)}) copy-start(bf16[4,2,2,80,960]{4,3,2,1,0:T(8,128)(2,1)} %slice.110) | copy-start | bytes 7372804
  61.0 2.7 %copy-start.8 = (bf16[1024,1280]{1,0:T(8,128)(2,1)}, bf16[1024,1280]{1,0:T(8,128)(2,1)S(1)}, u32[]{:S(2)}) copy-start(bf16[1024,1280]{1,0:T(8,128)(2,1)S(1)} %get-tuple-element.47) | copy-start | bytes 7864324
  84.9 2.3 %collective-permute-start.4 = (bf16[2,320,512]{2,1,0:T(8,128)(2,1)}, bf16[2,320,512]{2,1,0:T(8,128)(2,1)S(1)}, u32[]{:S(2)}, u32[]{:S(2)}) collective-permute-start(bf16[2,320,512]{2,1,0:T(8,128)(2,1)} %get-tuple-element.32), channel_id=1, source_target_pairs={{0,1},{1,0},{2,3},{3,2},{4,5},{5,4},{6,7},{7,6},{8,9},{9,8},{10,11... | collective-permute-start | bytes 1966088 | tf_op jit(solution)/shard_map/ppermute | solution.py:195
  87.1 2.6 %copy-start.7 = (f32[320,1280]{1,0:T(8,128)}, f32[320,1280]{1,0:T(8,128)S(1)}, u32[]{:S(2)}) copy-start(f32[320,1280]{1,0:T(8,128)S(1)} %fusion.17) | copy-start | bytes 4915204
  87.9 6.1 %collective-permute-start.7 = (bf16[160,512]{1,0:T(8,128)(2,1)S(1)}, bf16[160,512]{1,0:T(8,128)(2,1)S(1)}, u32[]{:S(2)}, u32[]{:S(2)}) collective-permute-start(bf16[160,512]{1,0:T(8,128)(2,1)S(1)} %get-tuple-element.58), channel_id=1, source_target_pairs={{0,3},{1,2},{2,1},{3,0},{4,7},{5,6},{6,5},{7,4},{8,11},{9,10},{10,... | collective-permute-start | bytes 491528 | tf_op jit(solution)/shard_map/ppermute | solution.py:195
  89.5 20.5 %copy-start.9 = (bf16[1024,1280]{1,0:T(8,128)(2,1)S(1)}, bf16[1024,1280]{1,0:T(8,128)(2,1)}, u32[]{:S(2)}) copy-start(bf16[1024,1280]{1,0:T(8,128)(2,1)} %copy-done.8) | copy-start | bytes 7864324
  89.5 19.0 %collective-permute-start.5 = (bf16[320,512]{1,0:T(8,128)(2,1)S(1)}, bf16[320,512]{1,0:T(8,128)(2,1)S(1)}, u32[]{:S(2)}, u32[]{:S(2)}) collective-permute-start(bf16[320,512]{1,0:T(8,128)(2,1)S(1)} %get-tuple-element.60), channel_id=1, source_target_pairs={{0,1},{1,0},{2,3},{3,2},{4,5},{5,4},{6,7},{7,6},{8,9},{9,8},{10,11... | collective-permute-start | bytes 983048 | tf_op jit(solution)/shard_map/ppermute | solution.py:195
  90.1 18.6 %collective-permute-start.10 = (bf16[320,320]{1,0:T(8,128)(2,1)S(1)}, bf16[320,320]{1,0:T(8,128)(2,1)S(1)}, u32[]{:S(2)}, u32[]{:S(2)}) collective-permute-start(bf16[320,320]{1,0:T(8,128)(2,1)S(1)} %get-tuple-element.51), channel_id=1, source_target_pairs={{0,3},{1,2},{2,1},{3,0},{4,7},{5,6},{6,5},{7,4},{8,11},{9,10},{10,... | collective-permute-start | bytes 614408 | tf_op jit(solution)/shard_map/ppermute | solution.py:195
  91.6 17.0 %collective-permute-start.9 = (bf16[320,320]{1,0:T(8,128)(2,1)S(1)}, bf16[320,320]{1,0:T(8,128)(2,1)S(1)}, u32[]{:S(2)}, u32[]{:S(2)}) collective-permute-start(bf16[320,320]{1,0:T(8,128)(2,1)S(1)} %get-tuple-element.52), channel_id=1, source_target_pairs={{0,2},{1,3},{2,0},{3,1},{4,6},{5,7},{6,4},{7,5},{8,10},{9,11},{10,... | collective-permute-start | bytes 614408 | tf_op jit(solution)/shard_map/ppermute | solution.py:195
  92.1 16.5 %collective-permute-start.8 = (bf16[320,320]{1,0:T(8,128)(2,1)S(1)}, bf16[320,320]{1,0:T(8,128)(2,1)S(1)}, u32[]{:S(2)}, u32[]{:S(2)}) collective-permute-start(bf16[320,320]{1,0:T(8,128)(2,1)S(1)} %get-tuple-element.53), channel_id=1, source_target_pairs={{0,1},{1,0},{2,3},{3,2},{4,5},{5,4},{6,7},{7,6},{8,9},{9,8},{10,11... | collective-permute-start | bytes 614408 | tf_op jit(solution)/shard_map/ppermute | solution.py:195
  94.0 14.5 %collective-permute-start.6 = (bf16[160,512]{1,0:T(8,128)(2,1)S(1)}, bf16[160,512]{1,0:T(8,128)(2,1)S(1)}, u32[]{:S(2)}, u32[]{:S(2)}) collective-permute-start(bf16[160,512]{1,0:T(8,128)(2,1)S(1)} %get-tuple-element.59), channel_id=1, source_target_pairs={{0,2},{1,3},{2,0},{3,1},{4,6},{5,7},{6,4},{7,5},{8,10},{9,11},{10,... | collective-permute-start | bytes 491528 | tf_op jit(solution)/shard_map/ppermute | solution.py:195
  108.6 4.0 %copy-start.5 = (bf16[4,2,2,80,960]{4,3,2,1,0:T(8,128)(2,1)S(1)}, bf16[4,2,2,80,960]{4,3,2,1,0:T(8,128)(2,1)}, u32[]{:S(2)}) copy-start(bf16[4,2,2,80,960]{4,3,2,1,0:T(8,128)(2,1)} %slice.110) | copy-start | bytes 7372804
  114.3 29.3 %collective-permute-start.11 = (bf16[256,1280]{1,0:T(8,128)(2,1)}, bf16[256,1280]{1,0:T(8,128)(2,1)S(1)}, u32[]{:S(2)}, u32[]{:S(2)}) collective-permute-start(bf16[256,1280]{1,0:T(8,128)(2,1)} %convolution_convert_fusion.1), channel_id=1, source_target_pairs={{0,2},{1,3},{2,0},{3,1},{4,6},{5,7},{6,4},{7,5},{8,10},{9,11},{10,... | collective-permute-start | bytes 1966088 | tf_op jit(solution)/shard_map/ppermute | solution.py:195
  116.4 27.2 %copy-start.6 = (bf16[4,2,2,80,960]{4,3,2,1,0:T(8,128)(2,1)S(1)}, bf16[4,2,2,80,960]{4,3,2,1,0:T(8,128)(2,1)}, u32[]{:S(2)}) copy-start(bf16[4,2,2,80,960]{4,3,2,1,0:T(8,128)(2,1)} %slice.110) | copy-start | bytes 7372804
  (8 other events, 12.3 us)

commit v5 on v4

--- a/solution.py
+++ b/solution.py
@@ -572,13 +572,11 @@
     packed_weights = jnp.concatenate([mine_out, mine_qkv], axis=1)
 
     upstream = cotangent[0]
-    marks = jnp.zeros((16, width), jnp.bfloat16).at[0, :length].set(live[0].astype(jnp.bfloat16))
-    packed = jnp.concatenate([frames[0], marks], axis=0)
-    packs = [packed, swap(packed, 2), swap(packed, 1), swap(packed, 3)]
+    marks = live.astype(jnp.float32)
+    packs = [frames[0]] + [swap(frames[0], flip) for flip in (2, 1, 3)]
     cots = jnp.concatenate([upstream, swap(upstream, 2)], axis=0)
-    rows = jnp.concatenate([pack[:length] for pack in packs], axis=0)
-    key_live = jnp.concatenate([pack[length, :length] for pack in packs], axis=0)
-    key_live = key_live.astype(jnp.float32)
+    rows = jnp.concatenate(packs, axis=0)
+    key_live = jnp.concatenate([marks] + [swap(marks, flip) for flip in (2, 1, 3)], axis=1)[0]
     step = jnp.arange(length, dtype=jnp.float32)
     key_pos = jnp.concatenate(
         [step + ((me ^ flip) * length).astype(jnp.float32) for flip in (0, 2, 1, 3)]
@@ -632,9 +630,11 @@
     def columns_of(flip):
         return lax.dynamic_slice_in_dim(partial_out, (me ^ flip) * block, block, 1)
 
-    columns = [swap(columns_of(flip).astype(jnp.bfloat16), flip) for flip in (1, 2, 3)]
+    blocks = [columns_of(flip).astype(jnp.bfloat16) for flip in (1, 2, 3)]
+    blocks, facing, corner = lax.optimization_barrier((blocks, facing, corner))
+    columns = [swap(value, flip) for value, flip in zip(blocks, (1, 2, 3))]
     keep_t = assemble(units(2 * (high + low), 2), beside, facing, corner)
-    keep_t, late_t, columns = lax.optimization_barrier((keep_t, grads_t, columns))
+    late_t, columns = lax.optimization_barrier((grads_t, columns))
     sum_qkv = lax.dot_general(
         normed, keep_t, (((0,), (1,)), ((), ())), preferred_element_type=jnp.float32
     )

time: 151 us -> 152 us (level)
  local copies, waits for them, and re-layouts: 17.9 us -> 11.8 us
  waiting for transfers between devices: 15.9 us -> 19.7 us
  starting transfers between devices: 9.43 us -> 13 us
    ppermute x12 -> x15, waiting for transfers between devices: 15.9 us -> 19.7 us  [swap(): lax.ppermute(value, 'seq', [(source, source ^ flip) for source in range(c...]
    slice x3 -> x0, local copies, waits for them, and re-layouts: 3.63 us -> none  [head_body(): rows = jnp.concatenate([pack[:length] for pack in packs], axis=0)]
    ppermute x12 -> x15, starting transfers between devices: 9.43 us -> 13 us  [swap(): lax.ppermute(value, 'seq', [(source, source ^ flip) for source in range(c...]
    concatenate x3 -> x0, local copies, waits for them, and re-layouts: 2.05 us -> none  [head_body(): jnp.concatenate([pack[length, :length] for pack in packs], axis=0)]
    concatenate x2 -> x1, other arithmetic: 1.86 us -> 0.01 us  [head_body(): jnp.concatenate([marks] + [swap(marks, flip) for flip in (2, 1, 3)], axis=1)]
    slice x1, local copies, waits for them, and re-layouts: 1.88 us -> 3.62 us  [head_body(): part_qkv = gathered[..., width // 2:].reshape(n_data * shard, 3 * part)]
    unnamed x40 -> x32, local copies, waits for them, and re-layouts: 3.17 us -> 3.43 us
  transfers between devices with their start and end apart: 12 -> 15, of which waited for: 2 -> 6; matrix products, arithmetic and copies ran while one was open for 21% -> 18% of each run, Pallas kernels for 38% -> 38%
where the time goes in v5:
time: 152 us
  Pallas kernels  76.1 us (50%)
  waiting for transfers between devices  19.7 us (13%)
  other arithmetic  15.9 us (10%)
  matrix products  13.9 us (9%)
  starting transfers between devices  13 us (9%)
  local copies, waits for them, and re-layouts  11.8 us (8%)
    pallas_call x1, Pallas kernels, gather_pieces(): pl.pallas_call(gather_kernel, out_shape=jax.ShapeDtypeStruct((count, 2, 2...  31.5 us
    pallas_call x1, Pallas kernels, sum_tiles(): pl.pallas_call(functools.partial(sum_kernel, chunks, factor), out_shape=[...  26.2 us
    ppermute x15, waiting for transfers between devices, swap(): lax.ppermute(value, 'seq', [(source, source ^ flip) for source in range(c...  19.7 us
    pallas_call x1, Pallas kernels, attend(): pl.pallas_call(functools.partial(attend_kernel, score_scale, blocks), gri...  18.3 us
    ppermute x15, starting transfers between devices, swap(): lax.ppermute(value, 'seq', [(source, source ^ flip) for source in range(c...  13 us
    convert_element_type x1, other arithmetic, head_body(): normed = (unit_rows * norm_gain).astype(jnp.bfloat16)  5.18 us
    dot_general x2, matrix products, through_weights(): lax.dot_general(piece, part_qkv, (((0,), (1,)), ((), ())), preferred_elem...  4.26 us
    slice x1, local copies, waits for them, and re-layouts, head_body(): part_qkv = gathered[..., width // 2:].reshape(n_data * shard, 3 * part)  3.62 us
  transfers between devices with their start and end apart: 15, of which 6 were waited for; matrix products, arithmetic and copies ran while one was open for 18% of the time, Pallas kernels for 38%

profile of v5, /device:TPU:0, one launch (start us, length us, event | category | flops | bytes accessed | tf_op | source)
XLA Modules:
  0.0 151.5 jit_solution(8239192938250894066)
XLA Ops:
  1.4 2.4 %collective-permute-start.6 = (f32[1,256]{1,0:T(1,128)S(1)}, f32[1,256]{1,0:T(1,128)S(1)}, u32[]{:S(2)}, u32[]{:S(2)}) collective-permute-start(f32[1,256]{1,0:T(1,128)S(1)} %convert_element_type.81), channel_id=1, source_target_pairs={{0,3},{1,2},{2,1},{3,0},{4,7},{5,6},{6,5},{7,4},{8,11},{9,10},{10,... | collective-permute-start | bytes 3080 | tf_op jit(solution)/shard_map/ppermute | solution.py:195
  4.5 2.1 %collective-permute-start = (bf16[256,1280]{1,0:T(8,128)(2,1)}, bf16[256,1280]{1,0:T(8,128)(2,1)}, u32[]{:S(2)}, u32[]{:S(2)}) collective-permute-start(bf16[256,1280]{1,0:T(8,128)(2,1)} %bitcast.34), channel_id=1, source_target_pairs={{0,2},{1,3},{2,0},{3,1},{4,6},{5,7},{6,4},{7,5},{8,10},{9,11},{10,... | collective-permute-start | bytes 1966088 | tf_op jit(solution)/shard_map/ppermute | solution.py:195
  7.9 31.5 %shard_map.85 = bf16[4,2,2,80,1600]{4,3,2,1,0:T(8,128)(2,1)S(1)} custom-call(bf16[80,1600]{1,0:T(8,128)(2,1)S(1)} %pad_maximum_fusion.6.piece_ref), custom_call_target="tpu_custom_call" | custom-call | bytes 32768000 | tf_op jit(solution)/shard_map/pallas_call | solution.py:413
  39.5 2.0 %copy-done.1 = bf16[4,2,2,80,1600]{4,3,2,1,0:T(8,128)(2,1)} copy-done((bf16[4,2,2,80,1600]{4,3,2,1,0:T(8,128)(2,1)}, bf16[4,2,2,80,1600]{4,3,2,1,0:T(8,128)(2,1)S(1)}, u32[]{:S(2)}) %copy-start.1) | copy-done | bytes 4096024
  43.2 3.6 %slice.70 = bf16[4,2,2,80,960]{4,3,2,1,0:T(8,128)(2,1)} slice(bf16[4,2,2,80,1600]{4,3,2,1,0:T(8,128)(2,1)} %copy-done.1), slice={[0:4], [0:2], [0:2], [0:80], [640:1600]} | slice | bytes 4915200 | tf_op jit(solution)/shard_map/slice | solution.py:591
  47.1 1.6 %collective-permute-start.3 = (bf16[256,1280]{1,0:T(8,128)(2,1)}, bf16[256,1280]{1,0:T(8,128)(2,1)}, u32[]{:S(2)}, u32[]{:S(2)}) collective-permute-start(bf16[256,1280]{1,0:T(8,128)(2,1)} %bitcast), channel_id=1, source_target_pairs={{0,2},{1,3},{2,0},{3,1},{4,6},{5,7},{6,4},{7,5},{8,10},{9,11},{10,... | collective-permute-start | bytes 1966088 | tf_op jit(solution)/shard_map/ppermute | solution.py:195
  50.5 2.0 %fusion.2 = f32[1024]{0:T(1024)S(1)} fusion(f32[1024]{0:T(1024)S(1)} %broadcast_multiply_fusion, bf16[256,1280]{1,0:T(8,128)(2,1)S(1)} %collective-permute-done.2, bf16[256,1280]{1,0:T(8,128)(2,1)S(1)} %collective-permute-done.1, bf16[256,1280]{1,0:T(8,128)(2,1)} %collective-permute-done, bf16[256,1280]{1,0:T(8,128)(2,1)S(1)} %bitcast.36), kind=kLoop, calls=%fused_computation.4 | loop fusion | flops 14416896 | bytes 2629632 | tf_op jit(solution)/shard_map/reduce_sum | solution.py:28
  52.6 5.2 %multiply_convert_fusion = (bf16[1024,1280]{1,0:T(8,128)(2,1)S(1)}, f32[1024,1280]{1,0:T(8,128)}) fusion(f32[1280]{0:T(1024)S(1)} %copy-done.13, f32[1024]{0:T(1024)S(1)} %add_rsqrt_fusion, f32[1024]{0:T(1024)S(1)} %broadcast_multiply_fusion, bf16[256,1280]{1,0:T(8,128)(2,1)S(1)} %collective-permute-done.2, bf16[256,1280]{1,0:T(8,128)(2,1)S(1)} %collective-permute-done.1, ...), kind=kLoop, calls=%fused_computation.5 | loop fusion | flops 15728640 | bytes 10499072 | tf_op jit(solution)/shard_map/convert_element_type | solution.py:588
  57.8 2.5 %fusion.6 = bf16[640,1024]{1,0:T(8,128)(2,1)S(1)} fusion(bf16[1024,1280]{1,0:T(8,128)(2,1)S(1)} %get-tuple-element.43, bf16[1280,960]{1,0:T(8,128)(2,1)S(1)} %bitcast.25), kind=kOutput, calls=%fused_computation.18 | convolution fusion | flops 1678376960 | bytes 5570560 | tf_op jit(solution)/shard_map/dot_general | solution.py:599
  61.3 2.9 %collective-permute-done.3 = bf16[256,1280]{1,0:T(8,128)(2,1)} collective-permute-done((bf16[256,1280]{1,0:T(8,128)(2,1)}, bf16[256,1280]{1,0:T(8,128)(2,1)}, u32[]{:S(2)}, u32[]{:S(2)}) %collective-permute-start.3) | collective-permute-done | bytes 655392 | tf_op jit(solution)/shard_map/ppermute | solution.py:195
  64.2 1.9 %fusion.14.g_ref = bf16[320,512]{1,0:T(8,128)(2,1)S(1)} fusion(bf16[256,1280]{1,0:T(8,128)(2,1)} %collective-permute-done.3, bf16[256,1280]{1,0:T(8,128)(2,1)} %bitcast, bf16[320,640]{1,0:T(8,128)(2,1)S(1)} %bitcast.40, bf16[320,640]{1,0:T(8,128)(2,1)S(1)} %bitcast.39, f32[512]{0:T(512)S(1)} %bitcast.43), kind=kOutput, calls=%fused_computation.27 | convolution fusion | flops 424017920 | bytes 2459648 | tf_op jit(solution)/shard_map/dot_general | solution.py:33
  66.1 18.3 %shard_map.86 = (bf16[320,512]{1,0:T(8,128)(2,1)S(1)}, bf16[320,512]{1,0:T(8,128)(2,1)S(1)}, f32[2,320,512]{2,1,0:T(8,128)S(1)}, bf16[2,320,512]{2,1,0:T(8,128)(2,1)}) custom-call(bf16[320,512]{1,0:T(8,128)(2,1)S(1)} %fusion.11.q_ref, bf16[320,512]{1,0:T(8,128)(2,1)S(1)} %fusion.14.g_ref, bf16[320,1024]{1,0:T(8,128)(2,1)S(1)} %get-tuple-element.53.k_ref, ...), custom_call_target="tpu_custom_call" | custom-call | flops 1677721600 | bytes 3932160 | tf_op jit(solution)/shard_map/pallas_call | solution.py:259
  84.4 1.9 %fusion.16 = f32[320,1280]{1,0:T(8,128)S(1)} fusion(bf16[320,512]{1,0:T(8,128)(2,1)S(1)} %get-tuple-element.25, bf16[256,1280]{1,0:T(8,128)(2,1)} %collective-permute-done.3, bf16[256,1280]{1,0:T(8,128)(2,1)} %bitcast), kind=kOutput, calls=%fused_computation.33 | convolution fusion | flops 422051840 | bytes 3276800 | tf_op jit(solution)/shard_map/dot_general | solution.py:614
  91.1 3.6 %collective-permute-done.9.corner_ref = bf16[160,512]{1,0:T(8,128)(2,1)S(1)} collective-permute-done((bf16[160,512]{1,0:T(8,128)(2,1)S(1)}, bf16[160,512]{1,0:T(8,128)(2,1)S(1)}, u32[]{:S(2)}, u32[]{:S(2)}) %collective-permute-start.9) | collective-permute-done | bytes 163872 | tf_op jit(solution)/shard_map/ppermute | solution.py:195
  94.8 4.0 %collective-permute-done.8.facing_ref = bf16[160,512]{1,0:T(8,128)(2,1)S(1)} collective-permute-done((bf16[160,512]{1,0:T(8,128)(2,1)S(1)}, bf16[160,512]{1,0:T(8,128)(2,1)S(1)}, u32[]{:S(2)}, u32[]{:S(2)}) %collective-permute-start.8) | collective-permute-done | bytes 163872 | tf_op jit(solution)/shard_map/ppermute | solution.py:195
  100.7 2.6 %convolution_convert_fusion = bf16[1280,480]{0,1:T(8,128)(2,1)} fusion(bf16[480,1024]{1,0:T(8,128)(2,1)S(1)} %shard_map.87, bf16[1024,1280]{1,0:T(8,128)(2,1)S(1)} %copy-done.8), kind=kOutput, calls=%fused_computation.6 | convolution fusion | flops 1258905600 | bytes 4833280 | tf_op jit(solution)/shard_map/dot_general | solution.py:638
  103.3 4.2 %collective-permute-done.11 = bf16[320,320]{1,0:T(8,128)(2,1)S(1)} collective-permute-done((bf16[320,320]{1,0:T(8,128)(2,1)S(1)}, bf16[320,320]{1,0:T(8,128)(2,1)S(1)}, u32[]{:S(2)}, u32[]{:S(2)}) %collective-permute-start.11) | collective-permute-done | bytes 204832 | tf_op jit(solution)/shard_map/ppermute | solution.py:195
  107.5 4.5 %collective-permute-done.12 = bf16[320,320]{1,0:T(8,128)(2,1)S(1)} collective-permute-done((bf16[320,320]{1,0:T(8,128)(2,1)S(1)}, bf16[320,320]{1,0:T(8,128)(2,1)S(1)}, u32[]{:S(2)}, u32[]{:S(2)}) %collective-permute-start.12) | collective-permute-done | bytes 204832 | tf_op jit(solution)/shard_map/ppermute | solution.py:195
  112.0 1.8 %convolution_convert_fusion.1 = bf16[256,1280]{1,0:T(8,128)(2,1)} fusion(bf16[1280,960]{1,0:T(8,128)(2,1)S(1)} %bitcast.27, bf16[960,512]{1,0:T(8,128)(2,1)S(1)} %pad_maximum_fusion.1), kind=kOutput, calls=%fused_computation.10 | convolution fusion | flops 629473280 | bytes 3768320 | tf_op jit(solution)/shard_map/dot_general | solution.py:649
  115.3 1.6 %copy.12 = bf16[1280,480]{1,0:T(8,128)(2,1)S(1)} copy(bf16[1280,480]{0,1:T(8,128)(2,1)} %convolution_convert_fusion) | data formatting | bytes 2457600 | tf_op jit(solution)/shard_map/optimization_barrier | solution.py:654
  116.9 1.7 %select_convert_fusion.1 = (bf16[320,320]{1,0:T(8,128)(2,1)S(1)}, bf16[320,320]{1,0:T(8,128)(2,1)S(1)}) fusion(bf16[320,320]{1,0:T(8,128)(2,1)} %copy-done.12, bf16[320,320]{1,0:T(8,128)(2,1)} %copy-done.11, bf16[320,320]{1,0:T(8,128)(2,1)S(1)} %collective-permute-done.10, f32[320,1280]{1,0:T(8,128)} %copy-done.5, s32[]{:T(128)S(6)} %select_n.79, pred[]{:T(512)S(6)} %eq.4), kind=kLoop, calls=%fused_computation.40 | loop fusion | flops 921600 | bytes 1433605 | tf_op jit(solution)/shard_map/convert | solution.py:679
  118.7 26.2 %shard_map.88 = (f32[160,480]{1,0:T(8,128)S(1)}, f32[80,320]{1,0:T(8,128)S(1)}) custom-call(bf16[4,2,160,480]{3,2,1,0:T(8,128)(2,1)S(1)} %bitcast.23, bf16[4,2,80,320]{3,2,1,0:T(8,128)(2,1)S(1)} %bitcast.24), custom_call_target="tpu_custom_call" | custom-call | bytes 39321600 | tf_op jit(solution)/shard_map/pallas_call | solution.py:503
  145.0 2.5 %fusion.29 = (f32[256]{0:T(256)S(1)}, f32[256]{0:T(256)S(1)}, f32[256,1280]{1,0:T(8,128)S(1)}) fusion(f32[1024,1280]{1,0:T(8,128)} %get-tuple-element.44, f32[1280]{0:T(1024)S(1)} %copy-done.13, bf16[256,1280]{1,0:T(8,128)(2,1)S(1)} %collective-permute-done.14, bf16[1280,960]{1,0:T(8,128)(2,1)S(1)} %bitcast.28, bf16[960,512]{1,0:T(8,128)(2,1)S(1)} %pad_maximum_fusion.1), kind=kOutput, calls=%fused_computation.73 | convolution fusion | flops 631111168 | bytes 6400000 | tf_op jit(solution)/shard_map/dot_general | solution.py:649
  147.5 2.7 %fusion.20 = bf16[1,256,1280]{2,1,0:T(8,128)(2,1)} fusion(f32[1024,1280]{1,0:T(8,128)} %get-tuple-element.44, f32[256,1280]{1,0:T(8,128)S(1)} %get-tuple-element.64, f32[256]{0:T(256)S(1)} %broadcast_multiply_fusion.1, f32[256]{0:T(256)S(1)} %broadcast_multiply_fusion.2, f32[256]{0:T(256)S(1)} %slice-done, bf16[1,256,1280]{2,1,0:T(8,128)(2,1)} %param.11), kind=kLoop, calls=%fused_computation.37 | loop fusion | flops 2293760 | bytes 3935232 | tf_op jit(solution)/shard_map/broadcast_in_dim | solution.py:668
  (85 shorter events, 17.1 us)
Async XLA Ops:
  0.6 6.0 %copy-start = (bf16[80,1280]{1,0:T(8,128)(2,1)S(1)}, bf16[80,1280]{1,0:T(8,128)(2,1)}, u32[]{:S(2)}) copy-start(bf16[80,1280]{1,0:T(8,128)(2,1)} %param.10) | copy-start | bytes 614404
  1.4 41.3 %collective-permute-start.6 = (f32[1,256]{1,0:T(1,128)S(1)}, f32[1,256]{1,0:T(1,128)S(1)}, u32[]{:S(2)}, u32[]{:S(2)}) collective-permute-start(f32[1,256]{1,0:T(1,128)S(1)} %convert_element_type.81), channel_id=1, source_target_pairs={{0,3},{1,2},{2,1},{3,0},{4,7},{5,6},{6,5},{7,4},{8,11},{9,10},{10,... | collective-permute-start | bytes 3080 | tf_op jit(solution)/shard_map/ppermute | solution.py:195
  3.8 43.3 %collective-permute-start.5 = (f32[1,256]{1,0:T(1,128)S(1)}, f32[1,256]{1,0:T(1,128)S(1)}, u32[]{:S(2)}, u32[]{:S(2)}) collective-permute-start(f32[1,256]{1,0:T(1,128)S(1)} %convert_element_type.81), channel_id=1, source_target_pairs={{0,1},{1,0},{2,3},{3,2},{4,5},{5,4},{6,7},{7,6},{8,9},{9,8},{10,11... | collective-permute-start | bytes 3080 | tf_op jit(solution)/shard_map/ppermute | solution.py:195
  4.5 44.5 %collective-permute-start.2 = (bf16[256,1280]{1,0:T(8,128)(2,1)}, bf16[256,1280]{1,0:T(8,128)(2,1)S(1)}, u32[]{:S(2)}, u32[]{:S(2)}) collective-permute-start(bf16[256,1280]{1,0:T(8,128)(2,1)} %bitcast.32), channel_id=1, source_target_pairs={{0,3},{1,2},{2,1},{3,0},{4,7},{5,6},{6,5},{7,4},{8,11},{9,10},{10,... | collective-permute-start | bytes 1966088 | tf_op jit(solution)/shard_map/ppermute | solution.py:195
  4.5 44.5 %collective-permute-start.1 = (bf16[256,1280]{1,0:T(8,128)(2,1)}, bf16[256,1280]{1,0:T(8,128)(2,1)S(1)}, u32[]{:S(2)}, u32[]{:S(2)}) collective-permute-start(bf16[256,1280]{1,0:T(8,128)(2,1)} %bitcast.33), channel_id=1, source_target_pairs={{0,1},{1,0},{2,3},{3,2},{4,5},{5,4},{6,7},{7,6},{8,9},{9,8},{10,11... | collective-permute-start | bytes 1966088 | tf_op jit(solution)/shard_map/ppermute | solution.py:195
  4.5 44.5 %collective-permute-start = (bf16[256,1280]{1,0:T(8,128)(2,1)}, bf16[256,1280]{1,0:T(8,128)(2,1)}, u32[]{:S(2)}, u32[]{:S(2)}) collective-permute-start(bf16[256,1280]{1,0:T(8,128)(2,1)} %bitcast.34), channel_id=1, source_target_pairs={{0,2},{1,3},{2,0},{3,1},{4,6},{5,7},{6,4},{7,5},{8,10},{9,11},{10,... | collective-permute-start | bytes 1966088 | tf_op jit(solution)/shard_map/ppermute | solution.py:195
  42.6 6.0 %collective-permute-start.4 = (f32[1,256]{1,0:T(1,128)S(1)}, f32[1,256]{1,0:T(1,128)S(1)}, u32[]{:S(2)}, u32[]{:S(2)}) collective-permute-start(f32[1,256]{1,0:T(1,128)S(1)} %convert_element_type.81), channel_id=1, source_target_pairs={{0,2},{1,3},{2,0},{3,1},{4,6},{5,7},{6,4},{7,5},{8,10},{9,11},{10,... | collective-permute-start | bytes 3080 | tf_op jit(solution)/shard_map/ppermute | solution.py:195
  43.2 5.8 %copy-start.6 = (bf16[1,256,1280]{2,1,0:T(8,128)(2,1)S(1)}, bf16[1,256,1280]{2,1,0:T(8,128)(2,1)}, u32[]{:S(2)}) copy-start(bf16[1,256,1280]{2,1,0:T(8,128)(2,1)} %param.6) | copy-start | bytes 1966084
  47.1 17.1 %collective-permute-start.3 = (bf16[256,1280]{1,0:T(8,128)(2,1)}, bf16[256,1280]{1,0:T(8,128)(2,1)}, u32[]{:S(2)}, u32[]{:S(2)}) collective-permute-start(bf16[256,1280]{1,0:T(8,128)(2,1)} %bitcast), channel_id=1, source_target_pairs={{0,2},{1,3},{2,0},{3,1},{4,6},{5,7},{6,4},{7,5},{8,10},{9,11},{10,... | collective-permute-start | bytes 1966088 | tf_op jit(solution)/shard_map/ppermute | solution.py:195
  52.6 62.7 %copy-start.14 = (f32[1024]{0:T(1024)}, f32[1024]{0:T(1024)S(1)}, u32[]{:S(2)}) copy-start(f32[1024]{0:T(1024)S(1)} %add_rsqrt_fusion) | copy-start | bytes 12292
  52.6 5.2 %copy-start.2 = (bf16[4,2,2,80,960]{4,3,2,1,0:T(8,128)(2,1)S(1)}, bf16[4,2,2,80,960]{4,3,2,1,0:T(8,128)(2,1)}, u32[]{:S(2)}) copy-start(bf16[4,2,2,80,960]{4,3,2,1,0:T(8,128)(2,1)} %slice.70) | copy-start | bytes 7372804
  84.4 2.3 %collective-permute-start.7 = (bf16[2,320,512]{2,1,0:T(8,128)(2,1)}, bf16[2,320,512]{2,1,0:T(8,128)(2,1)S(1)}, u32[]{:S(2)}, u32[]{:S(2)}) collective-permute-start(bf16[2,320,512]{2,1,0:T(8,128)(2,1)} %get-tuple-element.24), channel_id=1, source_target_pairs={{0,1},{1,0},{2,3},{3,2},{4,5},{5,4},{6,7},{7,6},{8,9},{9,8},{10,11... | collective-permute-start | bytes 1966088 | tf_op jit(solution)/shard_map/ppermute | solution.py:195
  86.3 4.5 %copy-start.5 = (f32[320,1280]{1,0:T(8,128)}, f32[320,1280]{1,0:T(8,128)S(1)}, u32[]{:S(2)}) copy-start(f32[320,1280]{1,0:T(8,128)S(1)} %fusion.16) | copy-start | bytes 4915204
  88.0 12.6 %collective-permute-start.13 = (bf16[320,512]{1,0:T(8,128)(2,1)S(1)}, bf16[320,512]{1,0:T(8,128)(2,1)S(1)}, u32[]{:S(2)}, u32[]{:S(2)}) collective-permute-start(bf16[320,512]{1,0:T(8,128)(2,1)S(1)} %get-tuple-element.54), channel_id=1, source_target_pairs={{0,1},{1,0},{2,3},{3,2},{4,5},{5,4},{6,7},{7,6},{8,9},{9,8},{10,11... | collective-permute-start | bytes 983048 | tf_op jit(solution)/shard_map/ppermute | solution.py:195
  88.7 6.1 %collective-permute-start.9 = (bf16[160,512]{1,0:T(8,128)(2,1)S(1)}, bf16[160,512]{1,0:T(8,128)(2,1)S(1)}, u32[]{:S(2)}, u32[]{:S(2)}) collective-permute-start(bf16[160,512]{1,0:T(8,128)(2,1)S(1)} %get-tuple-element.56), channel_id=1, source_target_pairs={{0,3},{1,2},{2,1},{3,0},{4,7},{5,6},{6,5},{7,4},{8,11},{9,10},{10,... | collective-permute-start | bytes 491528 | tf_op jit(solution)/shard_map/ppermute | solution.py:195
  90.2 10.5 %copy-start.8 = (bf16[1024,1280]{1,0:T(8,128)(2,1)S(1)}, bf16[1024,1280]{1,0:T(8,128)(2,1)}, u32[]{:S(2)}) copy-start(bf16[1024,1280]{1,0:T(8,128)(2,1)} %copy-done.7) | copy-start | bytes 7864324
  90.2 8.5 %collective-permute-start.8 = (bf16[160,512]{1,0:T(8,128)(2,1)S(1)}, bf16[160,512]{1,0:T(8,128)(2,1)S(1)}, u32[]{:S(2)}, u32[]{:S(2)}) collective-permute-start(bf16[160,512]{1,0:T(8,128)(2,1)S(1)} %get-tuple-element.57), channel_id=1, source_target_pairs={{0,2},{1,3},{2,0},{3,1},{4,6},{5,7},{6,4},{7,5},{8,10},{9,11},{10,... | collective-permute-start | bytes 491528 | tf_op jit(solution)/shard_map/ppermute | solution.py:195
  98.8 4.5 %collective-permute-start.10 = (bf16[320,320]{1,0:T(8,128)(2,1)S(1)}, bf16[320,320]{1,0:T(8,128)(2,1)S(1)}, u32[]{:S(2)}, u32[]{:S(2)}) collective-permute-start(bf16[320,320]{1,0:T(8,128)(2,1)S(1)} %get-tuple-element.28), channel_id=1, source_target_pairs={{0,1},{1,0},{2,3},{3,2},{4,5},{5,4},{6,7},{7,6},{8,9},{9,8},{10,11... | collective-permute-start | bytes 614408 | tf_op jit(solution)/shard_map/ppermute | solution.py:195
  98.8 8.8 %collective-permute-start.11 = (bf16[320,320]{1,0:T(8,128)(2,1)S(1)}, bf16[320,320]{1,0:T(8,128)(2,1)S(1)}, u32[]{:S(2)}, u32[]{:S(2)}) collective-permute-start(bf16[320,320]{1,0:T(8,128)(2,1)S(1)} %get-tuple-element.29), channel_id=1, source_target_pairs={{0,2},{1,3},{2,0},{3,1},{4,6},{5,7},{6,4},{7,5},{8,10},{9,11},{10,... | collective-permute-start | bytes 614408 | tf_op jit(solution)/shard_map/ppermute | solution.py:195
  100.3 11.7 %collective-permute-start.12 = (bf16[320,320]{1,0:T(8,128)(2,1)S(1)}, bf16[320,320]{1,0:T(8,128)(2,1)S(1)}, u32[]{:S(2)}, u32[]{:S(2)}) collective-permute-start(bf16[320,320]{1,0:T(8,128)(2,1)S(1)} %get-tuple-element.30), channel_id=1, source_target_pairs={{0,3},{1,2},{2,1},{3,0},{4,7},{5,6},{6,5},{7,4},{8,11},{9,10},{10,... | collective-permute-start | bytes 614408 | tf_op jit(solution)/shard_map/ppermute | solution.py:195
  100.7 11.3 %copy-start.3 = (bf16[4,2,2,80,960]{4,3,2,1,0:T(8,128)(2,1)S(1)}, bf16[4,2,2,80,960]{4,3,2,1,0:T(8,128)(2,1)}, u32[]{:S(2)}) copy-start(bf16[4,2,2,80,960]{4,3,2,1,0:T(8,128)(2,1)} %slice.70) | copy-start | bytes 7372804
  107.5 6.3 %copy-start.11 = (bf16[320,320]{1,0:T(8,128)(2,1)}, bf16[320,320]{1,0:T(8,128)(2,1)S(1)}, u32[]{:S(2)}) copy-start(bf16[320,320]{1,0:T(8,128)(2,1)S(1)} %collective-permute-done.11) | copy-start | bytes 614404
  113.8 31.1 %collective-permute-start.14 = (bf16[256,1280]{1,0:T(8,128)(2,1)}, bf16[256,1280]{1,0:T(8,128)(2,1)S(1)}, u32[]{:S(2)}, u32[]{:S(2)}) collective-permute-start(bf16[256,1280]{1,0:T(8,128)(2,1)} %convolution_convert_fusion.1), channel_id=1, source_target_pairs={{0,2},{1,3},{2,0},{3,1},{4,6},{5,7},{6,4},{7,5},{8,10},{9,11},{10,... | collective-permute-start | bytes 1966088 | tf_op jit(solution)/shard_map/ppermute | solution.py:195
  116.9 28.0 %copy-start.4 = (bf16[4,2,2,80,960]{4,3,2,1,0:T(8,128)(2,1)S(1)}, bf16[4,2,2,80,960]{4,3,2,1,0:T(8,128)(2,1)}, u32[]{:S(2)}) copy-start(bf16[4,2,2,80,960]{4,3,2,1,0:T(8,128)(2,1)} %slice.70) | copy-start | bytes 7372804
  (7 other events, 20.3 us)
